TPU v7x, 128 devices: a whole 4x4x4 slice. The times are simulated.
128 devices in a mesh: section: 2 (over core), ctx: 8 (over x_lo, z), fsdp: 8 (over y, x_hi).
Axes of the slice: x: 4 (x_hi: 2, x_lo: 2; x = x_hi * 2 + x_lo), y: 4, z: 4, core: 2. Of those that a mesh axis runs over, the one named last changes fastest.
Arguments:
- x_in: bfloat16 [2, 8, 1024, 768], P(None, 'fsdp', 'ctx'), may hold values from -6 to 6
- cotangent: bfloat16 [2, 8, 1024, 768], P(None, 'fsdp', 'ctx'), may hold values from -6 to 6
- group_ids: int32 [2, 8, 1024], P(None, 'fsdp'), may hold values from 0 to 8, as said below
- routes: int32 [2, 2, 8, 1024, 2], P('section', None, 'fsdp', 'ctx'), may hold values from 0 to 7, all different within a row
- priority: int32 [2, 2, 8, 1024, 2], P('section', None, 'fsdp', 'ctx'), may hold values from 0 to 4095
- gains: bfloat16 [2, 768, 2], P('section', ('ctx', 'fsdp')), may hold values from 0.5 to 1.5
- w_qkv: bfloat16 [2, 768, 2304], P('section', ('ctx', 'fsdp')), may hold values from -0.21875 to 0.21875
- w_out: bfloat16 [2, 768, 768], P('section', ('ctx', 'fsdp')), may hold values from -1.75 to 1.75
- router: bfloat16 [2, 768, 8], P('section', ('ctx', 'fsdp')), may hold values from -0.15625 to 0.15625
- shared_gate_up: bfloat16 [2, 768, 4096], P('section', ('ctx', 'fsdp')), may hold values from -0.21875 to 0.21875
- shared_down: bfloat16 [2, 2048, 768], P('section', ('ctx', 'fsdp')), may hold values from -0.125 to 0.125
- expert_gate_up: bfloat16 [2, 8, 768, 4096], P('section', 'ctx', 'fsdp'), may hold values from -0.21875 to 0.21875
- expert_down: bfloat16 [2, 8, 2048, 768], P('section', 'ctx', 'fsdp'), may hold values from -0.125 to 0.125
Outputs:
- section_outputs: bfloat16 [2, 2, 8, 1024, 768], P('section', None, 'fsdp', 'ctx')
- input_grads: float32 [2, 2, 8, 1024, 768], P('section', None, 'fsdp', 'ctx')
- gains_grad: float32 [2, 768, 2], P('section', ('ctx', 'fsdp'))
- w_qkv_grad: float32 [2, 768, 2304], P('section', ('ctx', 'fsdp'))
- w_out_grad: float32 [2, 768, 768], P('section', ('ctx', 'fsdp'))
- router_grad: float32 [2, 768, 8], P('section', ('ctx', 'fsdp'))
- shared_gate_up_grad: float32 [2, 768, 4096], P('section', ('ctx', 'fsdp'))
- shared_down_grad: float32 [2, 2048, 768], P('section', ('ctx', 'fsdp'))
- expert_gate_up_grad: float32 [2, 8, 768, 4096], P('section', 'ctx', 'fsdp')
- expert_down_grad: float32 [2, 8, 2048, 768], P('section', 'ctx', 'fsdp')
Inputs may be any that keep to these rules, and one draw needn't show every extreme that they name: `group_ids`: in each row a prompt labelled 0 takes the first 384 to 512 tokens; labels 1 to 8 follow in order, each a nonempty contiguous run. `routes`: each token names 2 different experts.
All inputs are finite; a program needn't handle non-finite values.
Results may differ from a plain program's by a relative error of at most 0.025.
Values may be sent and summed in bfloat16 or wider, within the bound.
A program may use at most 320 MiB of HBM per device.

v0:
```python
import math

import jax
import jax.numpy as jnp
from jax import lax
from jax.sharding import PartitionSpec as P

D = 768
HEADS = 12
HEAD_DIM = 64
TOP = 2
EXP_DEV = 1
CONT = 8


EPS = 1e-06
NEG = -1e30
HIGH = lax.Precision.HIGHEST


def shifted(value, axis, steps):
    count = lax.axis_size(axis)
    first, last = (max(0, -steps), min(count, count - steps))
    return lax.ppermute(value, axis, [(source, source + steps) for source in range(first, last)])


def rms_scale(values, gain):
    mean_sq = jnp.mean(values * values, axis=-1, keepdims=True)
    return values * lax.rsqrt(mean_sq + EPS) * gain


def swiglu(joined):
    half_width = joined.shape[-1] // 2
    return jax.nn.silu(joined[..., :half_width]) * joined[..., half_width:]


def rotary(values, angles):
    half_width = values.shape[-1] // 2
    cosine = jnp.cos(angles)[:, None, :]
    sine = jnp.sin(angles)[:, None, :]
    first_half = values[..., :half_width]
    second_half = values[..., half_width:]
    return jnp.concatenate(
        [first_half * cosine - second_half * sine, second_half * cosine + first_half * sine],
        axis=-1,
    )


def rotary_angles(positions, head_width):
    half_width = head_width // 2
    frequency = jnp.exp(-math.log(10000.0) * jnp.arange(half_width, dtype=jnp.float32) / half_width)
    return positions.astype(jnp.float32)[:, None] * frequency[None, :]


def token_positions(group_row, label_count):
    labels = jnp.arange(label_count + 1, dtype=jnp.int32)
    member = (group_row[:, None] == labels[None, :]).astype(jnp.int32)
    run_sizes = jnp.sum(member, axis=0)
    run_starts = jnp.cumsum(run_sizes) - run_sizes
    first_index = jnp.sum(member * run_starts[None, :], axis=1)
    token_index = jnp.arange(group_row.shape[0], dtype=jnp.int32)
    return jnp.where(group_row == 0, token_index, run_sizes[0] + token_index - first_index)


def slot_of_pairs(route_block, rank_block, capacity):
    pair_count = route_block.shape[0] * route_block.shape[1]
    expert_of = route_block.reshape(-1)
    order_key = rank_block.reshape(-1) * pair_count + jnp.arange(pair_count, dtype=jnp.int32)
    earlier = (expert_of[None, :] == expert_of[:, None]) & (order_key[None, :] < order_key[:, None])
    slot_number = jnp.sum(earlier.astype(jnp.int32), axis=1)
    kept_pair = slot_number < capacity
    place_of = expert_of * capacity + jnp.minimum(slot_number, capacity - 1)
    return (place_of, kept_pair)


def contract_rows(left, right, precision=None):
    return lax.dot_general(
        left,
        right,
        (((0,), (0,)), ((), ())),
        precision=precision,
        preferred_element_type=jnp.float32,
    )


def times_transposed(left, right, precision=None):
    return lax.dot_general(
        left,
        right,
        (((1,), (1,)), ((), ())),
        precision=precision,
        preferred_element_type=jnp.float32,
    )


def score_block(
    query_heads, key_block, key_index, key_group, query_index, query_group, score_scale
):
    raw_scores = (
        jnp.einsum("qhd,khd->hqk", query_heads, key_block, preferred_element_type=jnp.float32)
        * score_scale
    )
    visible = (key_index[None, :] <= query_index[:, None]) & (
        (key_group[None, :] == 0) | (key_group[None, :] == query_group[:, None])
    )
    return jnp.where(visible[None], raw_scores, NEG)


def key_blocks(keys, values, group_row, block_width):
    seq_len = keys.shape[0]
    block_count = seq_len // block_width
    heads_shape = (block_count, block_width, HEADS, HEAD_DIM)
    key_index = jnp.arange(seq_len, dtype=jnp.int32).reshape(block_count, block_width)
    return (
        keys.reshape(heads_shape),
        values.reshape(heads_shape),
        key_index,
        group_row.reshape(block_count, block_width),
    )


def attend_forward(query_heads, blocks, query_index, query_group, score_scale):
    row_count = query_heads.shape[0]

    def stats_step(running, block):
        running_max, running_sum = running
        key_block, value_block, key_index, key_group = block
        scores = score_block(
            query_heads, key_block, key_index, key_group, query_index, query_group, score_scale
        )
        new_max = jnp.maximum(running_max, jnp.max(scores, axis=-1))
        running_sum = running_sum * jnp.exp(running_max - new_max) + jnp.sum(
            jnp.exp(scores - new_max[..., None]), axis=-1
        )
        return ((new_max, running_sum), None)

    start_stats = (
        jnp.full((HEADS, row_count), NEG, jnp.float32),
        jnp.zeros((HEADS, row_count), jnp.float32),
    )
    (running_max, running_sum), _ = lax.scan(stats_step, start_stats, blocks)
    log_total = running_max + jnp.log(running_sum)

    def value_step(accum, block):
        key_block, value_block, key_index, key_group = block
        scores = score_block(
            query_heads, key_block, key_index, key_group, query_index, query_group, score_scale
        )
        weights = jnp.exp(scores - log_total[..., None]).astype(jnp.bfloat16)
        return (
            accum
            + jnp.einsum("hqk,khd->qhd", weights, value_block, preferred_element_type=jnp.float32),
            None,
        )

    accum, _ = lax.scan(value_step, jnp.zeros((row_count, HEADS, HEAD_DIM), jnp.float32), blocks)
    return (accum, log_total)


def query_probs(query_heads, query_index, query_group, score_scale, log_total, grad_heads):

    def probs_of(block):
        key_block, value_block, key_index, key_group = block
        scores = score_block(
            query_heads, key_block, key_index, key_group, query_index, query_group, score_scale
        )
        probs = jnp.exp(scores - log_total[..., None])
        grad_probs = jnp.einsum(
            "qhd,khd->hqk", grad_heads, value_block, preferred_element_type=jnp.float32
        )
        return (probs, grad_probs)

    return probs_of


def backward_delta(probs_of, blocks, row_count):

    def delta_step(delta, block):
        probs, grad_probs = probs_of(block)
        return (delta + jnp.sum(probs * grad_probs, axis=-1), None)

    delta, _ = lax.scan(delta_step, jnp.zeros((HEADS, row_count), jnp.float32), blocks)
    return delta


def attend_backward(
    query_heads, blocks, query_index, query_group, score_scale, log_total, grad_heads
):
    row_count = query_heads.shape[0]
    probs_of = query_probs(
        query_heads, query_index, query_group, score_scale, log_total, grad_heads
    )
    delta = backward_delta(probs_of, blocks, row_count)

    def grad_step(grad_queries, block):
        probs, grad_probs = probs_of(block)
        key_block = block[0]
        grad_scores = (probs * (grad_probs - delta[..., None])).astype(jnp.bfloat16)
        grad_queries = grad_queries + score_scale * jnp.einsum(
            "hqk,khd->qhd", grad_scores, key_block, preferred_element_type=jnp.float32
        )
        grad_keys = score_scale * jnp.einsum(
            "hqk,qhd->khd", grad_scores, query_heads, preferred_element_type=jnp.float32
        )
        grad_values = jnp.einsum(
            "hqk,qhd->khd",
            probs.astype(jnp.bfloat16),
            grad_heads,
            preferred_element_type=jnp.float32,
        )
        return (grad_queries, (grad_keys, grad_values))

    grad_queries, (grad_keys, grad_values) = lax.scan(
        grad_step, jnp.zeros((row_count, HEADS, HEAD_DIM), jnp.float32), blocks
    )
    seq_len = grad_keys.shape[0] * grad_keys.shape[1]
    return (grad_queries, grad_keys.reshape(seq_len, D), grad_values.reshape(seq_len, D))


def layer_forward(state, dense, experts, geom, block_width, score_scale):
    query_index, query_group, angles, group_row, route, place_of, kept_pair, onehot = geom
    gains, w_qkv, w_out, router, shared_gate_up, shared_down = dense
    expert_gate_up, expert_down = experts
    row_count = state.shape[0]
    heads_shape = (row_count, HEADS, HEAD_DIM)
    gain_values = gains.astype(jnp.float32)
    normed_attn = rms_scale(state, gain_values[:, 0]).astype(jnp.bfloat16)
    joined_qkv = jnp.dot(normed_attn, w_qkv, preferred_element_type=jnp.float32)
    queries = rotary(joined_qkv[:, :D].reshape(heads_shape), angles).astype(jnp.bfloat16)
    own_keys = (
        rotary(joined_qkv[:, D : 2 * D].reshape(heads_shape), angles)
        .astype(jnp.bfloat16)
        .reshape(row_count, D)
    )
    own_values = joined_qkv[:, 2 * D :].astype(jnp.bfloat16)
    keys, values = (
        lax.all_gather(own_keys, "ctx", axis=0, tiled=True),
        lax.all_gather(own_values, "ctx", axis=0, tiled=True),
    )
    blocks = key_blocks(keys, values, group_row, block_width)
    attended_heads, log_total = attend_forward(
        queries, blocks, query_index, query_group, score_scale
    )
    attended = attended_heads.reshape(row_count, D).astype(jnp.bfloat16)
    residual = state + jnp.dot(attended, w_out, preferred_element_type=jnp.float32)
    normed_ffn = rms_scale(residual, gain_values[:, 1]).astype(jnp.bfloat16)
    logits = jnp.dot(normed_ffn, router, preferred_element_type=jnp.float32)
    gates = jax.nn.softmax(jnp.take_along_axis(logits, route, axis=1), axis=-1)
    shared_joined = jnp.dot(normed_ffn, shared_gate_up, preferred_element_type=jnp.float32)
    shared_hidden = swiglu(shared_joined).astype(jnp.bfloat16)
    shared_out = jnp.dot(shared_hidden, shared_down, preferred_element_type=jnp.float32)
    places = lax.axis_size("ctx")
    slot_rows = onehot.shape[0] // places
    sent = jnp.dot(
        onehot, jnp.repeat(normed_ffn, TOP, axis=0), preferred_element_type=jnp.float32
    ).astype(jnp.bfloat16)
    received = lax.all_to_all(
        sent.reshape(places, slot_rows, D), "ctx", split_axis=0, concat_axis=0, tiled=True
    )
    received = received.reshape(places, EXP_DEV, slot_rows // EXP_DEV, D)
    expert_joined = jnp.einsum(
        "necd,edf->necf", received, expert_gate_up, preferred_element_type=jnp.float32
    )
    expert_hidden = swiglu(expert_joined).astype(jnp.bfloat16)
    expert_result = jnp.einsum(
        "necf,efd->necd", expert_hidden, expert_down, preferred_element_type=jnp.float32
    ).astype(jnp.bfloat16)
    returned = lax.all_to_all(
        expert_result.reshape(places, slot_rows, D), "ctx", split_axis=0, concat_axis=0, tiled=True
    ).reshape(places * slot_rows, D)
    picked = jnp.where(
        kept_pair[:, None], jnp.take(returned, place_of, axis=0).astype(jnp.float32), 0.0
    )
    mixed = jnp.sum((picked * gates.reshape(-1)[:, None]).reshape(row_count, TOP, D), axis=1)
    output = residual + shared_out + mixed
    kept = (
        state,
        normed_attn,
        queries,
        keys,
        values,
        log_total,
        attended,
        residual,
        normed_ffn,
        gates,
        shared_joined,
        shared_hidden,
        received,
        expert_joined,
        expert_hidden,
        picked,
        geom,
    )
    return (output, kept)


def layer_backward(grad_output, kept, dense, experts, block_width, score_scale):
    (
        state,
        normed_attn,
        queries,
        keys,
        values,
        log_total,
        attended,
        residual,
        normed_ffn,
        gates,
        shared_joined,
        shared_hidden,
        received,
        expert_joined,
        expert_hidden,
        picked,
        geom,
    ) = kept
    query_index, query_group, angles, group_row, route, place_of, kept_pair, onehot = geom
    gains, w_qkv, w_out, router, shared_gate_up, shared_down = dense
    expert_gate_up, expert_down = experts
    row_count = state.shape[0]
    gain_values = gains.astype(jnp.float32)
    grad_rounded = grad_output.astype(jnp.bfloat16)
    grad_shared_down = contract_rows(shared_hidden, grad_rounded)
    _, shared_back = jax.vjp(swiglu, shared_joined)
    grad_shared_joined = shared_back(times_transposed(grad_rounded, shared_down))[0].astype(
        jnp.bfloat16
    )
    grad_shared_gate_up = contract_rows(normed_ffn, grad_shared_joined)
    grad_normed = times_transposed(grad_shared_joined, shared_gate_up)
    pair_grads = jnp.repeat(grad_output, TOP, axis=0)
    grad_gates = jnp.sum(pair_grads * picked, axis=1).reshape(row_count, TOP)
    slot_terms = jnp.where(kept_pair[:, None], pair_grads * gates.reshape(-1)[:, None], 0.0)
    slot_grads = jnp.dot(onehot.astype(jnp.float32), slot_terms, precision=HIGH).astype(
        jnp.bfloat16
    )
    places = received.shape[0]
    slot_rows = onehot.shape[0] // places
    grad_received = lax.all_to_all(
        slot_grads.reshape(places, slot_rows, D), "ctx", split_axis=0, concat_axis=0, tiled=True
    ).reshape(received.shape)
    grad_expert_down = jnp.einsum(
        "necf,necd->efd", expert_hidden, grad_received, preferred_element_type=jnp.float32
    )
    _, expert_back = jax.vjp(swiglu, expert_joined)
    grad_hidden = jnp.einsum(
        "necd,efd->necf", grad_received, expert_down, preferred_element_type=jnp.float32
    )
    grad_joined = expert_back(grad_hidden)[0].astype(jnp.bfloat16)
    grad_expert_gate_up = jnp.einsum(
        "necd,necf->edf", received, grad_joined, preferred_element_type=jnp.float32
    )
    grad_sent = jnp.einsum(
        "necf,edf->necd", grad_joined, expert_gate_up, preferred_element_type=jnp.float32
    ).astype(jnp.bfloat16)
    grad_slots = lax.all_to_all(
        grad_sent.reshape(places, slot_rows, D), "ctx", split_axis=0, concat_axis=0, tiled=True
    ).reshape(places * slot_rows, D)
    grad_pairs = contract_rows(onehot, grad_slots)
    grad_normed = grad_normed + jnp.sum(grad_pairs.reshape(row_count, TOP, D), axis=1)
    grad_chosen = gates * (grad_gates - jnp.sum(gates * grad_gates, axis=1, keepdims=True))
    expert_labels = jnp.arange(router.shape[1], dtype=jnp.int32)
    grad_logits = jnp.sum(
        jnp.where(route[:, :, None] == expert_labels[None, None, :], grad_chosen[:, :, None], 0.0),
        axis=1,
    )
    grad_router = contract_rows(normed_ffn.astype(jnp.float32), grad_logits, HIGH)
    grad_normed = grad_normed + times_transposed(grad_logits, router.astype(jnp.float32), HIGH)
    _, ffn_norm_back = jax.vjp(rms_scale, residual, gain_values[:, 1])
    grad_residual, grad_gain_ffn = ffn_norm_back(grad_normed)
    grad_residual = grad_output + grad_residual
    grad_projected = grad_residual.astype(jnp.bfloat16)
    grad_w_out = contract_rows(attended, grad_projected)
    grad_attended = (
        times_transposed(grad_projected, w_out)
        .astype(jnp.bfloat16)
        .reshape(row_count, HEADS, HEAD_DIM)
    )
    blocks = key_blocks(keys, values, group_row, block_width)
    grad_queries, grad_keys_all, grad_values_all = attend_backward(
        queries, blocks, query_index, query_group, score_scale, log_total, grad_attended
    )
    grad_keys, grad_values = (
        lax.psum_scatter(grad_keys_all, "ctx", scatter_dimension=0, tiled=True),
        lax.psum_scatter(grad_values_all, "ctx", scatter_dimension=0, tiled=True),
    )
    _, rotary_back = jax.vjp(lambda part_heads: rotary(part_heads, angles), grad_queries)
    grad_query_raw = rotary_back(grad_queries)[0].reshape(row_count, D)
    grad_key_raw = rotary_back(grad_keys.reshape(row_count, HEADS, HEAD_DIM))[0].reshape(
        row_count, D
    )
    grad_joined_qkv = jnp.concatenate([grad_query_raw, grad_key_raw, grad_values], axis=1).astype(
        jnp.bfloat16
    )
    grad_w_qkv = contract_rows(normed_attn, grad_joined_qkv)
    grad_normed_attn = times_transposed(grad_joined_qkv, w_qkv)
    _, attn_norm_back = jax.vjp(rms_scale, state, gain_values[:, 0])
    grad_state, grad_gain_attn = attn_norm_back(grad_normed_attn)
    grad_input = grad_residual + grad_state
    dense_grads = (
        jnp.stack([grad_gain_attn, grad_gain_ffn], axis=1),
        grad_w_qkv,
        grad_w_out,
        grad_router,
        grad_shared_gate_up,
        grad_shared_down,
    )
    return (grad_input, dense_grads, (grad_expert_gate_up, grad_expert_down))


def on_device(
    x_in,
    cotangent,
    group_ids,
    routes,
    priority,
    gains,
    w_qkv,
    w_out,
    router,
    shared_gate_up,
    shared_down,
    expert_gate_up,
    expert_down,
):
    micro_count = x_in.shape[0]
    row_count = x_in.shape[2]
    seq_len = group_ids.shape[2]
    places = lax.axis_size("ctx")
    place = lax.axis_index("ctx")
    section_place = lax.axis_index("section")
    first_section = section_place == 0
    last_section = section_place == 1
    expert_count = EXP_DEV * places
    capacity = max(2, row_count * TOP * 5 // (4 * expert_count))
    block_width = math.gcd(seq_len, 512)
    score_scale = 1.0 / math.sqrt(HEAD_DIM)
    dense_raw = (
        lax.all_gather(gains, ("ctx", "fsdp"), axis=1, tiled=True),
        lax.all_gather(w_qkv, ("ctx", "fsdp"), axis=1, tiled=True),
        lax.all_gather(w_out, ("ctx", "fsdp"), axis=1, tiled=True),
        lax.all_gather(router, ("ctx", "fsdp"), axis=1, tiled=True),
        lax.all_gather(shared_gate_up, ("ctx", "fsdp"), axis=1, tiled=True),
        lax.all_gather(shared_down, ("ctx", "fsdp"), axis=1, tiled=True),
    )
    dense = tuple((piece[0] for piece in dense_raw))
    experts_raw = (
        lax.all_gather(expert_gate_up, "fsdp", axis=2, tiled=True),
        lax.all_gather(expert_down, "fsdp", axis=2, tiled=True),
    )
    experts = (experts_raw[0][0], experts_raw[1][0])
    forward_outs = []
    kept_all = []
    previous_out = jnp.zeros((row_count, D), jnp.bfloat16)
    for step_index in range(micro_count + 1):
        local_input = x_in[min(step_index, micro_count - 1), 0].astype(jnp.float32)
        if step_index == 0:
            incoming = jnp.zeros((row_count, D), jnp.bfloat16)
        else:
            incoming = shifted(previous_out, "section", 1)
        state = jnp.where(first_section, local_input, incoming.astype(jnp.float32))
        geometry_micro_index = jnp.clip(step_index - section_place, 0, micro_count - 1)
        group_row = jnp.take(group_ids[:, 0], geometry_micro_index, axis=0)
        route = jnp.take(routes[0, :, 0], geometry_micro_index, axis=0)
        rank = jnp.take(priority[0, :, 0], geometry_micro_index, axis=0)
        positions = token_positions(group_row, CONT)
        start_row = place * row_count
        query_index = start_row + jnp.arange(row_count, dtype=jnp.int32)
        query_group = lax.dynamic_slice_in_dim(group_row, start_row, row_count)
        angles = rotary_angles(lax.dynamic_slice_in_dim(positions, start_row, row_count), HEAD_DIM)
        place_of, kept_pair = slot_of_pairs(route, rank, capacity)
        slots_all = jnp.arange(expert_count * capacity, dtype=jnp.int32)
        onehot = ((place_of[None, :] == slots_all[:, None]) & kept_pair[None, :]).astype(
            jnp.bfloat16
        )
        output, kept = layer_forward(
            state,
            dense,
            experts,
            (query_index, query_group, angles, group_row, route, place_of, kept_pair, onehot),
            block_width,
            score_scale,
        )
        previous_out = output.astype(jnp.bfloat16)
        forward_outs.append(previous_out)
        kept_all.append(kept)
    dense_again = (
        lax.all_gather(gains, ("ctx", "fsdp"), axis=1, tiled=True),
        lax.all_gather(w_qkv, ("ctx", "fsdp"), axis=1, tiled=True),
        lax.all_gather(w_out, ("ctx", "fsdp"), axis=1, tiled=True),
        lax.all_gather(router, ("ctx", "fsdp"), axis=1, tiled=True),
        lax.all_gather(shared_gate_up, ("ctx", "fsdp"), axis=1, tiled=True),
        lax.all_gather(shared_down, ("ctx", "fsdp"), axis=1, tiled=True),
    )
    dense_back = tuple((piece[0] for piece in dense_again))
    experts_again = (
        lax.all_gather(expert_gate_up, "fsdp", axis=2, tiled=True),
        lax.all_gather(expert_down, "fsdp", axis=2, tiled=True),
    )
    experts_back = (experts_again[0][0], experts_again[1][0])
    backward_grads = []
    dense_sum = None
    expert_sum = None
    previous_grad = jnp.zeros((row_count, D), jnp.bfloat16)
    for step_index in range(micro_count + 1):
        if step_index < micro_count:
            own_grad = cotangent[step_index, 0].astype(jnp.float32)
        else:
            own_grad = jnp.zeros((row_count, D), jnp.float32)
        if step_index == 0:
            incoming = jnp.zeros((row_count, D), jnp.bfloat16)
        else:
            incoming = shifted(previous_grad, "section", -1)
        grad_output = jnp.where(last_section, own_grad, incoming.astype(jnp.float32))
        kept_upper = kept_all[min(step_index + 1, micro_count)]
        kept_lower = kept_all[max(step_index - 1, 0)]
        kept = jax.tree.map(
            lambda upper, lower: jnp.where(last_section, upper, lower), kept_upper, kept_lower
        )
        grad_input, dense_grads, expert_grads = layer_backward(
            grad_output, kept, dense_back, experts_back, block_width, score_scale
        )
        if dense_sum is None:
            dense_sum = dense_grads
            expert_sum = expert_grads
        else:
            dense_sum = jax.tree.map(jnp.add, dense_sum, dense_grads)
            expert_sum = jax.tree.map(jnp.add, expert_sum, expert_grads)
        previous_grad = grad_input.astype(jnp.bfloat16)
        backward_grads.append(grad_input)
    outputs_each = [
        jnp.where(first_section, forward_outs[micro_index], forward_outs[micro_index + 1])
        for micro_index in range(micro_count)
    ]
    section_outputs = jnp.stack(outputs_each).reshape(1, micro_count, 1, row_count, D)
    grads_each = [
        jnp.where(last_section, backward_grads[micro_index], backward_grads[micro_index + 1])
        for micro_index in range(micro_count)
    ]
    input_grads = jnp.stack(grads_each).reshape(1, micro_count, 1, row_count, D)
    dense_owned = (
        lax.psum_scatter(dense_sum[0][None], ("ctx", "fsdp"), scatter_dimension=1, tiled=True),
        lax.psum_scatter(dense_sum[1][None], ("ctx", "fsdp"), scatter_dimension=1, tiled=True),
        lax.psum_scatter(dense_sum[2][None], ("ctx", "fsdp"), scatter_dimension=1, tiled=True),
        lax.psum_scatter(dense_sum[3][None], ("ctx", "fsdp"), scatter_dimension=1, tiled=True),
        lax.psum_scatter(dense_sum[4][None], ("ctx", "fsdp"), scatter_dimension=1, tiled=True),
        lax.psum_scatter(dense_sum[5][None], ("ctx", "fsdp"), scatter_dimension=1, tiled=True),
    )
    expert_owned = (
        lax.psum_scatter(
            expert_sum[0][None].astype(jnp.bfloat16), "fsdp", scatter_dimension=2, tiled=True
        ).astype(jnp.float32),
        lax.psum_scatter(
            expert_sum[1][None].astype(jnp.bfloat16), "fsdp", scatter_dimension=2, tiled=True
        ).astype(jnp.float32),
    )
    return (
        section_outputs,
        input_grads,
        dense_owned[0],
        dense_owned[1],
        dense_owned[2],
        dense_owned[3],
        dense_owned[4],
        dense_owned[5],
        expert_owned[0],
        expert_owned[1],
    )


def solution(mesh):
    return jax.shard_map(
        on_device,
        mesh=mesh,
        in_specs=(
            P(None, "fsdp", "ctx", None),
            P(None, "fsdp", "ctx", None),
            P(None, "fsdp", None),
            P("section", None, "fsdp", "ctx", None),
            P("section", None, "fsdp", "ctx", None),
            P("section", ("ctx", "fsdp"), None),
            P("section", ("ctx", "fsdp"), None),
            P("section", ("ctx", "fsdp"), None),
            P("section", ("ctx", "fsdp"), None),
            P("section", ("ctx", "fsdp"), None),
            P("section", ("ctx", "fsdp"), None),
            P("section", "ctx", "fsdp", None),
            P("section", "ctx", "fsdp", None),
        ),
        out_specs=(
            P("section", None, "fsdp", "ctx", None),
            P("section", None, "fsdp", "ctx", None),
            P("section", ("ctx", "fsdp"), None),
            P("section", ("ctx", "fsdp"), None),
            P("section", ("ctx", "fsdp"), None),
            P("section", ("ctx", "fsdp"), None),
            P("section", ("ctx", "fsdp"), None),
            P("section", ("ctx", "fsdp"), None),
            P("section", "ctx", "fsdp", None),
            P("section", "ctx", "fsdp", None),
        ),
        check_vma=False,
    )
```

profile of v0, /device:TPU:0, one launch (start us, length us, event | category | flops | bytes accessed | tf_op | source)
XLA Modules:
  0.0 3938.3 jit_solution(7130448153857479373)
XLA Ops:
  11.1 182.9 %all_gather.50 = bf16[1,768,2]{2,0,1:T(2,128)(2,1)S(1)} all-gather(bf16[1,12,2]{2,0,1:T(2,128)(2,1)S(1)} %copy.342), channel_id=1, replica_groups=mesh['section'=2,'ctx'=8,'fsdp'=8] {'ctx','fsdp'}, dimensions={1}, use_global_device_ids=true | all-gather | bytes 3120 | tf_op jit(solution)/shard_map/all_gather | solution.py:439
  197.5 166.0 %all-gather.13.cloned.1.call-done = bf16[1,768,2304]{2,0,1:T(2,128)(2,1)} async-done(((bf16[1,12,2304]{2,0,1:T(2,128)(2,1)}), bf16[1,768,2304]{2,0,1:T(2,128)(2,1)}) %all-gather.13.cloned.1.call-update) | async-done | bytes 3538960 | tf_op jit(solution)/shard_map/all_gather | solution.py:440
  384.8 312.4 %all-gather.19.cloned.1.call-done = bf16[1,768,768]{2,0,1:T(2,128)(2,1)} async-done(((bf16[1,12,768]{2,0,1:T(2,128)(2,1)}), bf16[1,768,768]{2,0,1:T(2,128)(2,1)}) %all-gather.19.cloned.1.call-update) | async-done | bytes 1179664 | tf_op jit(solution)/shard_map/all_gather | solution.py:441
  700.8 37.7 all-gather.15.cloned.1.call-done
  742.9 37.6 all-gather.17.cloned.1.call-done
  784.9 15.2 while.152
  800.8 10.3 while.153
  817.9 225.6 %all_gather.59 = bf16[1,768,8]{2,0,1:T(2,128)(2,1)S(1)} all-gather(bf16[1,12,8]{2,0,1:T(2,128)(2,1)S(1)} %copy.356), channel_id=1, replica_groups=mesh['section'=2,'ctx'=8,'fsdp'=8] {'ctx','fsdp'}, dimensions={1}, use_global_device_ids=true | all-gather | bytes 12480 | tf_op jit(solution)/shard_map/all_gather | solution.py:442
  1062.7 9.4 all-to-all-done.1
  1075.8 283.9 %all-gather.21.cloned.1.call-done = bf16[1,768,4096]{2,0,1:T(2,128)(2,1)} async-done(((bf16[1,12,4096]{2,0,1:T(2,128)(2,1)}), bf16[1,768,4096]{2,0,1:T(2,128)(2,1)}) %all-gather.21.cloned.1.call-update) | async-done | bytes 6291472 | tf_op jit(solution)/shard_map/all_gather | solution.py:443
  1359.6 11.7 copy.451
  1376.5 317.6 %all-gather.23.cloned.1.call-done = bf16[1,2048,768]{2,1,0:T(8,128)(2,1)} async-done(((bf16[1,32,768]{2,1,0:T(8,128)(2,1)}), bf16[1,2048,768]{2,1,0:T(8,128)(2,1)}) %all-gather.23.cloned.1.call-update) | async-done | bytes 3145744 | tf_op jit(solution)/shard_map/all_gather | solution.py:444
  1713.6 28.9 all-gather.29.cloned.1.call-done
  1746.9 37.0 all-gather.31.cloned.1.call-done
  1788.4 5.9 while.154
  1794.4 7.9 while.155
  1805.7 5.9 broadcast_select_fusion.11
  1825.6 9.0 broadcast_select_fusion.2
  1878.1 5.9 fusion.324
  1904.7 5.7 fusion.351
  1912.4 8.3 while.158
  1926.5 148.7 %while.159 = (s32[]{:T(128)}, f32[128,12,64]{0,2,1:T(8,128)}, f32[2,512,12,64]{1,0,3,2:T(2,128)}, f32[2,512,12,64]{1,0,3,2:T(2,128)}, bf16[2,512,12,64]{1,3,2,0:...) while((s32[]{:T(128)}, f32[128,12,64]{0,2,1:T(8,128)}, ...), condition=%wide.region_55.60_spmd.clone, body=%wide.region_54.59_spmd.clone.sunk | while | flops 512131712 | bytes 46990216 | solution.py:213
  1939.9 28.9 dynamic_update_slice.31
  1972.2 28.8 dynamic_update_slice.32
  2014.1 28.9 dynamic_update_slice.31
  2046.4 28.8 dynamic_update_slice.32
  2095.0 32.1 reduce-scatter.12.cloned.1.call-done
  2129.3 46.0 %reduce-scatter.14.cloned.1.call-done = f32[128,768]{0,1:T(8,128)} async-done(((f32[1024,768]{0,1:T(8,128)}), f32[128,768]{0,1:T(8,128)}) %reduce-scatter.14.cloned.1.call-update) | async-done | bytes 393232 | tf_op jit(solution)/shard_map/reduce_scatter | solution.py:385
  2197.5 29.5 all-gather.33.cloned.1.call-done
  2231.3 37.0 all-gather.35.cloned.1.call-done
  2272.8 6.0 while.156
  2279.4 7.9 while.157
  2292.4 6.7 broadcast_select_fusion.9
  2306.6 6.2 broadcast_select_fusion.3
  2313.2 12.5 broadcast_select_fusion
  2335.7 7.8 all-to-all-done.5
  2370.7 5.8 fusion.327
  2408.9 8.2 while.160
  2422.8 147.0 %while.161 = (s32[]{:T(128)}, f32[128,12,64]{0,2,1:T(8,128)}, f32[2,512,12,64]{1,0,3,2:T(2,128)}, f32[2,512,12,64]{1,0,3,2:T(2,128)}, bf16[2,512,12,64]{1,3,2,0:...) while((s32[]{:T(128)}, f32[128,12,64]{0,2,1:T(8,128)}, ...), condition=%wide.region_70.75_spmd.clone, body=%wide.region_69.74_spmd.clone.sunk | while | flops 512131712 | bytes 46992296 | solution.py:213
  2435.3 28.9 dynamic_update_slice.33
  2467.6 28.8 dynamic_update_slice.34
  2508.7 28.9 dynamic_update_slice.33
  2541.0 28.8 dynamic_update_slice.34
  2579.2 42.4 %reduce-scatter.16.cloned.1.call-done = f32[128,768]{0,1:T(8,128)} async-done(((f32[1024,768]{0,1:T(8,128)}), f32[128,768]{0,1:T(8,128)}) %reduce-scatter.16.cloned.1.call-update) | async-done | bytes 393232 | tf_op jit(solution)/shard_map/reduce_scatter | solution.py:384
  2624.5 45.1 %reduce-scatter.18.cloned.1.call-done = f32[128,768]{0,1:T(8,128)} async-done(((f32[1024,768]{0,1:T(8,128)}), f32[128,768]{0,1:T(8,128)}) %reduce-scatter.18.cloned.1.call-update) | async-done | bytes 393232 | tf_op jit(solution)/shard_map/reduce_scatter | solution.py:385
  2730.2 6.0 all-to-all-done.11
  2744.5 10.4 while.162
  2760.7 149.4 %while.163 = (s32[]{:T(128)}, f32[128,12,64]{0,2,1:T(8,128)}, f32[2,512,12,64]{1,0,3,2:T(2,128)}, f32[2,512,12,64]{1,0,3,2:T(2,128)}, bf16[2,512,12,64]{1,3,2,0:...) while((s32[]{:T(128)}, f32[128,12,64]{0,2,1:T(8,128)}, ...), condition=%wide.region_85.90_spmd.clone, body=%wide.region_84.89_spmd.clone.sunk | while | flops 512131712 | bytes 40676176 | solution.py:213
  2774.0 28.9 dynamic_update_slice.35
  2806.4 28.8 dynamic_update_slice.36
  2848.6 28.9 dynamic_update_slice.35
  2881.0 28.8 dynamic_update_slice.36
  2935.0 6.5 fusion.544
  2941.4 11.5 add_bitcast_fusion
  2953.0 15.4 copy.417
  2969.4 10.9 fusion.423
  2980.3 6.5 fusion.421
  2986.8 16.4 fusion.227
  3020.9 6.3 add_bitcast_fusion.1
  3027.3 10.4 copy.415
  3058.4 32.9 reduce-scatter.28.cloned.1.call-done
  3097.2 353.7 %all-reduce.29 = (f32[1,768,2]{1,2,0:T(2,128)S(1)}, f32[1,768,8]{1,2,0:T(8,128)S(1)}) all-reduce(f32[1,768,2]{1,2,0:T(2,128)S(1)} %fusion.584, f32[1,768,8]{1,2,0:T(8,128)} %fusion.393), channel_id=8, replica_groups=mesh['section'=2,'ctx'=8,'fsdp'=8] {'ctx','fsdp'}, use_global_device_ids=true, to_apply=%region_96.101.clone | all-reduce | flops 7680 | bytes 61440
  3460.4 103.0 %all-reduce.36.cloned.1.call-done = (f32[1,768,2304]{2,0,1:T(1,128)}, f32[1,768,768]{2,0,1:T(1,128)}) async-done(((f32[1,768,2304]{2,0,1:T(1,128)}, f32[1,768,768]{2,0,1:T(1,128)}), (f32[1,768,2304]{2,0,1:T(1,128)}, f32[1,768,768]{2,0,1:T(1,128)})) %all-reduce.36.cloned.1.call-update) | async-done | bytes 9437200
  3566.4 365.2 %reduce-scatter.24.cloned.1.call-done = f32[1,32,768]{2,1,0:T(8,128)} async-done(((f32[1,2048,768]{2,1,0:T(8,128)}), f32[1,32,768]{2,1,0:T(8,128)}) %reduce-scatter.24.cloned.1.call-update) | async-done | bytes 98320 | tf_op jit(solution)/shard_map/reduce_scatter | solution.py:547
  (1325 shorter events, 677.2 us)
Async XLA Ops:
  7.2 356.4 %all-gather.13.cloned.1.call-start = ((), (), s32[]{:S(2)}) async-start(), calls=%async_computation.21 | async-start | bytes 7188480 | tf_op jit(solution)/shard_map/all_gather | solution.py:440
  8.9 688.4 %all-gather.19.cloned.1.call-start = ((), (), s32[]{:S(2)}) async-start(), calls=%async_computation.24 | async-start | bytes 2396160 | tf_op jit(solution)/shard_map/all_gather | solution.py:441
  10.3 728.2 %all-gather.15.cloned.1.call-start = ((), (), s32[]{:S(2)}) async-start(), calls=%async_computation.22 | async-start | bytes 1769472 | tf_op jit(solution)/shard_map/all_gather | solution.py:238
  195.2 182.9 %copy-start.205 = (s32[1,1024]{1,0:T(1,128)}, s32[1,1024]{1,0:T(1,128)S(1)}, u32[]{:S(2)}) copy-start(s32[1,1024]{1,0:T(1,128)S(1)} %get-tuple-element.2373) | copy-start | bytes 12292
  195.2 182.9 %copy-start.207 = (s32[1,1024]{1,0:T(1,128)}, s32[1,1024]{1,0:T(1,128)S(1)}, u32[]{:S(2)}) copy-start(s32[1,1024]{1,0:T(1,128)S(1)} %get-tuple-element.2372) | copy-start | bytes 12292
  197.5 1503.0 %copy-start.148 = (f32[768]{0:T(1024)}, f32[768]{0:T(1024)S(1)}, u32[]{:S(2)}) copy-start(f32[768]{0:T(1024)S(1)} %get-tuple-element.1948) | copy-start | bytes 9220
  197.5 169.6 %copy-start.246 = (f32[128]{0:T(128)}, f32[128]{0:T(128)S(1)}, u32[]{:S(2)}) copy-start(f32[128]{0:T(128)S(1)} %add_rsqrt_fusion.5) | copy-start | bytes 1540
  197.5 171.4 %copy-start.19 = (bf16[2,1,128,768]{3,2,1,0:T(8,128)(2,1)S(1)}, bf16[2,1,128,768]{3,2,1,0:T(8,128)(2,1)}, u32[]{:S(2)}) copy-start(bf16[2,1,128,768]{3,2,1,0:T(8,128)(2,1)} %param.45) | copy-start | bytes 1179652
  370.3 410.2 %all-gather.17.cloned.1.call-start = ((), (), s32[]{:S(2)}) async-start(), calls=%async_computation.23 | async-start | bytes 1769472 | tf_op jit(solution)/shard_map/all_gather | solution.py:237
  373.8 326.4 %copy-start.124 = (bf16[128,12,32]{0,2,1:T(8,128)(2,1)}, bf16[128,12,32]{0,2,1:T(8,128)(2,1)S(1)}, u32[]{:S(2)}) copy-start(bf16[128,12,32]{0,2,1:T(8,128)(2,1)S(1)} %get-tuple-element.2340) | copy-start | bytes 294916
  373.8 326.4 %copy-start.127 = (bf16[128,12,32]{0,2,1:T(8,128)(2,1)}, bf16[128,12,32]{0,2,1:T(8,128)(2,1)S(1)}, u32[]{:S(2)}) copy-start(bf16[128,12,32]{0,2,1:T(8,128)(2,1)S(1)} %get-tuple-element.2341) | copy-start | bytes 294916
  374.7 671.0 %all-gather.25.cloned.1.call-start = ((), (), s32[]{:S(2)}) async-start(), calls=%async_computation.27 | async-start | bytes 7077888 | tf_op jit(solution)/shard_map/all_gather | solution.py:448
  375.3 678.8 %all-gather.27.cloned.1.call-start = ((), (), s32[]{:S(2)}) async-start(), calls=%async_computation.28 | async-start | bytes 3538944 | tf_op jit(solution)/shard_map/all_gather | solution.py:449
  375.8 983.8 %all-gather.21.cloned.1.call-start = ((), (), s32[]{:S(2)}) async-start(), calls=%async_computation.25 | async-start | bytes 12779520 | tf_op jit(solution)/shard_map/all_gather | solution.py:443
  376.7 1317.4 %all-gather.23.cloned.1.call-start = ((), (), s32[]{:S(2)}) async-start(), calls=%async_computation.26 | async-start | bytes 3194880 | tf_op jit(solution)/shard_map/all_gather | solution.py:444
  378.8 321.4 %copy-start.210 = (s32[128]{0:T(128)}, s32[128]{0:T(128)S(1)}, u32[]{:S(2)}) copy-start(s32[128]{0:T(128)S(1)} %get-tuple-element.3554) | copy-start | bytes 1540
  379.9 358.6 %copy-start.101 = (s32[128,2]{1,0:T(8,128)}, s32[128,2]{1,0:T(8,128)S(1)}, u32[]{:S(2)}) copy-start(s32[128,2]{1,0:T(8,128)S(1)} %get-tuple-element.2255) | copy-start | bytes 3076
  379.9 358.6 %copy-start.103 = (s32[128,2]{1,0:T(8,128)}, s32[128,2]{1,0:T(8,128)S(1)}, u32[]{:S(2)}) copy-start(s32[128,2]{1,0:T(8,128)S(1)} %get-tuple-element.2256) | copy-start | bytes 3076
  381.1 357.4 %copy-start.105 = (s32[128,2]{1,0:T(8,128)}, s32[128,2]{1,0:T(8,128)S(1)}, u32[]{:S(2)}) copy-start(s32[128,2]{1,0:T(8,128)S(1)} %get-tuple-element.2267) | copy-start | bytes 3076
  383.1 355.4 %copy-start.238 = (pred[256]{0:T(512)(128)(4,1)}, pred[256]{0:T(512)(128)(4,1)S(1)}, u32[]{:S(2)}) copy-start(pred[256]{0:T(512)(128)(4,1)S(1)} %get-tuple-element.2402) | copy-start | bytes 772
  384.2 354.3 %copy-start.252 = (s32[256]{0:T(256)}, s32[256]{0:T(256)S(1)}, u32[]{:S(2)}) copy-start(s32[256]{0:T(256)S(1)} %convert_reduce_fusion.2) | copy-start | bytes 3076
  812.7 232.8 %copy-start.46 = (f32[128,768]{1,0:T(8,128)}, f32[128,768]{1,0:T(8,128)S(1)}, u32[]{:S(2)}) copy-start(f32[128,768]{1,0:T(8,128)S(1)} %get-tuple-element.2408) | copy-start | bytes 1179652
  812.7 231.0 %copy-start.191 = (s32[128,2,1]{1,0,2:T(8,128)S(1)}, s32[128,2,1]{1,0,2:T(8,128)}, u32[]{:S(2)}) copy-start(s32[128,2,1]{1,0,2:T(8,128)} %bitcast_or_fusion.2) | copy-start | bytes 3076
  812.8 558.5 %copy-start.29 = (bf16[128,768]{1,0:T(8,128)(2,1)}, bf16[128,768]{1,0:T(8,128)(2,1)S(1)}, u32[]{:S(2)}) copy-start(bf16[128,768]{1,0:T(8,128)(2,1)S(1)} %multiply_convert_fusion.4) | copy-start | bytes 589828
  814.3 231.3 %all-to-all-start = ((bf16[8,40,768]{2,1,0:T(8,128)(2,1)}), bf16[8,40,768]{2,1,0:T(8,128)(2,1)S(1)}, u32[]{:S(2)}, u32[]{:S(2)}) async-start(bf16[8,40,768]{2,1,0:T(8,128)(2,1)} %bitcast.16), calls=%async_computation | async-start | bytes 983040 | tf_op jit(solution)/shard_map/all_to_all | solution.py:257
  1058.4 13.7 all-to-all-start.1
  1062.0 680.5 %all-gather.29.cloned.1.call-start = ((), (), s32[]{:S(2)}) async-start(), calls=%async_computation.29 | async-start | bytes 1769472 | tf_op jit(solution)/shard_map/all_gather | solution.py:238
  1376.5 324.1 %copy-start.11 = (bf16[1,768,2304]{2,1,0:T(8,128)(2,1)S(1)}, bf16[1,768,2304]{2,1,0:T(8,128)(2,1)}, u32[]{:S(2)}) copy-start(bf16[1,768,2304]{2,1,0:T(8,128)(2,1)} %copy-done.10) | copy-start | bytes 10616836
  1697.4 2.4 collective-permute-start
  1703.1 80.8 %all-gather.31.cloned.1.call-start = ((), (), s32[]{:S(2)}) async-start(), calls=%async_computation.30 | async-start | bytes 1769472 | tf_op jit(solution)/shard_map/all_gather | solution.py:237
  1813.1 12.5 all-to-all-start.2
  1840.4 11.6 all-to-all-start.3
  1858.8 11.6 all-to-all-start.6
  1884.0 19.1 all-to-all-start.7
  1888.2 238.9 %reduce-scatter.12.cloned.1.call-start = ((), (), s32[]{:S(2)}) async-start(), calls=%async_computation.33 | async-start | bytes 3538944 | tf_op jit(solution)/shard_map/reduce_scatter | solution.py:384
  2079.5 95.7 %reduce-scatter.14.cloned.1.call-start = ((), (), s32[]{:S(2)}) async-start(), calls=%async_computation.34 | async-start | bytes 3538944 | tf_op jit(solution)/shard_map/reduce_scatter | solution.py:385
  2084.0 143.0 %all-gather.33.cloned.1.call-start = ((), (), s32[]{:S(2)}) async-start(), calls=%async_computation.31 | async-start | bytes 1769472 | tf_op jit(solution)/shard_map/all_gather | solution.py:238
  2089.2 89.4 %copy-start.12 = (bf16[1,768,2304]{2,1,0:T(8,128)(2,1)S(1)}, bf16[1,768,2304]{2,1,0:T(8,128)(2,1)}, u32[]{:S(2)}) copy-start(bf16[1,768,2304]{2,1,0:T(8,128)(2,1)} %copy-done.10) | copy-start | bytes 10616836
  2092.9 85.7 %copy-start.149 = (f32[768]{0:T(1024)S(1)}, f32[768]{0:T(1024)}, u32[]{:S(2)}) copy-start(f32[768]{0:T(1024)} %copy-done.148) | copy-start | bytes 9220
  2092.9 85.7 %collective-permute-start.1 = (bf16[128,768]{1,0:T(8,128)(2,1)}, bf16[128,768]{1,0:T(8,128)(2,1)}, u32[]{:S(2)}, u32[]{:S(2)}) collective-permute-start(bf16[128,768]{1,0:T(8,128)(2,1)} %fusion.381), channel_id=1, source_target_pairs={{0,64},{1,65},{2,66},{3,67},{4,68},{5,69},{6,70},{7,71},{8,72},{9,... | collective-permute-start | bytes 589832 | tf_op jit(solution)/shard_map/ppermute | solution.py:24
  2186.6 81.8 %all-gather.35.cloned.1.call-start = ((), (), s32[]{:S(2)}) async-start(), calls=%async_computation.32 | async-start | bytes 1769472 | tf_op jit(solution)/shard_map/all_gather | solution.py:237
  2191.6 3.3 collective-permute-start.2
  2300.5 12.7 all-to-all-start.4
  2329.9 13.6 all-to-all-start.5
  2350.6 12.3 all-to-all-start.8
  2359.4 42.0 %copy-start.80 = (f32[128,2048]{1,0:T(8,128)}, f32[128,2048]{1,0:T(8,128)S(1)}, u32[]{:S(2)}) copy-start(f32[128,2048]{1,0:T(8,128)S(1)} %get-tuple-element.2304) | copy-start | bytes 3145732
  2376.5 23.4 all-to-all-start.9
  2380.7 241.0 %reduce-scatter.16.cloned.1.call-start = ((), (), s32[]{:S(2)}) async-start(), calls=%async_computation.35 | async-start | bytes 3538944 | tf_op jit(solution)/shard_map/reduce_scatter | solution.py:384
  2574.2 95.5 %reduce-scatter.18.cloned.1.call-start = ((), (), s32[]{:S(2)}) async-start(), calls=%async_computation.36 | async-start | bytes 3538944 | tf_op jit(solution)/shard_map/reduce_scatter | solution.py:385
  2578.5 92.2 %copy-start.13 = (bf16[1,768,2304]{2,1,0:T(8,128)(2,1)S(1)}, bf16[1,768,2304]{2,1,0:T(8,128)(2,1)}, u32[]{:S(2)}) copy-start(bf16[1,768,2304]{2,1,0:T(8,128)(2,1)} %copy-done.10) | copy-start | bytes 10616836
  2578.5 92.2 %copy-start.150 = (f32[768]{0:T(1024)S(1)}, f32[768]{0:T(1024)}, u32[]{:S(2)}) copy-start(f32[768]{0:T(1024)} %copy-done.148) | copy-start | bytes 9220
  2676.2 3.5 collective-permute-start.3
  2690.2 19.6 all-to-all-start.10
  2709.8 32.0 copy-start.227
  2720.7 15.4 all-to-all-start.11
  2726.3 292.2 %reduce-scatter.22.cloned.1.call-start = ((), (), s32[]{:S(2)}) async-start(), calls=%async_computation.38 | async-start | bytes 3538944 | tf_op jit(solution)/shard_map/reduce_scatter | solution.py:385
  2804.7 30.5 copy-start.202
  2914.4 105.1 %reduce-scatter.20.cloned.1.call-start = ((), (), s32[]{:S(2)}) async-start(), calls=%async_computation.37 | async-start | bytes 3538944 | tf_op jit(solution)/shard_map/reduce_scatter | solution.py:384
  2918.7 172.6 %reduce-scatter.28.cloned.1.call-start = ((), (), s32[]{:S(2)}) async-start(), calls=%async_computation.41 | async-start | bytes 3538944 | tf_op jit(solution)/shard_map/reduce_scatter | solution.py:553
  2930.3 526.1 %all-reduce.34.cloned.1.call-start = ((), (), s32[]{:S(2)}) async-start(), calls=%async_computation.42 | async-start | bytes 25165824
  2968.4 489.6 %reduce-scatter.26.cloned.1.call-start = ((), (), s32[]{:S(2)}) async-start(), calls=%async_computation.40 | async-start | bytes 7077888 | tf_op jit(solution)/shard_map/reduce_scatter | solution.py:550
  3003.3 560.1 %all-reduce.36.cloned.1.call-start = ((), (), s32[]{:S(2)}) async-start(), calls=%async_computation.43 | async-start | bytes 18874368
  3037.7 893.9 %reduce-scatter.24.cloned.1.call-start = ((), (), s32[]{:S(2)}) async-start(), calls=%async_computation.39 | async-start | bytes 6389760 | tf_op jit(solution)/shard_map/reduce_scatter | solution.py:547
  3053.1 40.1 %copy-start.14 = (bf16[1,768,2304]{2,1,0:T(8,128)(2,1)S(1)}, bf16[1,768,2304]{2,1,0:T(8,128)(2,1)}, u32[]{:S(2)}) copy-start(bf16[1,768,2304]{2,1,0:T(8,128)(2,1)} %copy-done.10) | copy-start | bytes 10616836
  (309 other events, 1623.6 us)
Sparse Core Ops, SparseCore 0:
  10.2 353.2 all-gather.12
  365.8 331.4 all-gather.18
  699.5 39.0 all-gather.14
  740.6 39.8 all-gather.16
  782.7 91.0 all-gather.24
  875.9 62.0 all-gather.26
  939.7 419.8 all-gather.20
  1361.2 332.8 all-gather.22
  1703.2 39.2 all-gather.28
  1744.0 39.8 all-gather.30
  2079.7 47.3 reduce-scatter.11
  2129.3 45.8 reduce-scatter.13
  2186.6 40.3 all-gather.32
  2228.5 39.8 all-gather.34
  2574.3 47.3 reduce-scatter.15
  2623.9 45.6 reduce-scatter.17
  2914.6 46.1 reduce-scatter.21
  2963.0 45.3 reduce-scatter.19
  3012.2 79.0 reduce-scatter.27
  3096.4 187.1 all-reduce.33
  3287.5 98.3 reduce-scatter.25
  3391.4 172.0 all-reduce.35
  3566.5 364.9 reduce-scatter.23
where the time goes:
time: 3980 us; the launch traced here: 3940 us
  waiting for transfers between devices  2000 us (50%)
  blocking collectives  762 us (19%)
  local copies, waits for them, and re-layouts  626 us (16%)
  matrix products  360 us (9%)
  other arithmetic  110 us (3%)
  starting transfers between devices  60.1 us (2%)
    dynamic_update_slice x24, local copies, waits for them, and re-layouts, attend_backward(): lax.scan(grad_step, jnp.zeros((row_count, HEADS, HEAD_DIM), jnp.float32),...  373 us
    reduce_scatter x1, waiting for transfers between devices, on_device(): lax.psum_scatter(dense_sum[5][None], ('ctx', 'fsdp'), scatter_dimension=1...  365 us
    unnamed x1, blocking collectives  354 us
    all_gather x1, waiting for transfers between devices, on_device(): lax.all_gather(shared_down, ('ctx', 'fsdp'), axis=1, tiled=True)  318 us
    all_gather x1, waiting for transfers between devices, on_device(): lax.all_gather(w_out, ('ctx', 'fsdp'), axis=1, tiled=True)  312 us
    all_gather x1, waiting for transfers between devices, on_device(): lax.all_gather(shared_gate_up, ('ctx', 'fsdp'), axis=1, tiled=True)  284 us
    all_gather x1, blocking collectives, on_device(): lax.all_gather(router, ('ctx', 'fsdp'), axis=1, tiled=True)  226 us
    all_gather x1, blocking collectives, on_device(): lax.all_gather(gains, ('ctx', 'fsdp'), axis=1, tiled=True)  183 us
  transfers between devices with their start and end apart: 39, of which 28 were waited for; matrix products, arithmetic and copies ran while one was open for 9% of the time, Pallas kernels for 0%

commit v1 on v0

v1 whole, which is shorter than its diff:
```python
import functools
import math

import jax
import jax.numpy as jnp
from jax import lax
from jax.experimental import pallas as pl
from jax.experimental.pallas import tpu as pltpu
from jax.sharding import PartitionSpec as P

MESH = pl.DeviceIdType.MESH
ANY = pl.BlockSpec(memory_space=pl.ANY)
VMEM = pl.BlockSpec(memory_space=pltpu.VMEM)
DMA = pltpu.SemaphoreType.DMA

D = 768
FF = 2048
WIDE = 3072
SMALL = 128
PACK = WIDE + 2 * FF + SMALL
OWN = 12
HEADS = 12
HEAD_DIM = 64
TOP = 2
CONT = 8
EXPERTS = 8
SEQ = 1024
ROWS = 128
CAP = 40
PAD_CAP = 48
SLOTS = EXPERTS * PAD_CAP
SCALE = 1.0 / math.sqrt(HEAD_DIM)
EPS = 1e-06
NEG = -1e30
HIGH = lax.Precision.HIGHEST


def place_ids():
    section = lax.axis_index("section")
    ctx = lax.axis_index("ctx")
    fsdp = lax.axis_index("fsdp")
    return section, ctx // 4, lax.rem(ctx, 4), fsdp // 2, lax.rem(fsdp, 2)


def ctx_of(half, ring):
    return lax.rem(half + 2, 2) * 4 + lax.rem(ring + 4, 4)


def fsdp_of(ring, half):
    return lax.rem(ring + 4, 4) * 2 + lax.rem(half + 2, 2)


def neighbours():
    section, a, z, y, h = place_ids()
    ctx, fsdp = ctx_of(a, z), fsdp_of(y, h)
    return dict(
        core=(1 - section, ctx, fsdp),
        zp=(section, ctx_of(a, z + 1), fsdp),
        zm=(section, ctx_of(a, z - 1), fsdp),
        zx=(section, ctx_of(a + 1, z), fsdp),
        yp=(section, ctx, fsdp_of(y + 1, h)),
        ym=(section, ctx, fsdp_of(y - 1, h)),
        yx=(section, ctx, fsdp_of(y, h + 1)),
    )


def greet(devices):
    barrier = pltpu.get_barrier_semaphore()
    for device in devices:
        pl.semaphore_signal(barrier, inc=1, device_id=device, device_id_type=MESH)
    pl.semaphore_wait(barrier, len(devices))


def rows_at(ref, block, rows, part=None):
    if part is None:
        return ref.at[pl.ds(pl.multiple_of(block * rows, 16), rows)]
    half = rows // 2
    return ref.at[pl.ds(pl.multiple_of(block * rows + part * half, 16), half)]


class Hop:
    def __init__(self, sources, targets, device, send, recv):
        self.copies = [
            pltpu.make_async_remote_copy(s, t, send.at[i], recv.at[i], device_id=device, device_id_type=MESH)
            for i, (s, t) in enumerate(zip(sources, targets))
        ]

    def start(self):
        for copy in self.copies:
            copy.start()
        return self

    def wait_recv(self):
        for copy in self.copies:
            copy.wait_recv()

    def wait_send(self):
        for copy in self.copies:
            copy.wait_send()


def gather_kernel(
    pack, sd, egu, ed, sel,
    w_wide, w_gu, w_small, w_sd, w_egu, w_ed,
    packs, own_wide, own_gu, own_small, own_sd,
    s_send, s_recv, d_send, d_recv, e_send, e_recv, c_send, c_recv, l_sem,
):
    section, a, z, y, h = place_ids()
    ctx, fsdp = ctx_of(a, z), fsdp_of(y, h)
    near = neighbours()
    others = [(dy, dh) for dy in (1, 3, 2, 0) for dh in (0, 1) if (dy, dh) != (0, 0)]
    f_peers = [(section, ctx, fsdp_of(y + dy, h + dh)) for dy, dh in others]
    greet([near["core"], near["zp"], near["zm"], near["zx"]] + f_peers)

    first = []
    for k, device in enumerate(f_peers):
        hop = Hop(
            [pack, sd], [rows_at(packs, fsdp, 16), rows_at(own_sd, fsdp, 32)], device, s_send.at[k], s_recv.at[k]
        )
        first.append(hop.start())
    locals_ = [
        pltpu.make_async_copy(pack, rows_at(packs, fsdp, 16), l_sem.at[0]),
        pltpu.make_async_copy(sd, rows_at(own_sd, fsdp, 32), l_sem.at[1]),
    ]
    for copy in locals_:
        copy.start()

    me_w = [w.at[section] for w in (w_wide, w_gu, w_small, w_sd)]
    me_e = [w.at[section] for w in (w_egu, w_ed)]
    d_rows = (96, 96, 96, 256)
    e_rows = (96, 256)

    def dense(block, part=None):
        return [rows_at(w, block, r, part) for w, r in zip(me_w, d_rows)]

    def expert(block, part=None):
        return [rows_at(w, block, r, part) for w, r in zip(me_e, e_rows)]

    cores = []

    def to_core(refs, block_refs, index):
        cores.append(Hop(refs, block_refs, near["core"], c_send.at[index], c_recv.at[index]).start())

    for hop in first:
        hop.wait_recv()
    for copy in locals_:
        copy.wait()

    e_own = [egu, ed]
    e_hops = {}

    def e_hop(index, refs, block_refs, device):
        e_hops[index] = Hop(refs, block_refs, near[device], e_send.at[index], e_recv.at[index]).start()

    for index, device in ((0, "yp"), (1, "ym"), (2, "yx")):
        e_hop(index, e_own, expert(fsdp), device)

    for target, start, width in ((own_wide, 0, WIDE), (own_gu, WIDE, 2 * FF), (own_small, WIDE + 2 * FF, SMALL)):
        step = min(width, 512)

        @pl.loop(0, width // step)
        def _(j, target=target, start=start, step=step):
            off = pl.multiple_of(j * step, 128)
            block = packs[:, pl.ds(start + off, step)]
            target[:, pl.ds(off, step)] = jnp.dot(sel[...], block, preferred_element_type=jnp.float32).astype(jnp.bfloat16)

    d_own = [own_wide, own_gu, own_small, own_sd]
    d_hops = {}

    def d_hop(index, refs, block_refs, device):
        d_hops[index] = Hop(refs, block_refs, near[device], d_send.at[index], d_recv.at[index]).start()

    for index, device in ((0, "zp"), (1, "zm"), (2, "zx")):
        d_hop(index, d_own, dense(ctx), device)
    own_copies = [
        pltpu.make_async_copy(s, t, l_sem.at[2 + i])
        for i, (s, t) in enumerate(zip(d_own + e_own, dense(ctx) + expert(fsdp)))
    ]
    for copy in own_copies:
        copy.start()
    to_core(d_own + e_own, dense(ctx) + expert(fsdp), 0)

    def e_block(dy, dh):
        return fsdp_of(y + dy, h + dh)

    def d_block(dz, da):
        return ctx_of(a + da, z + dz)

    def e_pass(index, block, part, device):
        e_hop(index, expert(block, part), expert(block, part), device)

    def d_pass(index, block, part, device):
        d_hop(index, dense(block, part), dense(block, part), device)

    e_hops[0].wait_recv()
    e_pass(3, e_block(-1, 0), 0, "yp")
    e_hops[1].wait_recv()
    e_pass(4, e_block(1, 0), 1, "ym")
    d_hops[0].wait_recv()
    d_pass(3, d_block(-1, 0), 0, "zp")
    d_hops[1].wait_recv()
    d_pass(4, d_block(1, 0), 1, "zm")
    e_hops[2].wait_recv()
    e_pass(5, e_block(0, 1), None, "yp")
    e_pass(6, e_block(0, 1), None, "ym")
    d_hops[2].wait_recv()
    d_pass(5, d_block(0, 1), None, "zp")
    d_pass(6, d_block(0, 1), None, "zm")
    to_core(dense(d_block(-1, 0)) + expert(e_block(-1, 0)), dense(d_block(-1, 0)) + expert(e_block(-1, 0)), 1)
    to_core(dense(d_block(1, 0)) + expert(e_block(1, 0)), dense(d_block(1, 0)) + expert(e_block(1, 0)), 2)
    to_core(dense(d_block(0, 1)) + expert(e_block(0, 1)), dense(d_block(0, 1)) + expert(e_block(0, 1)), 3)
    d_hops[3].wait_recv()
    d_hops[4].wait_recv()
    d_pass(7, d_block(2, 0), None, "zx")
    e_hops[3].wait_recv()
    e_hops[4].wait_recv()
    to_core(dense(d_block(2, 0)) + expert(e_block(2, 0)), dense(d_block(2, 0)) + expert(e_block(2, 0)), 4)
    e_hops[5].wait_recv()
    e_pass(7, e_block(-1, 1), 0, "yp")
    e_hops[6].wait_recv()
    e_pass(8, e_block(1, 1), 1, "ym")
    d_hops[5].wait_recv()
    to_core(dense(d_block(-1, 1)) + expert(e_block(-1, 1)), dense(d_block(-1, 1)) + expert(e_block(-1, 1)), 5)
    d_hops[6].wait_recv()
    to_core(dense(d_block(1, 1)) + expert(e_block(1, 1)), dense(d_block(1, 1)) + expert(e_block(1, 1)), 6)
    d_hops[7].wait_recv()
    e_hops[7].wait_recv()
    e_hops[8].wait_recv()
    to_core(dense(d_block(2, 1)) + expert(e_block(2, 1)), dense(d_block(2, 1)) + expert(e_block(2, 1)), 7)
    for copy in own_copies:
        copy.wait()
    for hop in first + list(d_hops.values()) + list(e_hops.values()):
        hop.wait_send()
    for hop in cores:
        hop.wait_recv()
        hop.wait_send()


def gather_weights(pack, sd, egu, ed):
    rows = jnp.arange(96)
    cols = jnp.arange(128)
    sel = ((rows[:, None] // OWN == cols[None, :] // 16) & (rows[:, None] % OWN == cols[None, :] % 16)).astype(jnp.bfloat16)
    bf = jnp.bfloat16
    shapes = [(2, D, WIDE), (2, D, 2 * FF), (2, D, SMALL), (2, FF, D), (2, D, 2 * FF), (2, FF, D)]
    return pl.pallas_call(
        gather_kernel,
        out_shape=[jax.ShapeDtypeStruct(s, bf) for s in shapes],
        in_specs=[ANY, ANY, ANY, ANY, VMEM],
        out_specs=[ANY] * 6,
        scratch_shapes=[
            pltpu.VMEM((128, PACK), bf),
            pltpu.VMEM((96, WIDE), bf),
            pltpu.VMEM((96, 2 * FF), bf),
            pltpu.VMEM((96, SMALL), bf),
            pltpu.VMEM((256, D), bf),
            DMA((7, 2)), DMA((7, 2)),
            DMA((8, 4)), DMA((8, 4)),
            DMA((9, 2)), DMA((9, 2)),
            DMA((8, 6)), DMA((8, 6)),
            DMA((8,)),
        ],
        compiler_params=pltpu.CompilerParams(collective_id=0, has_side_effects=True, vmem_limit_bytes=48 << 20),
        name="gather_weights",
    )(pack, sd, egu, ed, sel)


def exchange_kernel(eight_from, with_eight, with_four, *refs):
    count = int(with_eight) + int(with_four)
    sources, targets = refs[:count], refs[count : 2 * count]
    send8, recv8, send4, recv4, l_sem = refs[2 * count :]
    section, a, z, y, h = place_ids()
    fsdp = fsdp_of(y, h)
    ctx = ctx_of(a, z)
    offsets = [(0, 1), (0, 3), (0, 2)]
    if with_eight:
        offsets = [(1, 0), (1, 1), (1, 3), (1, 2)] + offsets
    peers = [(ctx_of(a + da, z + dz), lax.rem(z + dz, 4)) for da, dz in offsets]
    greet([(section, c, fsdp) for c, _ in peers])
    copies = []
    for k, ((da, dz), (c, zz)) in enumerate(zip(offsets, peers)):
        device = (section, c, fsdp)
        if with_eight:
            block = c if eight_from == 8 else zz
            copies.append(
                pltpu.make_async_remote_copy(
                    sources[0].at[block], targets[0].at[ctx], send8.at[k], recv8.at[k], device_id=device, device_id_type=MESH
                )
            )
        if with_four and da == 0:
            copies.append(
                pltpu.make_async_remote_copy(
                    sources[-1].at[zz], targets[-1].at[z], send4.at[k], recv4.at[k], device_id=device, device_id_type=MESH
                )
            )
    for copy in copies:
        copy.start()
    stays = []
    if with_eight:
        stays.append(pltpu.make_async_copy(sources[0].at[ctx if eight_from == 8 else z], targets[0].at[ctx], l_sem.at[0]))
    if with_four:
        stays.append(pltpu.make_async_copy(sources[-1].at[z], targets[-1].at[z], l_sem.at[1]))
    for copy in stays:
        copy.start()
    for copy in stays + copies:
        copy.wait()


def exchange(name, collective_id, eight=None, four=None):
    arrays = [v for v in (eight, four) if v is not None]
    shapes = []
    if eight is not None:
        shapes.append(jax.ShapeDtypeStruct((8,) + eight.shape[1:], eight.dtype))
    if four is not None:
        shapes.append(jax.ShapeDtypeStruct(four.shape, four.dtype))
    return pl.pallas_call(
        functools.partial(exchange_kernel, 0 if eight is None else eight.shape[0], eight is not None, four is not None),
        out_shape=shapes,
        in_specs=[ANY] * len(arrays),
        out_specs=[ANY] * len(arrays),
        scratch_shapes=[DMA((7,)), DMA((7,)), DMA((7,)), DMA((7,)), DMA((2,))],
        compiler_params=pltpu.CompilerParams(collective_id=collective_id, has_side_effects=True),
        name=name,
    )(*arrays)


def visible_keys(qidx, qlab, klab):
    kidx = lax.broadcasted_iota(jnp.int32, (qidx.shape[0], klab.shape[1]), 1)
    return (kidx <= qidx) & ((klab == 0) | (klab == qlab))


def attend_kernel(q_ref, kv_ref, qidx_ref, qlab_ref, klab_ref, o_ref, lse_ref):
    seen = visible_keys(qidx_ref[...], qlab_ref[...], klab_ref[...])
    for head in range(3):
        q = q_ref[:, 64 * head : 64 * head + 64]
        k = kv_ref[:, 64 * head : 64 * head + 64]
        v = kv_ref[:, 192 + 64 * head : 256 + 64 * head]
        scores = lax.dot_general(q, k, (((1,), (1,)), ((), ())), preferred_element_type=jnp.float32) * SCALE
        scores = jnp.where(seen, scores, NEG)
        top = jnp.max(scores, axis=-1, keepdims=True)
        weights = jnp.exp(scores - top)
        total = jnp.sum(weights, axis=-1, keepdims=True)
        probs = (weights / total).astype(jnp.bfloat16)
        out = jnp.dot(probs, v, preferred_element_type=jnp.float32)
        o_ref[:, 64 * head : 64 * head + 64] = out.astype(jnp.bfloat16)
        lse_ref[:, head : head + 1] = top + jnp.log(total)


def attend_back_kernel(q_ref, kv_ref, do_ref, lse_ref, qidx_ref, qlab_ref, klab_ref, dq_ref, dkv_ref, acc):
    step = pl.program_id(0)

    @pl.when(step == 0)
    def _():
        acc[...] = jnp.zeros_like(acc)

    seen = visible_keys(qidx_ref[...], qlab_ref[...], klab_ref[...])
    rows = (((0,), (0,)), ((), ()))
    cols = (((1,), (1,)), ((), ()))
    for head in range(3):
        span = slice(64 * head, 64 * head + 64)
        vspan = slice(192 + 64 * head, 256 + 64 * head)
        q = q_ref[:, span]
        k = kv_ref[:, span]
        v = kv_ref[:, vspan]
        do = do_ref[:, span]
        scores = lax.dot_general(q, k, cols, preferred_element_type=jnp.float32) * SCALE
        probs = jnp.where(seen, jnp.exp(scores - lse_ref[:, head : head + 1]), 0.0)
        dprobs = lax.dot_general(do, v, cols, preferred_element_type=jnp.float32)
        delta = jnp.sum(probs * dprobs, axis=-1, keepdims=True)
        dscores = (probs * (dprobs - delta)).astype(jnp.bfloat16)
        dq_ref[:, span] = (jnp.dot(dscores, k, preferred_element_type=jnp.float32) * SCALE).astype(jnp.bfloat16)
        acc[:, span] += lax.dot_general(dscores, q, rows, preferred_element_type=jnp.float32) * SCALE
        acc[:, vspan] += lax.dot_general(probs.astype(jnp.bfloat16), do, rows, preferred_element_type=jnp.float32)

    @pl.when(step == pl.num_programs(0) - 1)
    def _():
        dkv_ref[...] = acc[...].astype(jnp.bfloat16)


def row_block(width):
    return pl.BlockSpec((128, width), lambda i: (i, 0))


def whole(rows, width):
    return pl.BlockSpec((rows, width), lambda i: (0, 0))


def attend(q, kv, qidx, qlab, klab):
    return pl.pallas_call(
        attend_kernel,
        grid=(4,),
        out_shape=[jax.ShapeDtypeStruct((512, 192), jnp.bfloat16), jax.ShapeDtypeStruct((512, 128), jnp.float32)],
        in_specs=[row_block(192), whole(1024, 384), row_block(1), row_block(1), whole(1, 1024)],
        out_specs=[row_block(192), row_block(128)],
        compiler_params=pltpu.CompilerParams(vmem_limit_bytes=40 << 20),
        name="attend",
    )(q, kv, qidx, qlab, klab)


def attend_back(q, kv, do, lse, qidx, qlab, klab):
    return pl.pallas_call(
        attend_back_kernel,
        grid=(4,),
        out_shape=[jax.ShapeDtypeStruct((512, 192), jnp.bfloat16), jax.ShapeDtypeStruct((1024, 384), jnp.bfloat16)],
        in_specs=[row_block(192), whole(1024, 384), row_block(192), row_block(128), row_block(1), row_block(1), whole(1, 1024)],
        out_specs=[row_block(192), whole(1024, 384)],
        scratch_shapes=[pltpu.VMEM((1024, 384), jnp.float32)],
        compiler_params=pltpu.CompilerParams(vmem_limit_bytes=40 << 20),
        name="attend_back",
    )(q, kv, do, lse, qidx, qlab, klab)


LEFT = (("na", D, 128), ("at", D, 128), ("nf", D, 128), ("sh", FF, 128), ("rc", D, SLOTS), ("hd", FF, SLOTS))
RIGHT = (("qkv", 128, 3 * D), ("pr", 128, D), ("gu", 128, 2 * FF), ("sd", 128, D), ("j", SLOTS, 2 * FF), ("er", SLOTS, D))
N_OPS = len(LEFT) + len(RIGHT)
DENSE = (("wide", "na", "qkv", 96, 0, 3 * D), ("wide", "at", "pr", 96, 3 * D, D), ("gu", "nf", "gu", 96, 0, 2 * FF), ("sd", "sh", "sd", 256, 0, D))
EXPERT = (("egu", "rc", "j", 96, 0, 2 * FF), ("ed", "hd", "er", 256, 0, D))


def grads_kernel(*refs):
    lower, upper = refs[:N_OPS], refs[N_OPS : 2 * N_OPS]
    small, sel_t = refs[2 * N_OPS : 2 * N_OPS + 2]
    out_pack, out_sd, out_egu, out_ed = refs[2 * N_OPS + 2 : 2 * N_OPS + 6]
    rest = refs[2 * N_OPS + 6 :]
    held = rest[:N_OPS]
    (b_wide, b_gu, b_small, b_sd, c_gu, c_sd, packs, in_pack, in_sd,
     o_send, o_recv, o_local, d_send, d_recv, e_send, e_recv, s_send, s_recv) = rest[N_OPS:]
    names = [n for n, _, _ in LEFT] + [n for n, _, _ in RIGHT]
    ops = dict(zip(names, held))
    section, a, z, y, h = place_ids()
    ctx, fsdp = ctx_of(a, z), fsdp_of(y, h)
    near = neighbours()
    others = [(dy, dh) for dy in (1, 3, 2, 0) for dh in (0, 1) if (dy, dh) != (0, 0)]
    f_peers = [(section, ctx, fsdp_of(y + dy, h + dh)) for dy, dh in others]
    greet([near["core"], near["zp"], near["zm"], near["zx"]] + f_peers)

    def slot_of(i, which):
        n, r, c = (LEFT + RIGHT)[i]
        if i < len(LEFT):
            return held[i].at[:, pl.ds(which * c, c)]
        return held[i].at[pl.ds(which * r, r)]

    def bring(mine, theirs):
        for i in range(N_OPS):
            pltpu.make_async_remote_copy(
                theirs[i], slot_of(i, 1), o_send.at[i], o_recv.at[i], device_id=near["core"], device_id_type=MESH
            ).start()
            pltpu.make_async_copy(mine[i], slot_of(i, 0), o_local.at[i]).start()

    @pl.when(section == 0)
    def _():
        bring(lower, upper)

    @pl.when(section == 1)
    def _():
        bring(upper, lower)

    def ready(wanted):
        for i, n in enumerate(names):
            if n in wanted:
                pltpu.make_async_copy(lower[i], slot_of(i, 0), o_local.at[i]).wait()
                pltpu.make_async_remote_copy(
                    lower[i], slot_of(i, 1), o_send.at[i], o_recv.at[i], device_id=near["core"], device_id_type=MESH
                ).wait_recv()

    kinds = dict(wide=b_wide, gu=b_gu, small=b_small, sd=b_sd, egu=c_gu, ed=c_sd)

    def combine(pieces, block, slot, adds=(), part=None, target=None):
        for kind, left, right, rows, first, width in pieces:
            n = rows if part is None else rows // 2
            off = 0 if part is None else part * n
            lhs_rows = pl.ds(pl.multiple_of(block * rows + off, 16), n)

            @pl.loop(0, width // 256)
            def _(j, kind=kind, left=left, right=right, first=first, n=n, off=off, lhs_rows=lhs_rows):
                at = pl.ds(pl.multiple_of(j * 256, 256), 256)
                to = pl.ds(pl.multiple_of(first + j * 256, 256), 256)
                total = jnp.dot(ops[left][lhs_rows, :], ops[right][:, at], preferred_element_type=jnp.float32)
                for other in adds:
                    total += kinds[kind][other, off : off + n, to].astype(jnp.float32)
                if target is None:
                    kinds[kind][slot, off : off + n, to] = total.astype(jnp.bfloat16)
                else:
                    target[kind][off : off + n, to] = total

        if pieces is DENSE:
            n = 96 if part is None else 48
            off = 0 if part is None else part * n
            total = small[pl.ds(pl.multiple_of(block * 96 + off, 16), n), :]
            for other in adds:
                total += b_small[other, off : off + n, :].astype(jnp.float32)
            b_small[slot, off : off + n, :] = total.astype(jnp.bfloat16)

    def views(pieces, slot, part):
        if pieces is DENSE:
            bufs = ((b_wide, 96), (b_gu, 96), (b_small, 96), (b_sd, 256))
        else:
            bufs = ((c_gu, 96), (c_sd, 256))
        return [rows_at(b.at[slot], 0, r, part) for b, r in bufs]

    hops = {}

    def send(pieces, index, slot, to_slot, device, part=None):
        sems = (d_send, d_recv) if pieces is DENSE else (e_send, e_recv)
        tag = "d" if pieces is DENSE else "e"
        hops[tag, index] = Hop(
            views(pieces, slot, part), views(pieces, to_slot, part), near[device], sems[0].at[index], sems[1].at[index]
        ).start()

    def d_block(dz, da):
        return ctx_of(a + da, z + dz)

    def e_block(dy, dh):
        return fsdp_of(y + dy, h + dh)

    ready(("na", "qkv", "at", "pr", "nf", "gu", "sh", "sd"))
    combine(DENSE, d_block(2, 1), 0)
    send(DENSE, 0, 0, 1, "zx")
    combine(DENSE, d_block(-1, 1), 2)
    send(DENSE, 1, 2, 5, "zm")
    combine(DENSE, d_block(1, 1), 3)
    send(DENSE, 2, 3, 6, "zp")
    ready(("rc", "j", "hd", "er"))
    combine(EXPERT, e_block(2, 1), 0)
    send(EXPERT, 0, 0, 4, "ym", 0)
    send(EXPERT, 1, 0, 4, "yp", 1)
    combine(EXPERT, e_block(2, 0), 1)
    send(EXPERT, 2, 1, 5, "ym", 0)
    send(EXPERT, 3, 1, 5, "yp", 1)
    hops["d", 0].wait_recv()
    combine(DENSE, d_block(2, 0), 1, (1,))
    send(DENSE, 3, 1, 4, "zm", 0)
    send(DENSE, 4, 1, 4, "zp", 1)
    combine(EXPERT, e_block(-1, 1), 2, (), 1)
    combine(EXPERT, e_block(1, 1), 3, (), 0)
    hops["e", 0].wait_recv()
    combine_half(combine, EXPERT, e_block(-1, 1), 2, 4, 0)
    send(EXPERT, 4, 2, 6, "ym")
    hops["e", 1].wait_recv()
    combine_half(combine, EXPERT, e_block(1, 1), 3, 4, 1)
    send(EXPERT, 5, 3, 7, "yp")
    hops["d", 0].wait_send()
    combine(DENSE, d_block(-1, 0), 0, (), 1)
    hops["d", 3].wait_recv()
    combine_half(combine, DENSE, d_block(-1, 0), 0, 4, 0)
    send(DENSE, 5, 0, 7, "zm")
    hops["d", 3].wait_send()
    hops["d", 4].wait_send()
    combine(DENSE, d_block(1, 0), 1, (), 0)
    hops["d", 4].wait_recv()
    combine_half(combine, DENSE, d_block(1, 0), 1, 4, 1)
    send(DENSE, 6, 1, 8, "zp")
    hops["e", 0].wait_send()
    hops["e", 1].wait_send()
    combine(EXPERT, e_block(-1, 0), 0, (), 1)
    hops["e", 2].wait_recv()
    combine_half(combine, EXPERT, e_block(-1, 0), 0, 5, 0)
    send(EXPERT, 6, 0, 8, "ym")
    hops["e", 2].wait_send()
    hops["e", 3].wait_send()
    combine(EXPERT, e_block(1, 0), 1, (), 0)
    hops["e", 3].wait_recv()
    combine_half(combine, EXPERT, e_block(1, 0), 1, 5, 1)
    send(EXPERT, 7, 1, 9, "yp")
    hops["d", 1].wait_recv()
    hops["d", 2].wait_recv()
    combine(DENSE, d_block(0, 1), 5, (5, 6))
    send(DENSE, 7, 5, 9, "zx")
    hops["e", 4].wait_recv()
    hops["e", 5].wait_recv()
    combine(EXPERT, e_block(0, 1), 6, (6, 7))
    send(EXPERT, 8, 6, 10, "yx")
    for index in (5, 6, 7):
        hops["d", index].wait_recv()
    combine(DENSE, ctx, 7, (7, 8, 9))

    for kind, start, width in (("wide", 0, WIDE), ("gu", WIDE, 2 * FF), ("small", WIDE + 2 * FF, SMALL)):
        step = min(width, 512)

        @pl.loop(0, width // step)
        def _(j, kind=kind, start=start, step=step):
            off = pl.multiple_of(j * step, 128)
            block = kinds[kind][7, :, pl.ds(off, step)]
            packs[:, pl.ds(start + off, step)] = jnp.dot(sel_t[...], block, preferred_element_type=jnp.float32).astype(jnp.bfloat16)

    last = []
    for k, ((dy, dh), device) in enumerate(zip(others, f_peers)):
        block = e_block(dy, dh)
        last.append(
            Hop(
                [rows_at(packs, block, 16), rows_at(b_sd.at[7], block, 32)],
                [in_pack.at[k], in_sd.at[k]],
                device, s_send.at[k], s_recv.at[k],
            ).start()
        )
    for index in (6, 7, 8):
        hops["e", index].wait_recv()
    combine(EXPERT, fsdp, 0, (8, 9, 10), None, dict(egu=out_egu, ed=out_ed))
    for hop in last:
        hop.wait_recv()

    @pl.loop(0, PACK // 128)
    def _(j):
        at = pl.ds(pl.multiple_of(j * 128, 128), 128)
        total = packs[pl.ds(pl.multiple_of(fsdp * 16, 16), 16), at].astype(jnp.float32)
        for k in range(7):
            total += in_pack[k, :, at].astype(jnp.float32)
        out_pack[:, at] = total

    total = b_sd[7, pl.ds(pl.multiple_of(fsdp * 32, 16), 32), :].astype(jnp.float32)
    for k in range(7):
        total += in_sd[k].astype(jnp.float32)
    out_sd[...] = total
    for hop in list(hops.values())[:]:
        pass
    for key in (("d", 1), ("d", 2), ("d", 5), ("d", 6), ("d", 7), ("e", 4), ("e", 5), ("e", 6), ("e", 7), ("e", 8)):
        hops[key].wait_send()
    for hop in last:
        hop.wait_send()
    for i in range(N_OPS):
        pltpu.make_async_remote_copy(
            lower[i], slot_of(i, 1), o_send.at[i], o_recv.at[i], device_id=near["core"], device_id_type=MESH
        ).wait_send()


def combine_half(combine, pieces, block, slot, half_slot, part):
    combine(pieces, block, slot, (half_slot,), part)


def weight_grads(lower, upper, small):
    rows = jnp.arange(128)
    cols = jnp.arange(96)
    sel_t = ((cols[None, :] // OWN == rows[:, None] // 16) & (cols[None, :] % OWN == rows[:, None] % 16)).astype(jnp.bfloat16)
    bf, f32 = jnp.bfloat16, jnp.float32
    held = [pltpu.VMEM((r, 2 * c), bf) for _, r, c in LEFT] + [pltpu.VMEM((2 * r, c), bf) for _, r, c in RIGHT]
    return pl.pallas_call(
        grads_kernel,
        out_shape=[
            jax.ShapeDtypeStruct((16, PACK), f32),
            jax.ShapeDtypeStruct((32, D), f32),
            jax.ShapeDtypeStruct((96, 2 * FF), f32),
            jax.ShapeDtypeStruct((256, D), f32),
        ],
        in_specs=[ANY] * (2 * N_OPS) + [VMEM, VMEM],
        out_specs=[VMEM] * 4,
        scratch_shapes=held + [
            pltpu.VMEM((10, 96, WIDE), bf),
            pltpu.VMEM((10, 96, 2 * FF), bf),
            pltpu.VMEM((10, 96, SMALL), bf),
            pltpu.VMEM((10, 256, D), bf),
            pltpu.VMEM((11, 96, 2 * FF), bf),
            pltpu.VMEM((11, 256, D), bf),
            pltpu.VMEM((128, PACK), bf),
            pltpu.VMEM((7, 16, PACK), bf),
            pltpu.VMEM((7, 32, D), bf),
            DMA((N_OPS,)), DMA((N_OPS,)), DMA((N_OPS,)),
            DMA((8, 4)), DMA((8, 4)),
            DMA((9, 2)), DMA((9, 2)),
            DMA((7, 2)), DMA((7, 2)),
        ],
        compiler_params=pltpu.CompilerParams(collective_id=5, has_side_effects=True, vmem_limit_bytes=62 << 20),
        name="weight_grads",
    )(*lower, *upper, small, sel_t)


def rms_parts(values):
    scale = lax.rsqrt(jnp.mean(values * values, axis=-1, keepdims=True) + EPS)
    return scale, values * scale


def rms_back(grad, gain, scale, unit):
    inner = grad * gain
    grad_values = scale * (inner - unit * jnp.mean(inner * unit, axis=-1, keepdims=True))
    return grad_values, jnp.sum(grad * unit, axis=0)


def token_positions(group_row):
    labels = jnp.arange(CONT + 1, dtype=jnp.int32)
    member = (group_row[:, None] == labels[None, :]).astype(jnp.int32)
    run_sizes = jnp.sum(member, axis=0)
    run_starts = jnp.cumsum(run_sizes) - run_sizes
    first_index = jnp.sum(member * run_starts[None, :], axis=1)
    token_index = jnp.arange(group_row.shape[0], dtype=jnp.int32)
    return jnp.where(group_row == 0, token_index, run_sizes[0] + token_index - first_index)


def rotation_tables(positions):
    half = HEAD_DIM // 2
    frequency = jnp.exp(-math.log(10000.0) * jnp.arange(half, dtype=jnp.float32) / half)
    angles = positions.astype(jnp.float32)[:, None] * frequency[None, :]
    cosine, sine = jnp.cos(angles), jnp.sin(angles)
    cosine = jnp.tile(jnp.concatenate([cosine, cosine], axis=1), (1, HEADS))
    sine = jnp.tile(jnp.concatenate([-sine, sine], axis=1), (1, HEADS))
    return cosine, sine


def rotate(values, cosine, sine):
    half = HEAD_DIM // 2
    ahead = jnp.concatenate([values[:, half:], values[:, :half]], axis=1)
    behind = jnp.concatenate([values[:, -half:], values[:, :-half]], axis=1)
    lower = lax.broadcasted_iota(jnp.int32, values.shape, 1) % HEAD_DIM < half
    return values * cosine + jnp.where(lower, ahead, behind) * sine


def slot_tables(route, rank):
    pairs = ROWS * TOP
    expert = route.reshape(-1)
    key = rank.reshape(-1) * pairs + jnp.arange(pairs, dtype=jnp.int32)
    earlier = (expert[None, :] == expert[:, None]) & (key[None, :] < key[:, None])
    slot = jnp.sum(earlier.astype(jnp.int32), axis=1)
    place = jnp.where(slot < CAP, expert * PAD_CAP + slot, -1).reshape(ROWS, TOP)
    every = jnp.arange(EXPERTS * PAD_CAP, dtype=jnp.int32)
    return [(place[:, c : c + 1] == every[None, :]) for c in range(TOP)]


def heads_out(values, count):
    return [values[:, 192 * g : 192 * g + 192] for g in range(count)]


def dot(left, right):
    return jnp.dot(left, right, preferred_element_type=jnp.float32)


def dot_t(left, right):
    return lax.dot_general(left, right, (((1,), (1,)), ((), ())), preferred_element_type=jnp.float32)


def t_dot(left, right, precision=None):
    return lax.dot_general(left, right, (((0,), (0,)), ((), ())), precision=precision, preferred_element_type=jnp.float32)


def low(values):
    return values.astype(jnp.bfloat16)


def silu_parts(joined):
    gate, up = joined[:, :FF], joined[:, FF:]
    return gate, up, jax.nn.sigmoid(gate)


def swiglu(joined):
    gate, up, sig = silu_parts(joined)
    return gate * sig * up


def swiglu_back(joined, grad):
    gate, up, sig = silu_parts(joined)
    return jnp.concatenate([grad * up * sig * (1.0 + gate * (1.0 - sig)), grad * gate * sig], axis=1)


def layer_forward(state, weights, geometry, route, chosen):
    w_wide, w_gu, w_small, w_sd, w_egu, w_ed = weights
    cosine, sine, qidx, qlab, klab = geometry
    gains = w_small[:, :2].astype(jnp.float32)
    router = w_small[:, 2 : 2 + EXPERTS]
    scale_attn, unit_attn = rms_parts(state)
    normed_attn = low(unit_attn * gains[:, 0])
    joined = dot(normed_attn, w_wide[:, : 3 * D])
    queries = low(rotate(joined[:, :D], cosine, sine))
    keys = low(rotate(joined[:, D : 2 * D], cosine, sine))
    values = low(joined[:, 2 * D :])
    kv = jnp.stack([jnp.concatenate([k, v], axis=1) for k, v in zip(heads_out(keys, 4), heads_out(values, 4))])
    kv_all, q_all = exchange("exchange_qkv", 1, kv, jnp.stack(heads_out(queries, 4)))
    kv_all, q_all = kv_all.reshape(SEQ, 384), q_all.reshape(512, 192)
    mixed_heads, lse = attend(q_all, kv_all, qidx, qlab, klab)
    (back,) = exchange("exchange_heads", 2, None, mixed_heads.reshape(4, ROWS, 192))
    attended = jnp.concatenate([back[g] for g in range(4)], axis=1)
    residual = state + dot(attended, w_wide[:, 3 * D :])
    scale_ffn, unit_ffn = rms_parts(residual)
    normed_ffn = low(unit_ffn * gains[:, 1])
    logits = dot(normed_ffn, router)
    labels = jnp.arange(EXPERTS, dtype=jnp.int32)
    picks = [(route[:, c : c + 1] == labels[None, :]) for c in range(TOP)]
    pair_logits = jnp.concatenate([jnp.sum(jnp.where(p, logits, 0.0), axis=1, keepdims=True) for p in picks], axis=1)
    gates = jax.nn.softmax(pair_logits, axis=-1)
    taken = low(chosen[0] | chosen[1])
    sent = low(t_dot(taken, normed_ffn))
    (received,) = exchange("exchange_slots", 4, sent.reshape(EXPERTS, PAD_CAP, D))
    shared_joined = dot(normed_ffn, w_gu)
    shared_hidden = low(swiglu(shared_joined))
    shared_out = dot(shared_hidden, w_sd)
    received = received.reshape(SLOTS, D)
    expert_joined = dot(received, w_egu)
    expert_hidden = low(swiglu(expert_joined))
    result = low(dot(expert_hidden, w_ed))
    (returned,) = exchange("exchange_slots", 4, result.reshape(EXPERTS, PAD_CAP, D))
    returned = returned.reshape(SLOTS, D)
    weights_of = jnp.where(chosen[0], gates[:, 0:1], 0.0) + jnp.where(chosen[1], gates[:, 1:2], 0.0)
    mixed = jnp.dot(weights_of, returned.astype(jnp.float32), precision=HIGH)
    output = residual + shared_out + mixed
    kept = dict(
        scale_attn=scale_attn, unit_attn=unit_attn, normed_attn=normed_attn, q_all=q_all, kv_all=kv_all, lse=lse,
        attended=attended, scale_ffn=scale_ffn, unit_ffn=unit_ffn, normed_ffn=normed_ffn, gates=gates, taken=taken,
        shared_joined=shared_joined, shared_hidden=shared_hidden, received=received, expert_joined=expert_joined,
        expert_hidden=expert_hidden, returned=returned, picks=picks, weights_of=weights_of,
    )
    return output, kept


def layer_backward(grad_output, kept, weights, geometry, chosen):
    w_wide, w_gu, w_small, w_sd, w_egu, w_ed = weights
    cosine, sine, qidx, qlab, klab = geometry
    gains = w_small[:, :2].astype(jnp.float32)
    router = w_small[:, 2 : 2 + EXPERTS]
    grad_rounded = low(grad_output)
    slot_grads = low(t_dot(kept["weights_of"], grad_output, HIGH))
    (grad_result,) = exchange("exchange_slots", 4, slot_grads.reshape(EXPERTS, PAD_CAP, D))
    grad_result = grad_result.reshape(SLOTS, D)
    grad_expert_joined = low(swiglu_back(kept["expert_joined"], dot_t(grad_result, w_ed)))
    grad_sent = low(dot_t(grad_expert_joined, w_egu))
    (grad_slots,) = exchange("exchange_slots", 4, grad_sent.reshape(EXPERTS, PAD_CAP, D))
    grad_shared_joined = low(swiglu_back(kept["shared_joined"], dot_t(grad_rounded, w_sd)))
    grad_normed = dot_t(grad_shared_joined, w_gu)
    grad_normed = grad_normed + dot(kept["taken"], grad_slots.reshape(SLOTS, D))
    products = dot_t(grad_rounded, kept["returned"])
    grad_gates = jnp.concatenate(
        [jnp.sum(jnp.where(c, products, 0.0), axis=1, keepdims=True) for c in chosen], axis=1
    )
    gates = kept["gates"]
    grad_chosen = gates * (grad_gates - jnp.sum(gates * grad_gates, axis=1, keepdims=True))
    grad_logits = sum(jnp.where(p, grad_chosen[:, c : c + 1], 0.0) for c, p in enumerate(kept["picks"]))
    grad_router = t_dot(kept["normed_ffn"].astype(jnp.float32), grad_logits, HIGH)
    grad_normed = grad_normed + lax.dot_general(
        grad_logits, router.astype(jnp.float32), (((1,), (1,)), ((), ())), precision=HIGH
    )
    grad_residual, grad_gain_ffn = rms_back(grad_normed, gains[:, 1], kept["scale_ffn"], kept["unit_ffn"])
    grad_residual = grad_output + grad_residual
    grad_projected = low(grad_residual)
    grad_attended = low(dot_t(grad_projected, w_wide[:, 3 * D :]))
    (grad_heads,) = exchange("exchange_heads", 2, None, jnp.stack(heads_out(grad_attended, 4)))
    dq, dkv = attend_back(
        kept["q_all"], kept["kv_all"], grad_heads.reshape(512, 192), kept["lse"], qidx, qlab, klab
    )
    dkv_all, dq_all = exchange("exchange_grads", 3, dkv.reshape(8, ROWS, 384), dq.reshape(4, ROWS, 192))
    dkv_all = dkv_all.astype(jnp.float32)
    dkv_all = dkv_all[:4] + dkv_all[4:]
    grad_queries = jnp.concatenate([dq_all[g] for g in range(4)], axis=1).astype(jnp.float32)
    grad_keys = jnp.concatenate([dkv_all[g, :, :192] for g in range(4)], axis=1)
    grad_values = jnp.concatenate([dkv_all[g, :, 192:] for g in range(4)], axis=1)
    grad_joined = low(
        jnp.concatenate([rotate(grad_queries, cosine, -sine), rotate(grad_keys, cosine, -sine), grad_values], axis=1)
    )
    grad_normed_attn = dot_t(grad_joined, w_wide[:, : 3 * D])
    grad_state, grad_gain_attn = rms_back(grad_normed_attn, gains[:, 0], kept["scale_attn"], kept["unit_attn"])
    grad_input = grad_residual + grad_state
    operands = [
        kept["normed_attn"].T, kept["attended"].T, kept["normed_ffn"].T, kept["shared_hidden"].T,
        kept["received"].T, kept["expert_hidden"].T,
        grad_joined, grad_projected, grad_shared_joined, grad_rounded, grad_expert_joined, grad_result,
    ]
    small = jnp.concatenate(
        [grad_gain_attn[:, None], grad_gain_ffn[:, None], grad_router, jnp.zeros((D, SMALL - 2 - EXPERTS), jnp.float32)],
        axis=1,
    )
    return grad_input, operands, small


def swap_cores(value):
    return lax.ppermute(value, "section", [(0, 1), (1, 0)])


def on_device(
    x_in, cotangent, group_ids, routes, priority,
    gains, w_qkv, w_out, router, shared_gate_up, shared_down, expert_gate_up, expert_down,
):
    section = lax.axis_index("section")
    ctx = lax.axis_index("ctx")
    first = section == 0

    pack = jnp.concatenate(
        [w_qkv[0], w_out[0], shared_gate_up[0], gains[0], router[0], jnp.zeros((OWN, SMALL - 2 - EXPERTS), jnp.bfloat16)],
        axis=1,
    )
    gathered = gather_weights(
        jnp.pad(pack, ((0, 16 - OWN), (0, 0))), shared_down[0], expert_gate_up[0, 0], expert_down[0, 0]
    )
    weights = [tuple(w[layer] for w in gathered) for layer in range(2)]

    def mine(value):
        return jnp.where(first, value[0], value[1])

    def other(value):
        return jnp.where(first, value[1], value[0])

    picked = jnp.stack([routes[0, :, 0], priority[0, :, 0]], axis=1)
    passed = swap_cores(other(picked))
    own = mine(picked)
    plans = [jnp.where(first, own, passed), jnp.where(first, passed, own)]
    chosen = [slot_tables(plan[0], plan[1]) for plan in plans]

    group_row = mine(group_ids[:, 0])
    positions = token_positions(group_row)
    cosine, sine = rotation_tables(lax.dynamic_slice_in_dim(positions, ctx * ROWS, ROWS))
    half_start = ctx // 4 * 512
    qlab = lax.dynamic_slice_in_dim(group_row, half_start, 512)[:, None]
    qidx = (half_start + jnp.arange(512, dtype=jnp.int32))[:, None]
    geometry = (cosine, sine, qidx, qlab, group_row[None, :])

    state = mine(x_in[:, 0]).astype(jnp.float32)
    output, kept_lower = layer_forward(state, weights[0], geometry, plans[0][0], chosen[0])
    hidden = low(output)
    output, kept_upper = layer_forward(hidden.astype(jnp.float32), weights[1], geometry, plans[1][0], chosen[1])
    final = low(output)

    grad_final = mine(cotangent[:, 0]).astype(jnp.float32)
    hidden_grad, operands_upper, small_upper = layer_backward(grad_final, kept_upper, weights[1], geometry, chosen[1])
    input_grad, operands_lower, small_lower = layer_backward(
        low(hidden_grad).astype(jnp.float32), kept_lower, weights[0], geometry, chosen[0]
    )
    small = jnp.where(first, small_lower, small_upper) + swap_cores(jnp.where(first, small_upper, small_lower))
    pack_grad, sd_grad, egu_grad, ed_grad = weight_grads(operands_lower, operands_upper, small)

    def per_layer(lower, upper):
        kept_here = jnp.where(first, lower, upper)
        arrived = swap_cores(jnp.where(first, upper, lower))
        both = jnp.stack([jnp.where(first, kept_here, arrived), jnp.where(first, arrived, kept_here)])
        return both.reshape(1, 2, 1, ROWS, D)

    pack_grad = pack_grad[None, :OWN]
    tail = WIDE + 2 * FF
    return (
        per_layer(hidden, final),
        per_layer(input_grad, hidden_grad),
        pack_grad[:, :, tail : tail + 2],
        pack_grad[:, :, : 3 * D],
        pack_grad[:, :, 3 * D : WIDE],
        pack_grad[:, :, tail + 2 : tail + 2 + EXPERTS],
        pack_grad[:, :, WIDE:tail],
        sd_grad[None],
        egu_grad[None, None],
        ed_grad[None, None],
    )


def solution(mesh):
    dense = P("section", ("ctx", "fsdp"), None)
    expert = P("section", "ctx", "fsdp", None)
    tokens = P("section", None, "fsdp", "ctx", None)
    rows = P(None, "fsdp", "ctx", None)
    return jax.shard_map(
        on_device,
        mesh=mesh,
        in_specs=(rows, rows, P(None, "fsdp", None), tokens, tokens) + (dense,) * 6 + (expert,) * 2,
        out_specs=(tokens, tokens) + (dense,) * 6 + (expert,) * 2,
        check_vma=False,
    )
```

time: 3980 us -> 821 us (0.21)
  waiting for transfers between devices: 2000 us -> 0.01 us
  blocking collectives: 762 us -> 0 us
  Pallas kernels: 0 us -> 565 us
  local copies, waits for them, and re-layouts: 626 us -> 75.6 us
  matrix products: 360 us -> 116 us
  other arithmetic: 110 us -> 49.1 us
  starting transfers between devices: 60.1 us -> 0.53 us
    all_gather x12 -> x0, waiting for transfers between devices: 1290 us -> none  [the longest x1 318 us: on_device(): lax.all_gather(shared_down, ('ctx', 'fsdp'), axis=1, tiled=True)]
    pallas_call x0 -> x22, Pallas kernels: none -> 565 us  [the longest x1 216 us: weight_grads(): pl.pallas_call(grads_kernel, out_shape=[jax.ShapeDtypeStruct((16, PACK),...]
    reduce_scatter x9 -> x0, waiting for transfers between devices: 564 us -> none  [the longest x1 365 us: on_device(): lax.psum_scatter(dense_sum[5][None], ('ctx', 'fsdp'), scatter_dimension=1...]
    all_gather x2 -> x0, blocking collectives: 409 us -> none  [the longest x1 226 us: on_device(): lax.all_gather(router, ('ctx', 'fsdp'), axis=1, tiled=True)]
    dynamic_update_slice x24 -> x0, local copies, waits for them, and re-layouts: 373 us -> none  [attend_backward(): lax.scan(grad_step, jnp.zeros((row_count, HEADS, HEAD_DIM), jnp.float32),...]
    unnamed x1 -> x0, blocking collectives: 354 us -> none
    dot_general x126 -> x40, matrix products: 360 us -> 116 us  [the longest x14 58.1 us: dot_t(): lax.dot_general(left, right, (((1,), (1,)), ((), ())), preferred_element_...]
    unnamed x25 -> x0, waiting for transfers between devices: 105 us -> none
  transfers between devices with their start and end apart: 39 -> 4, of which waited for: 28 -> 0; matrix products, arithmetic and copies ran while one was open for 9% -> 10% of each run, Pallas kernels for 0% -> 50%
where the time goes in v1:
time: 821 us; the launch traced here: 810 us
  Pallas kernels  565 us (69%)
  matrix products  116 us (14%)
  local copies, waits for them, and re-layouts  75.6 us (9%)
  other arithmetic  49.1 us (6%)
    pallas_call x1, Pallas kernels, weight_grads(): pl.pallas_call(grads_kernel, out_shape=[jax.ShapeDtypeStruct((16, PACK),...  216 us
    pallas_call x16, Pallas kernels, exchange(): pl.pallas_call(functools.partial(exchange_kernel, 0 if eight is None else...  160 us
    pallas_call x1, Pallas kernels, gather_weights(): pl.pallas_call(gather_kernel, out_shape=[jax.ShapeDtypeStruct(s, bf) for...  156 us
    dot_general x14, matrix products, dot_t(): lax.dot_general(left, right, (((1,), (1,)), ((), ())), preferred_element_...  58.1 us
    dot_general x16, matrix products, dot(): return jnp.dot(left, right, preferred_element_type=jnp.float32)  43.7 us
    unnamed x396, local copies, waits for them, and re-layouts  26.6 us
    pallas_call x2, Pallas kernels, attend_back(): pl.pallas_call(attend_back_kernel, grid=(4,), out_shape=[jax.ShapeDtypeSt...  18.6 us
  transfers between devices with their start and end apart: 4, of which 0 were waited for; matrix products, arithmetic and copies ran while one was open for 10% of the time, Pallas kernels for 50%

profile of v1, /device:TPU:0, one launch (start us, length us, event | category | flops | bytes accessed | tf_op | source)
XLA Modules:
  0.0 809.8 jit_solution(2823400799472568227)
XLA Ops:
  8.6 156.3 %gather_weights.1 = (bf16[2,768,3072]{2,1,0:T(8,128)(2,1)}, bf16[2,768,4096]{2,1,0:T(8,128)(2,1)}, bf16[2,768,128]{2,1,0:T(8,128)(2,1)S(1)}, bf16[2,2048,768]{2,...) custom-call(bf16[16,7296]{1,0:T(8,128)(2,1)S(1)} %pad.4.pack, ...), custom_call_target="tpu_custom_call" | custom-call | tf_op jit(solution)/shard_map/gather_weights/pallas_call | solution.py:245
  165.0 6.9 slice_bitcast_fusion.1
  179.6 1.5 tile.20
  182.3 1.6 fusion.117
  190.3 17.6 %exchange_qkv.2 = (bf16[8,128,384]{2,1,0:T(8,128)(2,1)}, bf16[4,128,192]{2,1,0:T(8,128)(2,1)}) custom-call(bf16[4,128,384]{2,1,0:T(8,128)(2,1)} %pad_maximum_fusion.4.refs_0_, bf16[4,128,192]{2,1,0:T(8,128)(2,1)} %pad_maximum_fusion.8.refs_1_), custom_call_target="tpu_custom_call" | custom-call | tf_op jit(solution)/shard_map/exchange_qkv/pallas_call | solution.py:315
  210.0 6.8 attend.2
  217.5 7.1 exchange_heads.4
  226.0 1.7 multiply_reduce_fusion.5
  231.2 3.8 fusion.14
  238.1 1.7 copy.250.refs_2_
  245.4 10.4 %exchange_slots.8 = bf16[8,48,768]{2,1,0:T(8,128)(2,1)} custom-call(bf16[8,48,768]{2,1,0:T(8,128)(2,1)} %bitcast.404), custom_call_target="tpu_custom_call" | custom-call | tf_op jit(solution)/shard_map/exchange_slots/pallas_call | solution.py:315
  255.7 5.2 fusion.10
  260.9 6.8 fusion.56
  267.7 9.7 %exchange_slots.9 = bf16[8,48,768]{2,1,0:T(8,128)(2,1)} custom-call(bf16[8,48,768]{2,1,0:T(8,128)(2,1)} %bitcast.411), custom_call_target="tpu_custom_call" | custom-call | tf_op jit(solution)/shard_map/exchange_slots/pallas_call | solution.py:315
  278.1 1.8 fusion.139
  280.1 3.4 fusion.104
  287.5 12.1 %exchange_qkv.3 = (bf16[8,128,384]{2,1,0:T(8,128)(2,1)}, bf16[4,128,192]{2,1,0:T(8,128)(2,1)}) custom-call(bf16[4,128,384]{2,1,0:T(8,128)(2,1)} %pad_maximum_fusion.5.refs_0_, bf16[4,128,192]{2,1,0:T(8,128)(2,1)} %pad_maximum_fusion.9.refs_1_), custom_call_target="tpu_custom_call" | custom-call | tf_op jit(solution)/shard_map/exchange_qkv/pallas_call | solution.py:315
  301.8 6.8 attend.3
  309.2 7.1 exchange_heads.5
  317.8 1.7 multiply_reduce_fusion.4
  319.9 5.2 fusion.6
  326.3 9.7 %exchange_slots.10 = bf16[8,48,768]{2,1,0:T(8,128)(2,1)} custom-call(bf16[8,48,768]{2,1,0:T(8,128)(2,1)} %bitcast.405), custom_call_target="tpu_custom_call" | custom-call | tf_op jit(solution)/shard_map/exchange_slots/pallas_call | solution.py:315
  336.1 5.0 fusion.2
  341.1 6.8 fusion.59
  347.9 9.7 %exchange_slots.11 = bf16[8,48,768]{2,1,0:T(8,128)(2,1)} custom-call(bf16[8,48,768]{2,1,0:T(8,128)(2,1)} %bitcast.412), custom_call_target="tpu_custom_call" | custom-call | tf_op jit(solution)/shard_map/exchange_slots/pallas_call | solution.py:315
  357.9 1.6 select_reduce_fusion.3
  359.9 2.3 fusion.137
  362.2 1.6 convolution_convert_fusion.3
  363.8 4.3 multiply_convert_fusion.9
  368.2 9.7 %exchange_slots.12 = bf16[8,48,768]{2,1,0:T(8,128)(2,1)} custom-call(bf16[8,48,768]{2,1,0:T(8,128)(2,1)} %bitcast.402), custom_call_target="tpu_custom_call" | custom-call | tf_op jit(solution)/shard_map/exchange_slots/pallas_call | solution.py:315
  377.9 6.0 multiply_convert_fusion.3
  383.9 7.6 fusion.65
  391.5 9.7 %exchange_slots.13 = bf16[8,48,768]{2,1,0:T(8,128)(2,1)} custom-call(bf16[8,48,768]{2,1,0:T(8,128)(2,1)} %bitcast.413), custom_call_target="tpu_custom_call" | custom-call | tf_op jit(solution)/shard_map/exchange_slots/pallas_call | solution.py:315
  401.3 5.4 fusion.4
  409.0 2.3 convolution_convert_fusion.5
  412.2 7.1 exchange_heads.6
  420.2 9.2 %attend_back.2 = (bf16[512,192]{1,0:T(8,128)(2,1)S(1)}, bf16[1024,384]{1,0:T(8,128)(2,1)S(1)}) custom-call(bf16[512,192]{1,0:T(8,128)(2,1)S(1)} %bitcast.372, bf16[1024,384]{1,0:T(8,128)(2,1)S(1)} %bitcast.366, bf16[512,192]{1,0:T(8,128)(2,1)S(1)} %bitcast.368, f32[512,128]{1,0:T(8,128)S(1)} %get-tuple-element.48.lse_ref, ...), custom_call_target="tpu_custom_call" | custom-call | tf_op jit(solution)/shard_map/attend_back/pallas_call | solution.py:400
  431.0 12.2 %exchange_grads.2 = (bf16[8,128,384]{2,1,0:T(8,128)(2,1)}, bf16[4,128,192]{2,1,0:T(8,128)(2,1)}) custom-call(bf16[8,128,384]{2,1,0:T(8,128)(2,1)} %bitcast.375, bf16[4,128,192]{2,1,0:T(8,128)(2,1)} %bitcast.380), custom_call_target="tpu_custom_call" | custom-call | tf_op jit(solution)/shard_map/exchange_grads/pallas_call | solution.py:315
  447.8 3.5 fusion.40
  453.9 3.3 multiply_convert_fusion.7
  457.2 1.6 convolution_convert_fusion.2
  459.2 9.9 %exchange_slots.14 = bf16[8,48,768]{2,1,0:T(8,128)(2,1)} custom-call(bf16[8,48,768]{2,1,0:T(8,128)(2,1)} %bitcast.403), custom_call_target="tpu_custom_call" | custom-call | tf_op jit(solution)/shard_map/exchange_slots/pallas_call | solution.py:315
  469.1 6.0 multiply_convert_fusion.1
  475.1 7.6 fusion.62
  482.7 9.7 %exchange_slots.15 = bf16[8,48,768]{2,1,0:T(8,128)(2,1)} custom-call(bf16[8,48,768]{2,1,0:T(8,128)(2,1)} %bitcast.410), custom_call_target="tpu_custom_call" | custom-call | tf_op jit(solution)/shard_map/exchange_slots/pallas_call | solution.py:315
  492.6 5.1 fusion.12
  500.8 1.8 convolution_convert_fusion.4
  503.5 7.1 exchange_heads.7
  511.6 9.4 %attend_back.3 = (bf16[512,192]{1,0:T(8,128)(2,1)S(1)}, bf16[1024,384]{1,0:T(8,128)(2,1)S(1)}) custom-call(bf16[512,192]{1,0:T(8,128)(2,1)S(1)} %bitcast.370, bf16[1024,384]{1,0:T(8,128)(2,1)S(1)} %bitcast.364, bf16[512,192]{1,0:T(8,128)(2,1)S(1)} %bitcast.367, f32[512,128]{1,0:T(8,128)S(1)} %get-tuple-element.53.lse_ref, ...), custom_call_target="tpu_custom_call" | custom-call | tf_op jit(solution)/shard_map/attend_back/pallas_call | solution.py:400
  522.5 11.3 %exchange_grads.3 = (bf16[8,128,384]{2,1,0:T(8,128)(2,1)}, bf16[4,128,192]{2,1,0:T(8,128)(2,1)}) custom-call(bf16[8,128,384]{2,1,0:T(8,128)(2,1)} %bitcast.374, bf16[4,128,192]{2,1,0:T(8,128)(2,1)} %bitcast.379), custom_call_target="tpu_custom_call" | custom-call | tf_op jit(solution)/shard_map/exchange_grads/pallas_call | solution.py:315
  535.2 3.9 fusion.285
  540.3 2.0 pad_maximum_fusion.1.refs_10_
  543.1 2.1 fusion.283
  546.4 2.0 pad_maximum_fusion.refs_22_
  556.8 3.3 fusion.44
  565.8 2.1 copy.241
  568.0 2.2 copy.242
  570.2 1.8 copy.249.refs_0_
  572.0 1.8 copy.252.refs_5_
  574.6 1.8 copy.254.refs_14_
  576.4 2.1 copy.255.refs_15_
  578.4 1.6 copy.256.refs_17_
  581.8 1.9 select_add_fusion.refs_24_
  583.7 216.2 %weight_grads.1 = (f32[16,7296]{1,0:T(8,128)}, f32[32,768]{1,0:T(8,128)}, f32[96,4096]{1,0:T(8,128)}, f32[256,768]{1,0:T(8,128)}) custom-call(bf16[768,128]{1,0:T(8,128)(2,1)} %copy.249.refs_0_, bf16[768,128]{1,0:T(8,128)(2,1)} %fusion.183.refs_1_, bf16[768,128]{1,0:T(8,128)(2,1)} %copy.250.refs_2_, bf16[2048,128]{1,0:T(8,128)(2,1)} %copy.251.refs_3_, ...), custom_call_target="tpu_custom_call" | custom-call | tf_op jit(solution)/shard_map/weight_grads/pallas_call | solution.py:635
  (588 shorter events, 99.7 us)
Async XLA Ops:
  2.4 239.2 %collective-permute-start = (s32[2,128,2]{2,1,0:T(8,128)}, s32[2,128,2]{2,1,0:T(8,128)}, u32[]{:S(2)}, u32[]{:S(2)}) collective-permute-start(s32[2,128,2]{2,1,0:T(8,128)} %select_bitcast_fusion.5), channel_id=1, source_target_pairs={{0,64},{64,0},{1,65},{65,1},{2,66},{66,2},{3,67},{67,3},{4,68},{68... | collective-permute-start | bytes 6152 | tf_op jit(solution)/shard_map/ppermute | solution.py:858
  165.0 6.9 copy-start.91
  172.0 54.0 %copy-start.47 = (bf16[1,1,128,768]{3,2,1,0:T(8,128)(2,1)}, bf16[1,1,128,768]{3,2,1,0:T(8,128)(2,1)S(1)}, u32[]{:S(2)}) copy-start(bf16[1,1,128,768]{3,2,1,0:T(8,128)(2,1)S(1)} %get-tuple-element.154) | copy-start | bytes 589828
  172.9 104.8 %copy-start.49 = (bf16[768,128]{1,0:T(8,128)(2,1)}, bf16[768,128]{1,0:T(8,128)(2,1)S(1)}, u32[]{:S(2)}) copy-start(bf16[768,128]{1,0:T(8,128)(2,1)S(1)} %get-tuple-element.233) | copy-start | bytes 589828
  176.6 7.3 copy-start.108
  209.9 18.7 %copy-start.172 = (s32[128]{0:T(128)S(1)}, s32[128]{0:T(128)}, u32[]{:S(2)}) copy-start(s32[128]{0:T(128)} %copy-done.171) | copy-start | bytes 1540
  210.0 18.7 %copy-start.174 = (s32[128]{0:T(128)S(1)}, s32[128]{0:T(128)}, u32[]{:S(2)}) copy-start(s32[128]{0:T(128)} %copy-done.173) | copy-start | bytes 1540
  210.0 18.7 %copy-start.176 = (s32[96]{0:T(128)S(1)}, s32[96]{0:T(128)}, u32[]{:S(2)}) copy-start(s32[96]{0:T(128)} %copy-done.175) | copy-start | bytes 1156
  210.0 18.7 %copy-start.178 = (s32[96]{0:T(128)S(1)}, s32[96]{0:T(128)}, u32[]{:S(2)}) copy-start(s32[96]{0:T(128)} %copy-done.177) | copy-start | bytes 1156
  210.0 19.5 %copy-start.51 = (bf16[768,128]{1,0:T(8,128)(2,1)S(1)}, bf16[768,128]{1,0:T(8,128)(2,1)}, u32[]{:S(2)}) copy-start(bf16[768,128]{1,0:T(8,128)(2,1)} %get-tuple-element.232) | copy-start | bytes 589828
  217.5 13.0 %copy-start.35 = (bf16[2,1,128,768]{3,2,1,0:T(8,128)(2,1)S(1)}, bf16[2,1,128,768]{3,2,1,0:T(8,128)(2,1)}, u32[]{:S(2)}) copy-start(bf16[2,1,128,768]{3,2,1,0:T(8,128)(2,1)} %param.14) | copy-start | bytes 1179652
  227.9 49.8 %copy-start.31 = (bf16[128,768]{1,0:T(8,128)(2,1)}, bf16[128,768]{1,0:T(8,128)(2,1)S(1)}, u32[]{:S(2)}) copy-start(bf16[128,768]{1,0:T(8,128)(2,1)S(1)} %multiply_convert_fusion.13) | copy-start | bytes 589828
  244.1 34.0 %copy-start.125 = (s32[128]{0:T(128)}, s32[128]{0:T(128)S(1)}, u32[]{:S(2)}) copy-start(s32[128]{0:T(128)S(1)} %get-tuple-element.134) | copy-start | bytes 1540
  244.1 34.0 %copy-start.127 = (s32[128]{0:T(128)}, s32[128]{0:T(128)S(1)}, u32[]{:S(2)}) copy-start(s32[128]{0:T(128)S(1)} %get-tuple-element.135) | copy-start | bytes 1540
  260.9 6.8 copy-start.26
  277.7 5.9 slice-start
  283.5 169.3 %copy-start.44 = (bf16[128,768]{1,0:T(8,128)(2,1)}, bf16[128,768]{1,0:T(8,128)(2,1)S(1)}, u32[]{:S(2)}) copy-start(bf16[128,768]{1,0:T(8,128)(2,1)S(1)} %get-tuple-element.300) | copy-start | bytes 589828
  317.4 7.7 copy-start.94
  317.5 7.6 copy-start.96
  319.5 88.8 %copy-start.133 = (f32[128]{0:T(128)}, f32[128]{0:T(128)S(1)}, u32[]{:S(2)}) copy-start(f32[128]{0:T(128)S(1)} %add_rsqrt_fusion) | copy-start | bytes 1540
  319.8 39.6 %copy-start.33 = (bf16[128,768]{1,0:T(8,128)(2,1)}, bf16[128,768]{1,0:T(8,128)(2,1)S(1)}, u32[]{:S(2)}) copy-start(bf16[128,768]{1,0:T(8,128)(2,1)S(1)} %multiply_convert_fusion.12) | copy-start | bytes 589828
  341.1 6.8 copy-start.27
  341.1 16.8 %copy-start.59 = (bf16[128,768]{1,0:T(8,128)(2,1)S(1)}, bf16[128,768]{1,0:T(8,128)(2,1)}, u32[]{:S(2)}) copy-start(bf16[128,768]{1,0:T(8,128)(2,1)} %select_bitcast_fusion.2.refs_21_) | copy-start | bytes 589828
  357.6 6.2 copy-start.58
  357.8 49.2 %copy-start.145 = (s32[128]{0:T(128)}, s32[128]{0:T(128)S(1)}, u32[]{:S(2)}) copy-start(s32[128]{0:T(128)S(1)} %get-tuple-element.128) | copy-start | bytes 1540
  357.8 49.2 %copy-start.147 = (s32[128]{0:T(128)}, s32[128]{0:T(128)S(1)}, u32[]{:S(2)}) copy-start(s32[128]{0:T(128)S(1)} %get-tuple-element.129) | copy-start | bytes 1540
  383.8 7.6 copy-start.61
  383.9 7.6 copy-start.63
  401.2 5.9 copy-start.159
  401.2 5.9 copy-start.161
  401.3 7.0 copy-start.36
  407.0 12.2 %copy-start.3 = (bf16[8,128,384]{2,1,0:T(8,128)(2,1)S(1)}, bf16[8,128,384]{2,1,0:T(8,128)(2,1)}, u32[]{:S(2)}) copy-start(bf16[8,128,384]{2,1,0:T(8,128)(2,1)} %get-tuple-element.46) | copy-start | bytes 2359300
  407.1 12.2 %copy-start.9 = (bf16[4,128,192]{2,1,0:T(8,128)(2,1)S(1)}, bf16[4,128,192]{2,1,0:T(8,128)(2,1)}, u32[]{:S(2)}) copy-start(bf16[4,128,192]{2,1,0:T(8,128)(2,1)} %get-tuple-element.45) | copy-start | bytes 589828
  408.3 21.2 %copy-start.169 = (f32[128]{0:T(128)}, f32[128]{0:T(128)S(1)}, u32[]{:S(2)}) copy-start(f32[128]{0:T(128)S(1)} %broadcast_multiply_fusion.3) | copy-start | bytes 1540
  447.7 6.1 copy-start.53
  447.8 6.1 copy-start.25
  453.8 45.4 %copy-start.29 = (bf16[128,768]{1,0:T(8,128)(2,1)}, bf16[128,768]{1,0:T(8,128)(2,1)S(1)}, u32[]{:S(2)}) copy-start(bf16[128,768]{1,0:T(8,128)(2,1)S(1)} %get-tuple-element.147.refs_9_) | copy-start | bytes 589828
  457.2 35.3 %copy-start.87 = (bf16[128,2048]{1,0:T(8,128)(2,1)}, bf16[128,2048]{1,0:T(8,128)(2,1)S(1)}, u32[]{:S(2)}) copy-start(bf16[128,2048]{1,0:T(8,128)(2,1)S(1)} %get-tuple-element.161) | copy-start | bytes 1572868
  457.2 35.3 %copy-start.89 = (bf16[128,2048]{1,0:T(8,128)(2,1)}, bf16[128,2048]{1,0:T(8,128)(2,1)S(1)}, u32[]{:S(2)}) copy-start(bf16[128,2048]{1,0:T(8,128)(2,1)S(1)} %get-tuple-element.162) | copy-start | bytes 1572868
  475.0 7.6 copy-start.65
  475.0 7.6 copy-start.67
  475.1 17.3 %copy-start.130 = (f32[128]{0:T(128)S(1)}, f32[128]{0:T(128)}, u32[]{:S(2)}) copy-start(f32[128]{0:T(128)} %copy-done.129) | copy-start | bytes 1540
  475.1 17.3 %copy-start.132 = (f32[128]{0:T(128)S(1)}, f32[128]{0:T(128)}, u32[]{:S(2)}) copy-start(f32[128]{0:T(128)} %copy-done.131) | copy-start | bytes 1540
  475.1 17.3 %copy-start.150 = (f32[128]{0:T(128)S(1)}, f32[128]{0:T(128)}, u32[]{:S(2)}) copy-start(f32[128]{0:T(128)} %copy-done.149) | copy-start | bytes 1540
  475.1 17.3 %copy-start.152 = (f32[128]{0:T(128)S(1)}, f32[128]{0:T(128)}, u32[]{:S(2)}) copy-start(f32[128]{0:T(128)} %copy-done.151) | copy-start | bytes 1540
  498.0 12.6 %copy-start.1 = (bf16[8,128,384]{2,1,0:T(8,128)(2,1)S(1)}, bf16[8,128,384]{2,1,0:T(8,128)(2,1)}, u32[]{:S(2)}) copy-start(bf16[8,128,384]{2,1,0:T(8,128)(2,1)} %get-tuple-element.39) | copy-start | bytes 2359300
  498.0 12.6 %copy-start.7 = (bf16[4,128,192]{2,1,0:T(8,128)(2,1)S(1)}, bf16[4,128,192]{2,1,0:T(8,128)(2,1)}, u32[]{:S(2)}) copy-start(bf16[4,128,192]{2,1,0:T(8,128)(2,1)} %get-tuple-element.38) | copy-start | bytes 589828
  499.2 21.7 %copy-start.179 = (f32[128]{0:T(128)}, f32[128]{0:T(128)S(1)}, u32[]{:S(2)}) copy-start(f32[128]{0:T(128)S(1)} %broadcast_multiply_fusion.1) | copy-start | bytes 1540
  535.2 7.9 slice-start.2
  540.3 10.4 %slice-start.4 = ((s8[6291456]{0:T(1024)(128)(4,1)}), s8[4194304]{0:T(1024)(128)(4,1)S(1)}, s32[]{:S(2)}) async-start(s8[6291456]{0:T(1024)(128)(4,1)} %bitcast.464), calls=%async_computation.4 | async-start | bytes 8388608
  543.1 7.6 slice-start.5
  552.1 27.9 %collective-permute-start.1 = (bf16[128,768]{1,0:T(8,128)(2,1)}, bf16[128,768]{1,0:T(8,128)(2,1)}, u32[]{:S(2)}, u32[]{:S(2)}) collective-permute-start(bf16[128,768]{1,0:T(8,128)(2,1)} %get-tuple-element.305), channel_id=1, source_target_pairs={{0,64},{64,0},{1,65},{65,1},{2,66},{66,2},{3,67},{67,3},{4,68},{68... | collective-permute-start | bytes 589832 | tf_op jit(solution)/shard_map/ppermute | solution.py:858
  563.4 18.4 %collective-permute-start.3 = (f32[768,128]{1,0:T(8,128)}, f32[768,128]{1,0:T(8,128)}, u32[]{:S(2)}, u32[]{:S(2)}) collective-permute-start(f32[768,128]{1,0:T(8,128)} %get-tuple-element.140), channel_id=1, source_target_pairs={{0,64},{64,0},{1,65},{65,1},{2,66},{66,2},{3,67},{67,3},{4,68},{68... | collective-permute-start | bytes 1179656 | tf_op jit(solution)/shard_map/ppermute | solution.py:858
  565.1 8.6 %copy-start.81 = (bf16[768,128]{0,1:T(8,128)(2,1)S(1)}, bf16[768,128]{0,1:T(8,128)(2,1)}, u32[]{:S(2)}) copy-start(bf16[768,128]{0,1:T(8,128)(2,1)} %get-tuple-element.250) | copy-start | bytes 589828
  568.0 10.5 %copy-start.28 = (bf16[2048,384]{0,1:T(8,128)(2,1)S(1)}, bf16[2048,384]{0,1:T(8,128)(2,1)}, u32[]{:S(2)}) copy-start(bf16[2048,384]{0,1:T(8,128)(2,1)} %fusion.283) | copy-start | bytes 4718596
  570.2 234.6 %collective-permute-start.2 = (f32[128,768]{1,0:T(8,128)}, f32[128,768]{1,0:T(8,128)}, u32[]{:S(2)}, u32[]{:S(2)}) collective-permute-start(f32[128,768]{1,0:T(8,128)} %get-tuple-element.143), channel_id=1, source_target_pairs={{0,64},{64,0},{1,65},{65,1},{2,66},{66,2},{3,67},{67,3},{4,68},{68... | collective-permute-start | bytes 1179656 | tf_op jit(solution)/shard_map/ppermute | solution.py:858
  573.7 6.3 copy-start.46
  573.7 6.3 copy-start.93
  574.5 7.2 copy-start.72
  574.5 7.2 copy-start.73
  583.6 221.2 %copy-start.43 = (f32[128,768]{1,0:T(8,128)S(1)}, f32[128,768]{1,0:T(8,128)}, u32[]{:S(2)}) copy-start(f32[128,768]{1,0:T(8,128)} %get-tuple-element.148) | copy-start | bytes 1179652
  583.7 221.2 %copy-start.71 = (f32[128,768]{1,0:T(8,128)S(1)}, f32[128,768]{1,0:T(8,128)}, u32[]{:S(2)}) copy-start(f32[128,768]{1,0:T(8,128)} %get-tuple-element.144) | copy-start | bytes 1179652
  799.9 7.0 copy-start.112
  799.9 7.7 copy-start.60
  (129 other events, 413.6 us)

commit v2 on v1

--- a/solution.py
+++ b/solution.py
@@ -32,7 +32,6 @@
 SCALE = 1.0 / math.sqrt(HEAD_DIM)
 EPS = 1e-06
 NEG = -1e30
-HIGH = lax.Precision.HIGHEST
 
 
 def place_ids():
@@ -262,151 +261,6 @@
         compiler_params=pltpu.CompilerParams(collective_id=0, has_side_effects=True, vmem_limit_bytes=48 << 20),
         name="gather_weights",
     )(pack, sd, egu, ed, sel)
-
-
-def exchange_kernel(eight_from, with_eight, with_four, *refs):
-    count = int(with_eight) + int(with_four)
-    sources, targets = refs[:count], refs[count : 2 * count]
-    send8, recv8, send4, recv4, l_sem = refs[2 * count :]
-    section, a, z, y, h = place_ids()
-    fsdp = fsdp_of(y, h)
-    ctx = ctx_of(a, z)
-    offsets = [(0, 1), (0, 3), (0, 2)]
-    if with_eight:
-        offsets = [(1, 0), (1, 1), (1, 3), (1, 2)] + offsets
-    peers = [(ctx_of(a + da, z + dz), lax.rem(z + dz, 4)) for da, dz in offsets]
-    greet([(section, c, fsdp) for c, _ in peers])
-    copies = []
-    for k, ((da, dz), (c, zz)) in enumerate(zip(offsets, peers)):
-        device = (section, c, fsdp)
-        if with_eight:
-            block = c if eight_from == 8 else zz
-            copies.append(
-                pltpu.make_async_remote_copy(
-                    sources[0].at[block], targets[0].at[ctx], send8.at[k], recv8.at[k], device_id=device, device_id_type=MESH
-                )
-            )
-        if with_four and da == 0:
-            copies.append(
-                pltpu.make_async_remote_copy(
-                    sources[-1].at[zz], targets[-1].at[z], send4.at[k], recv4.at[k], device_id=device, device_id_type=MESH
-                )
-            )
-    for copy in copies:
-        copy.start()
-    stays = []
-    if with_eight:
-        stays.append(pltpu.make_async_copy(sources[0].at[ctx if eight_from == 8 else z], targets[0].at[ctx], l_sem.at[0]))
-    if with_four:
-        stays.append(pltpu.make_async_copy(sources[-1].at[z], targets[-1].at[z], l_sem.at[1]))
-    for copy in stays:
-        copy.start()
-    for copy in stays + copies:
-        copy.wait()
-
-
-def exchange(name, collective_id, eight=None, four=None):
-    arrays = [v for v in (eight, four) if v is not None]
-    shapes = []
-    if eight is not None:
-        shapes.append(jax.ShapeDtypeStruct((8,) + eight.shape[1:], eight.dtype))
-    if four is not None:
-        shapes.append(jax.ShapeDtypeStruct(four.shape, four.dtype))
-    return pl.pallas_call(
-        functools.partial(exchange_kernel, 0 if eight is None else eight.shape[0], eight is not None, four is not None),
-        out_shape=shapes,
-        in_specs=[ANY] * len(arrays),
-        out_specs=[ANY] * len(arrays),
-        scratch_shapes=[DMA((7,)), DMA((7,)), DMA((7,)), DMA((7,)), DMA((2,))],
-        compiler_params=pltpu.CompilerParams(collective_id=collective_id, has_side_effects=True),
-        name=name,
-    )(*arrays)
-
-
-def visible_keys(qidx, qlab, klab):
-    kidx = lax.broadcasted_iota(jnp.int32, (qidx.shape[0], klab.shape[1]), 1)
-    return (kidx <= qidx) & ((klab == 0) | (klab == qlab))
-
-
-def attend_kernel(q_ref, kv_ref, qidx_ref, qlab_ref, klab_ref, o_ref, lse_ref):
-    seen = visible_keys(qidx_ref[...], qlab_ref[...], klab_ref[...])
-    for head in range(3):
-        q = q_ref[:, 64 * head : 64 * head + 64]
-        k = kv_ref[:, 64 * head : 64 * head + 64]
-        v = kv_ref[:, 192 + 64 * head : 256 + 64 * head]
-        scores = lax.dot_general(q, k, (((1,), (1,)), ((), ())), preferred_element_type=jnp.float32) * SCALE
-        scores = jnp.where(seen, scores, NEG)
-        top = jnp.max(scores, axis=-1, keepdims=True)
-        weights = jnp.exp(scores - top)
-        total = jnp.sum(weights, axis=-1, keepdims=True)
-        probs = (weights / total).astype(jnp.bfloat16)
-        out = jnp.dot(probs, v, preferred_element_type=jnp.float32)
-        o_ref[:, 64 * head : 64 * head + 64] = out.astype(jnp.bfloat16)
-        lse_ref[:, head : head + 1] = top + jnp.log(total)
-
-
-def attend_back_kernel(q_ref, kv_ref, do_ref, lse_ref, qidx_ref, qlab_ref, klab_ref, dq_ref, dkv_ref, acc):
-    step = pl.program_id(0)
-
-    @pl.when(step == 0)
-    def _():
-        acc[...] = jnp.zeros_like(acc)
-
-    seen = visible_keys(qidx_ref[...], qlab_ref[...], klab_ref[...])
-    rows = (((0,), (0,)), ((), ()))
-    cols = (((1,), (1,)), ((), ()))
-    for head in range(3):
-        span = slice(64 * head, 64 * head + 64)
-        vspan = slice(192 + 64 * head, 256 + 64 * head)
-        q = q_ref[:, span]
-        k = kv_ref[:, span]
-        v = kv_ref[:, vspan]
-        do = do_ref[:, span]
-        scores = lax.dot_general(q, k, cols, preferred_element_type=jnp.float32) * SCALE
-        probs = jnp.where(seen, jnp.exp(scores - lse_ref[:, head : head + 1]), 0.0)
-        dprobs = lax.dot_general(do, v, cols, preferred_element_type=jnp.float32)
-        delta = jnp.sum(probs * dprobs, axis=-1, keepdims=True)
-        dscores = (probs * (dprobs - delta)).astype(jnp.bfloat16)
-        dq_ref[:, span] = (jnp.dot(dscores, k, preferred_element_type=jnp.float32) * SCALE).astype(jnp.bfloat16)
-        acc[:, span] += lax.dot_general(dscores, q, rows, preferred_element_type=jnp.float32) * SCALE
-        acc[:, vspan] += lax.dot_general(probs.astype(jnp.bfloat16), do, rows, preferred_element_type=jnp.float32)
-
-    @pl.when(step == pl.num_programs(0) - 1)
-    def _():
-        dkv_ref[...] = acc[...].astype(jnp.bfloat16)
-
-
-def row_block(width):
-    return pl.BlockSpec((128, width), lambda i: (i, 0))
-
-
-def whole(rows, width):
-    return pl.BlockSpec((rows, width), lambda i: (0, 0))
-
-
-def attend(q, kv, qidx, qlab, klab):
-    return pl.pallas_call(
-        attend_kernel,
-        grid=(4,),
-        out_shape=[jax.ShapeDtypeStruct((512, 192), jnp.bfloat16), jax.ShapeDtypeStruct((512, 128), jnp.float32)],
-        in_specs=[row_block(192), whole(1024, 384), row_block(1), row_block(1), whole(1, 1024)],
-        out_specs=[row_block(192), row_block(128)],
-        compiler_params=pltpu.CompilerParams(vmem_limit_bytes=40 << 20),
-        name="attend",
-    )(q, kv, qidx, qlab, klab)
-
-
-def attend_back(q, kv, do, lse, qidx, qlab, klab):
-    return pl.pallas_call(
-        attend_back_kernel,
-        grid=(4,),
-        out_shape=[jax.ShapeDtypeStruct((512, 192), jnp.bfloat16), jax.ShapeDtypeStruct((1024, 384), jnp.bfloat16)],
-        in_specs=[row_block(192), whole(1024, 384), row_block(192), row_block(128), row_block(1), row_block(1), whole(1, 1024)],
-        out_specs=[row_block(192), whole(1024, 384)],
-        scratch_shapes=[pltpu.VMEM((1024, 384), jnp.float32)],
-        compiler_params=pltpu.CompilerParams(vmem_limit_bytes=40 << 20),
-        name="attend_back",
-    )(q, kv, do, lse, qidx, qlab, klab)
 
 
 LEFT = (("na", D, 128), ("at", D, 128), ("nf", D, 128), ("sh", FF, 128), ("rc", D, SLOTS), ("hd", FF, SLOTS))
@@ -662,6 +516,11 @@
     )(*lower, *upper, small, sel_t)
 
 
+def split(values):
+    high = low(values)
+    return high, low(values - high.astype(jnp.float32))
+
+
 def rms_parts(values):
     scale = lax.rsqrt(jnp.mean(values * values, axis=-1, keepdims=True) + EPS)
     return scale, values * scale
@@ -670,7 +529,487 @@
 def rms_back(grad, gain, scale, unit):
     inner = grad * gain
     grad_values = scale * (inner - unit * jnp.mean(inner * unit, axis=-1, keepdims=True))
-    return grad_values, jnp.sum(grad * unit, axis=0)
+    return grad_values, jnp.sum(grad * unit, axis=0, keepdims=True)
+
+
+def dot(left, right):
+    return jnp.dot(left, right, preferred_element_type=jnp.float32)
+
+
+def dot_t(left, right):
+    return lax.dot_general(left, right, (((1,), (1,)), ((), ())), preferred_element_type=jnp.float32)
+
+
+def t_dot(left, right):
+    return lax.dot_general(left, right, (((0,), (0,)), ((), ())), preferred_element_type=jnp.float32)
+
+
+def low(values):
+    return values.astype(jnp.bfloat16)
+
+
+def rotate(values, cosine, sine):
+    half = HEAD_DIM // 2
+    lower = lax.broadcasted_iota(jnp.int32, (values.shape[0], 128), 1) % HEAD_DIM < half
+    parts = []
+    for start in range(0, values.shape[1], 128):
+        span = slice(start, start + 128)
+        part = values[:, span]
+        other = jnp.where(lower, pltpu.roll(part, 128 - half, 1), pltpu.roll(part, half, 1))
+        parts.append(part * cosine[:, span] + other * sine[:, span])
+    return jnp.concatenate(parts, axis=1)
+
+
+def visible_keys(qidx, qlab, klab):
+    kidx = lax.broadcasted_iota(jnp.int32, (qidx.shape[0], klab.shape[1]), 1)
+    return (kidx <= qidx) & ((klab == 0) | (klab == qlab))
+
+
+def pair_gates(logits, route):
+    lane = lax.broadcasted_iota(jnp.int32, logits.shape, 1)
+    picks = [lane == route[:, c : c + 1] + 2 for c in range(TOP)]
+    first, second = [jnp.sum(jnp.where(p, logits, 0.0), axis=1, keepdims=True) for p in picks]
+    top = jnp.maximum(first, second)
+    first, second = jnp.exp(first - top), jnp.exp(second - top)
+    total = first + second
+    return picks, [first / total, second / total]
+
+
+class Exchange:
+    def __init__(self, source, target, send, recv, everyone, block_of=None):
+        section, a, z, y, h = place_ids()
+        fsdp = fsdp_of(y, h)
+        offsets = [(1, 0), (1, 1), (1, 3), (1, 2)] if everyone else []
+        self.copies = []
+        for k, (da, dz) in enumerate(offsets + [(0, 1), (0, 3), (0, 2)]):
+            c, zz = ctx_of(a + da, z + dz), lax.rem(z + dz, 4)
+            block = zz if block_of == "ring" or not everyone else c
+            to = ctx_of(a, z) if everyone else z
+            self.copies.append(
+                pltpu.make_async_remote_copy(
+                    source.at[block], target.at[to], send.at[k], recv.at[k], device_id=(section, c, fsdp), device_id_type=MESH
+                )
+            )
+
+    def start(self):
+        for copy in self.copies:
+            copy.start()
+
+    def wait_recv(self):
+        for copy in self.copies:
+            copy.wait_recv()
+
+    def wait_send(self):
+        for copy in self.copies:
+            copy.wait_send()
+
+
+def ctx_peers():
+    section, a, z, y, h = place_ids()
+    fsdp = fsdp_of(y, h)
+    return [(section, ctx_of(a + da, z + dz), fsdp) for da in range(2) for dz in range(4) if (da, dz) != (0, 0)]
+
+
+def forward_kernel(
+    layer,
+    state, cosine, sine, qidx, qlab, klab, route, first_table, second_table, taken_t, small_t,
+    g_wide, g_gu, g_small, g_sd, g_egu, g_ed,
+    out, k_q, k_kv, k_lse, k_att, k_res, k_sj, k_rc, k_ej, k_ret,
+    wide, gu, small, sd, egu, ed, w_sem,
+    kv_pack, q_pack, kv_all, q_all, o_pack, o_in, lse, att, res, sj, sh, sent, rc, ej, eh, result, ret, k_sem,
+    kv_send, kv_recv, q_send, q_recv, o_send, o_recv, s_send, s_recv, r_send, r_recv,
+):
+    section, a, z, y, h = place_ids()
+    ctx = ctx_of(a, z)
+    loads = [
+        pltpu.make_async_copy(s.at[layer], t, w_sem.at[i])
+        for i, (s, t) in enumerate(((g_wide, wide), (g_gu, gu), (g_small, small), (g_sd, sd), (g_egu, egu), (g_ed, ed)))
+    ]
+    for load in (0, 2, 1, 3, 4, 5):
+        loads[load].start()
+    greet(ctx_peers())
+    saves = []
+
+    def save(source, target):
+        copy = pltpu.make_async_copy(source, target, k_sem.at[len(saves)])
+        copy.start()
+        saves.append(copy)
+
+    x = state[...].astype(jnp.float32)
+    scale, unit = rms_parts(x)
+    normed = low(unit * small_t[0:1, :])
+    loads[0].wait()
+    keys = low(rotate(dot(normed, wide[:, D : 2 * D]), cosine[...], sine[...]))
+    values = low(dot(normed, wide[:, 2 * D : 3 * D]))
+    for g in range(4):
+        kv_pack[g, :, 0:192] = keys[:, 192 * g : 192 * g + 192]
+        kv_pack[g, :, 192:384] = values[:, 192 * g : 192 * g + 192]
+    ex_kv = Exchange(kv_pack, kv_all, kv_send, kv_recv, True, "ring")
+    ex_kv.start()
+    queries = low(rotate(dot(normed, wide[:, 0:D]), cosine[...], sine[...]))
+    for g in range(4):
+        q_pack[g] = queries[:, 192 * g : 192 * g + 192]
+    ex_q = Exchange(q_pack, q_all, q_send, q_recv, False)
+    ex_q.start()
+    kv_all[ctx] = kv_pack[z]
+    q_all[z] = q_pack[z]
+    ex_q.wait_recv()
+    ex_kv.wait_recv()
+    save(kv_all, k_kv)
+    save(q_all, k_q)
+
+    @pl.loop(0, 4)
+    def _(d):
+        block = lax.rem(z + d + 1, 4)
+        seen = visible_keys(qidx[block], qlab[block], klab[...])
+        for head in range(3):
+            span = slice(64 * head, 64 * head + 64)
+            vspan = slice(192 + 64 * head, 256 + 64 * head)
+            k = kv_all[:, :, span].reshape(SEQ, HEAD_DIM)
+            v = kv_all[:, :, vspan].reshape(SEQ, HEAD_DIM)
+            scores = jnp.where(seen, dot_t(q_all[block, :, span], k) * SCALE, NEG)
+            top = jnp.max(scores, axis=-1, keepdims=True)
+            weights = jnp.exp(scores - top)
+            total = jnp.sum(weights, axis=-1, keepdims=True)
+            o_pack[block, :, span] = low(dot(low(weights / total), v))
+            lse[block, :, head : head + 1] = top + jnp.log(total)
+
+    ex_o = Exchange(o_pack, o_in, o_send, o_recv, False)
+    ex_o.start()
+    save(lse, k_lse)
+    o_in[z] = o_pack[z]
+    ex_o.wait_recv()
+    for g in range(4):
+        att[:, 192 * g : 192 * g + 192] = o_in[g]
+    save(att, k_att)
+    res[...] = x + dot(att[...], wide[:, 3 * D :])
+    save(res, k_res)
+    scale, unit = rms_parts(res[...])
+    normed = low(unit * small_t[1:2, :])
+    sent[...] = low(dot(taken_t[...], normed)).reshape(EXPERTS, PAD_CAP, D)
+    ex_s = Exchange(sent, rc, s_send, s_recv, True)
+    ex_s.start()
+    rc[ctx] = sent[ctx]
+    loads[2].wait()
+    _, gates = pair_gates(dot(normed, small[...]), route[...])
+    mix = first_table[...].astype(jnp.float32) * gates[0] + second_table[...].astype(jnp.float32) * gates[1]
+    loads[1].wait()
+
+    @pl.loop(0, FF // 256)
+    def _(j):
+        at = pl.ds(pl.multiple_of(j * 256, 256), 256)
+        up_at = pl.ds(pl.multiple_of(FF + j * 256, 256), 256)
+        gate, up = dot(normed, gu[:, at]), dot(normed, gu[:, up_at])
+        sj[:, at] = gate
+        sj[:, up_at] = up
+        sh[:, at] = low(gate * jax.nn.sigmoid(gate) * up)
+
+    save(sj, k_sj)
+    loads[3].wait()
+    shared_out = dot(sh[...], sd[...])
+    loads[4].wait()
+    ex_s.wait_recv()
+    save(rc, k_rc)
+
+    @pl.loop(0, FF // 256)
+    def _(j):
+        at = pl.ds(pl.multiple_of(j * 256, 256), 256)
+        up_at = pl.ds(pl.multiple_of(FF + j * 256, 256), 256)
+        gate, up = dot(rc[...].reshape(SLOTS, D), egu[:, at]), dot(rc[...].reshape(SLOTS, D), egu[:, up_at])
+        ej[:, at] = gate
+        ej[:, up_at] = up
+        eh[:, at] = low(gate * jax.nn.sigmoid(gate) * up)
+
+    save(ej, k_ej)
+    loads[5].wait()
+    for j in range(D // 256):
+        span = slice(256 * j, 256 * j + 256)
+        result[:, :, span] = low(dot(eh[...], ed[:, span])).reshape(EXPERTS, PAD_CAP, 256)
+    ex_r = Exchange(result, ret, r_send, r_recv, True)
+    ex_r.start()
+    ret[ctx] = result[ctx]
+    ex_r.wait_recv()
+    save(ret, k_ret)
+    high, rest = split(mix)
+    returned = ret[...].reshape(SLOTS, D)
+    mixed = dot(high, returned) + dot(rest, returned)
+    out[...] = low(res[...] + shared_out + mixed)
+    for ex in (ex_kv, ex_q, ex_o, ex_s, ex_r):
+        ex.wait_send()
+    for copy in saves:
+        copy.wait()
+
+
+def weight_scratch():
+    bf = jnp.bfloat16
+    return [
+        pltpu.VMEM((D, WIDE), bf), pltpu.VMEM((D, 2 * FF), bf), pltpu.VMEM((D, SMALL), bf),
+        pltpu.VMEM((FF, D), bf), pltpu.VMEM((D, 2 * FF), bf), pltpu.VMEM((FF, D), bf), DMA((6,)),
+    ]
+
+
+KEPT = (
+    ((4, ROWS, 192), jnp.bfloat16), ((8, ROWS, 384), jnp.bfloat16), ((4, ROWS, 128), jnp.float32), ((ROWS, D), jnp.bfloat16),
+    ((ROWS, D), jnp.float32), ((ROWS, 2 * FF), jnp.float32), ((EXPERTS, PAD_CAP, D), jnp.bfloat16),
+    ((SLOTS, 2 * FF), jnp.float32), ((EXPERTS, PAD_CAP, D), jnp.bfloat16),
+)
+
+
+def layer_forward(layer, state, geometry, plan, small_t, weights):
+    bf, f32 = jnp.bfloat16, jnp.float32
+    cosine, sine, qidx, qlab, klab = geometry
+    route, first_table, second_table, taken_t = plan
+    slots = pltpu.VMEM((EXPERTS, PAD_CAP, D), bf)
+    outs = pl.pallas_call(
+        functools.partial(forward_kernel, layer),
+        out_shape=[jax.ShapeDtypeStruct((ROWS, D), bf)] + [jax.ShapeDtypeStruct(s, t) for s, t in KEPT],
+        in_specs=[VMEM] * 11 + [ANY] * 6,
+        out_specs=[VMEM] + [ANY] * len(KEPT),
+        scratch_shapes=weight_scratch() + [
+            pltpu.VMEM((4, ROWS, 384), bf), pltpu.VMEM((4, ROWS, 192), bf),
+            pltpu.VMEM((8, ROWS, 384), bf), pltpu.VMEM((4, ROWS, 192), bf),
+            pltpu.VMEM((4, ROWS, 192), bf), pltpu.VMEM((4, ROWS, 192), bf),
+            pltpu.VMEM((4, ROWS, 128), f32), pltpu.VMEM((ROWS, D), bf), pltpu.VMEM((ROWS, D), f32),
+            pltpu.VMEM((ROWS, 2 * FF), f32), pltpu.VMEM((ROWS, FF), bf),
+            slots, slots, pltpu.VMEM((SLOTS, 2 * FF), f32), pltpu.VMEM((SLOTS, FF), bf), slots, slots, DMA((len(KEPT),)),
+            DMA((7,)), DMA((7,)), DMA((3,)), DMA((3,)), DMA((3,)), DMA((3,)), DMA((7,)), DMA((7,)), DMA((7,)), DMA((7,)),
+        ],
+        compiler_params=pltpu.CompilerParams(collective_id=1 + layer, has_side_effects=True, vmem_limit_bytes=60 << 20),
+        name="layer_forward",
+    )(state, cosine, sine, qidx, qlab, klab, route, first_table, second_table, taken_t, small_t, *weights)
+    return outs[0], outs[1:]
+
+
+def backward_kernel(
+    layer,
+    grad, state, cosine, sine, qidx, qlab, klab, route, first_table, second_table, taken, small_t,
+    g_wide, g_gu, g_small, g_sd, g_egu, g_ed,
+    k_q, k_kv, k_lse, k_att, k_res, k_sj, k_rc, k_ej, k_ret,
+    out, grad_small,
+    p_na, p_at, p_nf, p_sh, p_rc, p_hd, p_qkv, p_pr, p_gu, p_sd, p_j, p_er,
+    wide, gu, small, sd, egu, ed, w_sem,
+    q_all, kv_all, lse, att, res, sj, rc, ej, ret, i_sem,
+    t_na, t_at, t_nf, t_sh, t_rc, t_hd, m_qkv, m_pr, m_gu, m_sd, m_j, p_sem,
+    sent, er, back, slots, o_pack, o_in, dq_pack, dq_in, dkv_pack, dkv_in, dkv_sum, normed_grad, sh, eh,
+    s_send, s_recv, r_send, r_recv, o_send, o_recv, q_send, q_recv, kv_send, kv_recv,
+):
+    section, a, z, y, h = place_ids()
+    ctx = ctx_of(a, z)
+    loads = [
+        pltpu.make_async_copy(s.at[layer], t, w_sem.at[i])
+        for i, (s, t) in enumerate(((g_wide, wide), (g_gu, gu), (g_small, small), (g_sd, sd), (g_egu, egu), (g_ed, ed)))
+    ]
+    reads = [
+        pltpu.make_async_copy(s, t, i_sem.at[i])
+        for i, (s, t) in enumerate(zip((k_q, k_kv, k_lse, k_att, k_res, k_sj, k_rc, k_ej, k_ret), (q_all, kv_all, lse, att, res, sj, rc, ej, ret)))
+    ]
+    loads[2].start()
+    reads[4].start()
+    loads[3].start()
+    reads[5].start()
+    loads[1].start()
+    reads[8].start()
+    loads[5].start()
+    reads[7].start()
+    loads[4].start()
+    for i in (6, 3, 0, 1, 2):
+        reads[i].start()
+    loads[0].start()
+    greet(ctx_peers())
+    saves = []
+
+    def save(source, target):
+        copy = pltpu.make_async_copy(source, target, p_sem.at[len(saves)])
+        copy.start()
+        saves.append(copy)
+
+    grad_out = grad[...].astype(jnp.float32)
+    m_sd[...] = low(grad_out)
+    save(m_sd, p_sd)
+    loads[2].wait()
+    reads[4].wait()
+    scale_ffn, unit_ffn = rms_parts(res[...])
+    normed = low(unit_ffn * small_t[1:2, :])
+    picks, gates = pair_gates(dot(normed, small[...]), route[...])
+    first, second = first_table[...].astype(jnp.float32), second_table[...].astype(jnp.float32)
+    mix_high, mix_rest = split(first * gates[0] + second * gates[1])
+    out_high, out_rest = split(grad_out)
+    slot_grads = t_dot(mix_high, out_high) + t_dot(mix_rest, out_high) + t_dot(mix_high, out_rest)
+    sent[...] = low(slot_grads).reshape(EXPERTS, PAD_CAP, D)
+    ex_s = Exchange(sent, er, s_send, s_recv, True)
+    ex_s.start()
+    er[ctx] = sent[ctx]
+
+    loads[3].wait()
+    reads[5].wait()
+
+    @pl.loop(0, FF // 256)
+    def _(j):
+        at = pl.ds(pl.multiple_of(j * 256, 256), 256)
+        up_at = pl.ds(pl.multiple_of(FF + j * 256, 256), 256)
+        hidden_grad = dot_t(m_sd[...], sd[at, :])
+        gate, up = sj[:, at], sj[:, up_at]
+        sig = jax.nn.sigmoid(gate)
+        m_gu[:, at] = low(hidden_grad * up * sig * (1.0 + gate * (1.0 - sig)))
+        m_gu[:, up_at] = low(hidden_grad * gate * sig)
+        sh[:, at] = low(gate * sig * up)
+        t_sh[at, :] = low(jnp.transpose(gate * sig * up))
+
+    save(m_gu, p_gu)
+    save(t_sh, p_sh)
+    t_nf[...] = low(jnp.transpose(unit_ffn * small_t[1:2, :]))
+    save(t_nf, p_nf)
+    loads[1].wait()
+
+    @pl.loop(0, D // 256)
+    def _(j):
+        at = pl.ds(pl.multiple_of(j * 256, 256), 256)
+        normed_grad[:, at] = dot_t(m_gu[...], gu[at, :])
+
+    reads[8].wait()
+    products = dot_t(m_sd[...], ret[...].reshape(SLOTS, D))
+    gate_grads = [jnp.sum(products * first, axis=1, keepdims=True), jnp.sum(products * second, axis=1, keepdims=True)]
+    inner = gates[0] * gate_grads[0] + gates[1] * gate_grads[1]
+    chosen = [g * (d - inner) for g, d in zip(gates, gate_grads)]
+    logit_grads = jnp.where(picks[0], chosen[0], 0.0) + jnp.where(picks[1], chosen[1], 0.0)
+    logit_high, logit_rest = split(logit_grads)
+    grad_small[...] = t_dot(normed, logit_high) + t_dot(normed, logit_rest)
+    normed_grad[...] += dot_t(logit_high, small[...]) + dot_t(logit_rest, small[...])
+
+    loads[5].wait()
+    reads[7].wait()
+    ex_s.wait_recv()
+    save(er, p_er)
+
+    @pl.loop(0, FF // 256)
+    def _(j):
+        at = pl.ds(pl.multiple_of(j * 256, 256), 256)
+        up_at = pl.ds(pl.multiple_of(FF + j * 256, 256), 256)
+        hidden_grad = dot_t(er[...].reshape(SLOTS, D), ed[at, :])
+        gate, up = ej[:, at], ej[:, up_at]
+        sig = jax.nn.sigmoid(gate)
+        m_j[:, at] = low(hidden_grad * up * sig * (1.0 + gate * (1.0 - sig)))
+        m_j[:, up_at] = low(hidden_grad * gate * sig)
+        eh[:, at] = low(gate * sig * up)
+
+    save(m_j, p_j)
+    loads[4].wait()
+
+    @pl.loop(0, D // 256)
+    def _(j):
+        at = pl.ds(pl.multiple_of(j * 256, 256), 256)
+        back[:, :, at] = low(dot_t(m_j[...], egu[at, :])).reshape(EXPERTS, PAD_CAP, 256)
+
+    ex_r = Exchange(back, slots, r_send, r_recv, True)
+    ex_r.start()
+    slots[ctx] = back[ctx]
+    reads[6].wait()
+    t_hd[...] = jnp.transpose(eh[...])
+    save(t_hd, p_hd)
+    t_rc[...] = jnp.transpose(rc[...].reshape(SLOTS, D))
+    save(t_rc, p_rc)
+    reads[3].wait()
+    t_at[...] = jnp.transpose(att[...])
+    save(t_at, p_at)
+    loads[0].wait()
+    ex_r.wait_recv()
+    grad_normed = normed_grad[...] + dot(taken[...], slots[...].reshape(SLOTS, D))
+    grad_values, gain_ffn = rms_back(grad_normed, small_t[1:2, :], scale_ffn, unit_ffn)
+    grad_res = grad_out + grad_values
+    m_pr[...] = low(grad_res)
+    save(m_pr, p_pr)
+    grad_att = low(dot_t(m_pr[...], wide[:, 3 * D :]))
+    for g in range(4):
+        o_pack[g] = grad_att[:, 192 * g : 192 * g + 192]
+    ex_o = Exchange(o_pack, o_in, o_send, o_recv, False)
+    ex_o.start()
+    o_in[z] = o_pack[z]
+    scale_attn, unit_attn = rms_parts(state[...].astype(jnp.float32))
+    t_na[...] = low(jnp.transpose(unit_attn * small_t[0:1, :]))
+    save(t_na, p_na)
+    dkv_sum[...] = jnp.zeros_like(dkv_sum)
+    for i in (0, 1, 2):
+        reads[i].wait()
+    ex_o.wait_recv()
+
+    @pl.loop(0, 4)
+    def _(d):
+        block = lax.rem(z + d + 1, 4)
+        seen = visible_keys(qidx[block], qlab[block], klab[...])
+        for head in range(3):
+            span = slice(64 * head, 64 * head + 64)
+            vspan = slice(192 + 64 * head, 256 + 64 * head)
+            q, do = q_all[block, :, span], o_in[block, :, span]
+            k = kv_all[:, :, span].reshape(SEQ, HEAD_DIM)
+            v = kv_all[:, :, vspan].reshape(SEQ, HEAD_DIM)
+            scores = dot_t(q, k) * SCALE
+            probs = jnp.where(seen, jnp.exp(scores - lse[block, :, head : head + 1]), 0.0)
+            dprobs = dot_t(do, v)
+            delta = jnp.sum(probs * dprobs, axis=-1, keepdims=True)
+            dscores = low(probs * (dprobs - delta))
+            dq_pack[block, :, span] = low(dot(dscores, k) * SCALE)
+            dkv_sum[:, span] += t_dot(dscores, q) * SCALE
+            dkv_sum[:, vspan] += t_dot(low(probs), do)
+
+    ex_q = Exchange(dq_pack, dq_in, q_send, q_recv, False)
+    ex_q.start()
+    dkv_pack[...] = low(dkv_sum[...]).reshape(8, ROWS, 384)
+    ex_kv = Exchange(dkv_pack, dkv_in, kv_send, kv_recv, True)
+    ex_kv.start()
+    dq_in[z] = dq_pack[z]
+    dkv_in[ctx] = dkv_pack[ctx]
+    ex_q.wait_recv()
+    ex_kv.wait_recv()
+    dq = jnp.concatenate([dq_in[g].astype(jnp.float32) for g in range(4)], axis=1)
+    both = [dkv_in[g].astype(jnp.float32) + dkv_in[4 + g].astype(jnp.float32) for g in range(4)]
+    dk = jnp.concatenate([v[:, :192] for v in both], axis=1)
+    dv = jnp.concatenate([v[:, 192:] for v in both], axis=1)
+    m_qkv[:, 0:D] = low(rotate(dq, cosine[...], -sine[...]))
+    m_qkv[:, D : 2 * D] = low(rotate(dk, cosine[...], -sine[...]))
+    m_qkv[:, 2 * D :] = low(dv)
+    save(m_qkv, p_qkv)
+    grad_normed = dot_t(m_qkv[...], wide[:, 0 : 3 * D])
+    grad_values, gain_attn = rms_back(grad_normed, small_t[0:1, :], scale_attn, unit_attn)
+    out[...] = grad_res + grad_values
+    lane = lax.broadcasted_iota(jnp.int32, (D, SMALL), 1)
+    gains_t = jnp.transpose(jnp.concatenate([gain_attn, gain_ffn, jnp.zeros((SMALL - 2, D), jnp.float32)], axis=0))
+    grad_small[...] = jnp.where(lane < 2, gains_t, grad_small[...])
+    for ex in (ex_s, ex_r, ex_o, ex_q, ex_kv):
+        ex.wait_send()
+    for copy in saves:
+        copy.wait()
+
+
+def layer_backward(layer, grad, state, geometry, plan, taken, small_t, weights, kept):
+    bf, f32 = jnp.bfloat16, jnp.float32
+    cosine, sine, qidx, qlab, klab = geometry
+    route, first_table, second_table, _ = plan
+    slots = pltpu.VMEM((EXPERTS, PAD_CAP, D), bf)
+    shapes = [(r, c) for _, r, c in LEFT + RIGHT]
+    shapes[-1] = (EXPERTS, PAD_CAP, D)
+    outs = pl.pallas_call(
+        functools.partial(backward_kernel, layer),
+        out_shape=[jax.ShapeDtypeStruct((ROWS, D), f32), jax.ShapeDtypeStruct((D, SMALL), f32)]
+        + [jax.ShapeDtypeStruct(s, bf) for s in shapes],
+        in_specs=[VMEM] * 12 + [ANY] * (6 + len(KEPT)),
+        out_specs=[VMEM, VMEM] + [ANY] * N_OPS,
+        scratch_shapes=weight_scratch()
+        + [pltpu.VMEM(s, t) for s, t in KEPT] + [DMA((len(KEPT),))]
+        + [pltpu.VMEM(s, bf) for s in shapes[:-1]] + [DMA((N_OPS,))]
+        + [
+            slots, slots, slots, slots,
+            pltpu.VMEM((4, ROWS, 192), bf), pltpu.VMEM((4, ROWS, 192), bf),
+            pltpu.VMEM((4, ROWS, 192), bf), pltpu.VMEM((4, ROWS, 192), bf),
+            pltpu.VMEM((8, ROWS, 384), bf), pltpu.VMEM((8, ROWS, 384), bf), pltpu.VMEM((SEQ, 384), f32),
+            pltpu.VMEM((ROWS, D), f32), pltpu.VMEM((ROWS, FF), bf), pltpu.VMEM((SLOTS, FF), bf),
+            DMA((7,)), DMA((7,)), DMA((7,)), DMA((7,)), DMA((3,)), DMA((3,)), DMA((3,)), DMA((3,)), DMA((7,)), DMA((7,)),
+        ],
+        compiler_params=pltpu.CompilerParams(collective_id=3 + layer, has_side_effects=True, vmem_limit_bytes=62 << 20),
+        name="layer_backward",
+    )(grad, state, cosine, sine, qidx, qlab, klab, route, first_table, second_table, taken, small_t, *weights, *kept)
+    operands = list(outs[2:])
+    operands[-1] = operands[-1].reshape(SLOTS, D)
+    return outs[0], operands, outs[1]
 
 
 def token_positions(group_row):
@@ -693,14 +1032,6 @@
     return cosine, sine
 
 
-def rotate(values, cosine, sine):
-    half = HEAD_DIM // 2
-    ahead = jnp.concatenate([values[:, half:], values[:, :half]], axis=1)
-    behind = jnp.concatenate([values[:, -half:], values[:, :-half]], axis=1)
-    lower = lax.broadcasted_iota(jnp.int32, values.shape, 1) % HEAD_DIM < half
-    return values * cosine + jnp.where(lower, ahead, behind) * sine
-
-
 def slot_tables(route, rank):
     pairs = ROWS * TOP
     expert = route.reshape(-1)
@@ -708,150 +1039,10 @@
     earlier = (expert[None, :] == expert[:, None]) & (key[None, :] < key[:, None])
     slot = jnp.sum(earlier.astype(jnp.int32), axis=1)
     place = jnp.where(slot < CAP, expert * PAD_CAP + slot, -1).reshape(ROWS, TOP)
-    every = jnp.arange(EXPERTS * PAD_CAP, dtype=jnp.int32)
-    return [(place[:, c : c + 1] == every[None, :]) for c in range(TOP)]
-
-
-def heads_out(values, count):
-    return [values[:, 192 * g : 192 * g + 192] for g in range(count)]
-
-
-def dot(left, right):
-    return jnp.dot(left, right, preferred_element_type=jnp.float32)
-
-
-def dot_t(left, right):
-    return lax.dot_general(left, right, (((1,), (1,)), ((), ())), preferred_element_type=jnp.float32)
-
-
-def t_dot(left, right, precision=None):
-    return lax.dot_general(left, right, (((0,), (0,)), ((), ())), precision=precision, preferred_element_type=jnp.float32)
-
-
-def low(values):
-    return values.astype(jnp.bfloat16)
-
-
-def silu_parts(joined):
-    gate, up = joined[:, :FF], joined[:, FF:]
-    return gate, up, jax.nn.sigmoid(gate)
-
-
-def swiglu(joined):
-    gate, up, sig = silu_parts(joined)
-    return gate * sig * up
-
-
-def swiglu_back(joined, grad):
-    gate, up, sig = silu_parts(joined)
-    return jnp.concatenate([grad * up * sig * (1.0 + gate * (1.0 - sig)), grad * gate * sig], axis=1)
-
-
-def layer_forward(state, weights, geometry, route, chosen):
-    w_wide, w_gu, w_small, w_sd, w_egu, w_ed = weights
-    cosine, sine, qidx, qlab, klab = geometry
-    gains = w_small[:, :2].astype(jnp.float32)
-    router = w_small[:, 2 : 2 + EXPERTS]
-    scale_attn, unit_attn = rms_parts(state)
-    normed_attn = low(unit_attn * gains[:, 0])
-    joined = dot(normed_attn, w_wide[:, : 3 * D])
-    queries = low(rotate(joined[:, :D], cosine, sine))
-    keys = low(rotate(joined[:, D : 2 * D], cosine, sine))
-    values = low(joined[:, 2 * D :])
-    kv = jnp.stack([jnp.concatenate([k, v], axis=1) for k, v in zip(heads_out(keys, 4), heads_out(values, 4))])
-    kv_all, q_all = exchange("exchange_qkv", 1, kv, jnp.stack(heads_out(queries, 4)))
-    kv_all, q_all = kv_all.reshape(SEQ, 384), q_all.reshape(512, 192)
-    mixed_heads, lse = attend(q_all, kv_all, qidx, qlab, klab)
-    (back,) = exchange("exchange_heads", 2, None, mixed_heads.reshape(4, ROWS, 192))
-    attended = jnp.concatenate([back[g] for g in range(4)], axis=1)
-    residual = state + dot(attended, w_wide[:, 3 * D :])
-    scale_ffn, unit_ffn = rms_parts(residual)
-    normed_ffn = low(unit_ffn * gains[:, 1])
-    logits = dot(normed_ffn, router)
-    labels = jnp.arange(EXPERTS, dtype=jnp.int32)
-    picks = [(route[:, c : c + 1] == labels[None, :]) for c in range(TOP)]
-    pair_logits = jnp.concatenate([jnp.sum(jnp.where(p, logits, 0.0), axis=1, keepdims=True) for p in picks], axis=1)
-    gates = jax.nn.softmax(pair_logits, axis=-1)
-    taken = low(chosen[0] | chosen[1])
-    sent = low(t_dot(taken, normed_ffn))
-    (received,) = exchange("exchange_slots", 4, sent.reshape(EXPERTS, PAD_CAP, D))
-    shared_joined = dot(normed_ffn, w_gu)
-    shared_hidden = low(swiglu(shared_joined))
-    shared_out = dot(shared_hidden, w_sd)
-    received = received.reshape(SLOTS, D)
-    expert_joined = dot(received, w_egu)
-    expert_hidden = low(swiglu(expert_joined))
-    result = low(dot(expert_hidden, w_ed))
-    (returned,) = exchange("exchange_slots", 4, result.reshape(EXPERTS, PAD_CAP, D))
-    returned = returned.reshape(SLOTS, D)
-    weights_of = jnp.where(chosen[0], gates[:, 0:1], 0.0) + jnp.where(chosen[1], gates[:, 1:2], 0.0)
-    mixed = jnp.dot(weights_of, returned.astype(jnp.float32), precision=HIGH)
-    output = residual + shared_out + mixed
-    kept = dict(
-        scale_attn=scale_attn, unit_attn=unit_attn, normed_attn=normed_attn, q_all=q_all, kv_all=kv_all, lse=lse,
-        attended=attended, scale_ffn=scale_ffn, unit_ffn=unit_ffn, normed_ffn=normed_ffn, gates=gates, taken=taken,
-        shared_joined=shared_joined, shared_hidden=shared_hidden, received=received, expert_joined=expert_joined,
-        expert_hidden=expert_hidden, returned=returned, picks=picks, weights_of=weights_of,
-    )
-    return output, kept
-
-
-def layer_backward(grad_output, kept, weights, geometry, chosen):
-    w_wide, w_gu, w_small, w_sd, w_egu, w_ed = weights
-    cosine, sine, qidx, qlab, klab = geometry
-    gains = w_small[:, :2].astype(jnp.float32)
-    router = w_small[:, 2 : 2 + EXPERTS]
-    grad_rounded = low(grad_output)
-    slot_grads = low(t_dot(kept["weights_of"], grad_output, HIGH))
-    (grad_result,) = exchange("exchange_slots", 4, slot_grads.reshape(EXPERTS, PAD_CAP, D))
-    grad_result = grad_result.reshape(SLOTS, D)
-    grad_expert_joined = low(swiglu_back(kept["expert_joined"], dot_t(grad_result, w_ed)))
-    grad_sent = low(dot_t(grad_expert_joined, w_egu))
-    (grad_slots,) = exchange("exchange_slots", 4, grad_sent.reshape(EXPERTS, PAD_CAP, D))
-    grad_shared_joined = low(swiglu_back(kept["shared_joined"], dot_t(grad_rounded, w_sd)))
-    grad_normed = dot_t(grad_shared_joined, w_gu)
-    grad_normed = grad_normed + dot(kept["taken"], grad_slots.reshape(SLOTS, D))
-    products = dot_t(grad_rounded, kept["returned"])
-    grad_gates = jnp.concatenate(
-        [jnp.sum(jnp.where(c, products, 0.0), axis=1, keepdims=True) for c in chosen], axis=1
-    )
-    gates = kept["gates"]
-    grad_chosen = gates * (grad_gates - jnp.sum(gates * grad_gates, axis=1, keepdims=True))
-    grad_logits = sum(jnp.where(p, grad_chosen[:, c : c + 1], 0.0) for c, p in enumerate(kept["picks"]))
-    grad_router = t_dot(kept["normed_ffn"].astype(jnp.float32), grad_logits, HIGH)
-    grad_normed = grad_normed + lax.dot_general(
-        grad_logits, router.astype(jnp.float32), (((1,), (1,)), ((), ())), precision=HIGH
-    )
-    grad_residual, grad_gain_ffn = rms_back(grad_normed, gains[:, 1], kept["scale_ffn"], kept["unit_ffn"])
-    grad_residual = grad_output + grad_residual
-    grad_projected = low(grad_residual)
-    grad_attended = low(dot_t(grad_projected, w_wide[:, 3 * D :]))
-    (grad_heads,) = exchange("exchange_heads", 2, None, jnp.stack(heads_out(grad_attended, 4)))
-    dq, dkv = attend_back(
-        kept["q_all"], kept["kv_all"], grad_heads.reshape(512, 192), kept["lse"], qidx, qlab, klab
-    )
-    dkv_all, dq_all = exchange("exchange_grads", 3, dkv.reshape(8, ROWS, 384), dq.reshape(4, ROWS, 192))
-    dkv_all = dkv_all.astype(jnp.float32)
-    dkv_all = dkv_all[:4] + dkv_all[4:]
-    grad_queries = jnp.concatenate([dq_all[g] for g in range(4)], axis=1).astype(jnp.float32)
-    grad_keys = jnp.concatenate([dkv_all[g, :, :192] for g in range(4)], axis=1)
-    grad_values = jnp.concatenate([dkv_all[g, :, 192:] for g in range(4)], axis=1)
-    grad_joined = low(
-        jnp.concatenate([rotate(grad_queries, cosine, -sine), rotate(grad_keys, cosine, -sine), grad_values], axis=1)
-    )
-    grad_normed_attn = dot_t(grad_joined, w_wide[:, : 3 * D])
-    grad_state, grad_gain_attn = rms_back(grad_normed_attn, gains[:, 0], kept["scale_attn"], kept["unit_attn"])
-    grad_input = grad_residual + grad_state
-    operands = [
-        kept["normed_attn"].T, kept["attended"].T, kept["normed_ffn"].T, kept["shared_hidden"].T,
-        kept["received"].T, kept["expert_hidden"].T,
-        grad_joined, grad_projected, grad_shared_joined, grad_rounded, grad_expert_joined, grad_result,
-    ]
-    small = jnp.concatenate(
-        [grad_gain_attn[:, None], grad_gain_ffn[:, None], grad_router, jnp.zeros((D, SMALL - 2 - EXPERTS), jnp.float32)],
-        axis=1,
-    )
-    return grad_input, operands, small
+    every = jnp.arange(SLOTS, dtype=jnp.int32)
+    first, second = [place[:, c : c + 1] == every[None, :] for c in range(TOP)]
+    both = low(first | second)
+    return (route, low(first), low(second), both.T), both
 
 
 def swap_cores(value):
@@ -873,7 +1064,7 @@
     gathered = gather_weights(
         jnp.pad(pack, ((0, 16 - OWN), (0, 0))), shared_down[0], expert_gate_up[0, 0], expert_down[0, 0]
     )
-    weights = [tuple(w[layer] for w in gathered) for layer in range(2)]
+    small_t = [gathered[2][layer, :, :8].astype(jnp.float32).T for layer in range(2)]
 
     def mine(value):
         return jnp.where(first, value[0], value[1])
@@ -885,26 +1076,24 @@
     passed = swap_cores(other(picked))
     own = mine(picked)
     plans = [jnp.where(first, own, passed), jnp.where(first, passed, own)]
-    chosen = [slot_tables(plan[0], plan[1]) for plan in plans]
+    plans, taken = zip(*[slot_tables(plan[0], plan[1]) for plan in plans])
 
     group_row = mine(group_ids[:, 0])
     positions = token_positions(group_row)
     cosine, sine = rotation_tables(lax.dynamic_slice_in_dim(positions, ctx * ROWS, ROWS))
     half_start = ctx // 4 * 512
-    qlab = lax.dynamic_slice_in_dim(group_row, half_start, 512)[:, None]
-    qidx = (half_start + jnp.arange(512, dtype=jnp.int32))[:, None]
+    qlab = lax.dynamic_slice_in_dim(group_row, half_start, 512).reshape(4, ROWS, 1)
+    qidx = (half_start + jnp.arange(512, dtype=jnp.int32)).reshape(4, ROWS, 1)
     geometry = (cosine, sine, qidx, qlab, group_row[None, :])
 
-    state = mine(x_in[:, 0]).astype(jnp.float32)
-    output, kept_lower = layer_forward(state, weights[0], geometry, plans[0][0], chosen[0])
-    hidden = low(output)
-    output, kept_upper = layer_forward(hidden.astype(jnp.float32), weights[1], geometry, plans[1][0], chosen[1])
-    final = low(output)
-
-    grad_final = mine(cotangent[:, 0]).astype(jnp.float32)
-    hidden_grad, operands_upper, small_upper = layer_backward(grad_final, kept_upper, weights[1], geometry, chosen[1])
+    state = mine(x_in[:, 0])
+    hidden, kept_lower = layer_forward(0, state, geometry, plans[0], small_t[0], gathered)
+    final, kept_upper = layer_forward(1, hidden, geometry, plans[1], small_t[1], gathered)
+    hidden_grad, operands_upper, small_upper = layer_backward(
+        1, mine(cotangent[:, 0]), hidden, geometry, plans[1], taken[1], small_t[1], gathered, kept_upper
+    )
     input_grad, operands_lower, small_lower = layer_backward(
-        low(hidden_grad).astype(jnp.float32), kept_lower, weights[0], geometry, chosen[0]
+        0, low(hidden_grad), state, geometry, plans[0], taken[0], small_t[0], gathered, kept_lower
     )
     small = jnp.where(first, small_lower, small_upper) + swap_cores(jnp.where(first, small_upper, small_lower))
     pack_grad, sd_grad, egu_grad, ed_grad = weight_grads(operands_lower, operands_upper, small)

time: 821 us -> 640 us (0.78)
  matrix products: 116 us -> 0 us
  local copies, waits for them, and re-layouts: 75.6 us -> 17.5 us
  other arithmetic: 49.1 us -> 18.2 us
  Pallas kernels: 565 us -> 591 us
    dot_general x40 -> x0, matrix products: 116 us -> none  [the longest x14 58.1 us: dot_t(): lax.dot_general(left, right, (((1,), (1,)), ((), ())), preferred_element_...]
    pallas_call x20 -> x4, Pallas kernels: 192 us -> 215 us  [the longest x2 108 us: layer_forward(): pl.pallas_call(functools.partial(forward_kernel, layer), out_shape=[jax.S...]
    unnamed x396 -> x38, local copies, waits for them, and re-layouts: 26.6 us -> 9.51 us
    transpose x8 -> x0, local copies, waits for them, and re-layouts: 12.5 us -> none  [the longest x2 3.56 us: layer_backward(): kept['normed_ffn']]
    squeeze x8 -> x0, local copies, waits for them, and re-layouts: 11.4 us -> none  [the longest x2 7.75 us: on_device(): weights = [tuple((w[layer] for w in gathered)) for layer in range(2)]]
    another operation x21 -> x1, other arithmetic: 10.8 us -> 0.18 us  [the longest x10 5.72 us: layer_forward(): jnp.stack([jnp.concatenate([k, v], axis=1) for k, v in zip(heads_out(keys...]
    transpose x7 -> x1, other arithmetic: 10 us -> 0.62 us  [on_device(): gathered[2][layer, :, :8].astype(jnp.float32)]
  transfers between devices with their start and end apart: 4 -> 4, of which waited for: 0 -> 0; matrix products, arithmetic and copies ran while one was open for 10% -> 3% of each run, Pallas kernels for 50% -> 60%
where the time goes in v2:
time: 640 us; the launch traced here: 630 us
  Pallas kernels  591 us (92%)
  other arithmetic  18.2 us (3%)
  local copies, waits for them, and re-layouts  17.5 us (3%)
    pallas_call x1, Pallas kernels, weight_grads(): pl.pallas_call(grads_kernel, out_shape=[jax.ShapeDtypeStruct((16, PACK),...  220 us
    pallas_call x1, Pallas kernels, gather_weights(): pl.pallas_call(gather_kernel, out_shape=[jax.ShapeDtypeStruct(s, bf) for...  156 us
    pallas_call x2, Pallas kernels, layer_forward(): pl.pallas_call(functools.partial(forward_kernel, layer), out_shape=[jax.S...  108 us
    pallas_call x2, Pallas kernels, layer_backward(): pl.pallas_call(functools.partial(backward_kernel, layer), out_shape=[jax....  107 us
  transfers between devices with their start and end apart: 4, of which 0 were waited for; matrix products, arithmetic and copies ran while one was open for 3% of the time, Pallas kernels for 60%

profile of v2, /device:TPU:0, one launch (start us, length us, event | category | flops | bytes accessed | tf_op | source)
XLA Modules:
  0.0 630.1 jit_solution(12855455732117819626)
XLA Ops:
  0.7 0.8 fusion.13
  1.5 0.1 copy.111
  1.6 0.1 copy.112
  1.9 0.7 add_add_fusion.qidx
  2.7 0.7 broadcast_select_fusion.6
  3.4 1.3 fusion.16.klab
  4.7 0.1 and_convert_fusion.1.sel
  4.8 0.7 and_convert_fusion.refs_25_
  5.5 0.1 convert_reduce_fusion.2
  5.6 0.2 reduce-window.8
  5.8 0.1 select_reduce_fusion
  5.9 0.7 copy.88
  6.6 0.8 copy.89
  7.4 1.1 concatenate.11
  8.5 1.1 copy-done.1
  9.6 1.0 copy-done.2
  10.6 0.8 copy-done.3
  11.4 156.2 %gather_weights.1 = (bf16[2,768,3072]{2,1,0:T(8,128)(2,1)}, bf16[2,768,4096]{2,1,0:T(8,128)(2,1)}, bf16[2,768,128]{2,1,0:T(8,128)(2,1)S(1)}, bf16[2,2048,768]{2,...) custom-call(bf16[16,7296]{1,0:T(8,128)(2,1)S(1)} %pad.4.pack, ...), custom_call_target="tpu_custom_call" | custom-call | tf_op jit(solution)/shard_map/gather_weights/pallas_call | solution.py:244
  167.7 0.2 copy.90
  167.9 0.6 convert_bitcast_fusion.1
  168.5 0.7 select_bitcast_fusion.5.state
  169.2 0.7 select_bitcast_fusion.2.grad
  170.0 0.1 fusion.12
  170.2 0.9 copy.91.cosine
  171.2 0.9 copy.92.sine
  172.1 0.9 copy.93.qlab
  173.0 0.6 fusion.15
  173.6 0.1 mul.74
  173.8 0.1 eq.206
  173.9 0.2 convert_reduce_fusion.1
  174.1 0.1 reduce_sum.43
  174.3 0.6 fusion.14
  174.9 0.1 mul.77
  175.1 0.1 eq.230
  175.2 0.2 convert_reduce_fusion
  175.4 0.1 reduce_sum.45
  175.6 0.2 slice_reduce_fusion.2
  175.8 0.7 fusion.9.taken_t
  176.5 0.8 fusion.6
  177.3 0.2 slice_reduce_fusion
  177.5 0.8 fusion.7
  178.3 0.7 fusion.11.taken_t
  179.0 56.0 %layer_forward.2 = (bf16[128,768]{1,0:T(8,128)(2,1)}, bf16[4,128,192]{2,1,0:T(8,128)(2,1)}, bf16[8,128,384]{2,1,0:T(8,128)(2,1)}, f32[4,128,128]{2,1,0:T(8,128)}...) custom-call(bf16[128,768]{1,0:T(8,128)(2,1)} %select_bitcast_fusion., ...), custom_call_target="tpu_custom_call" | custom-call | tf_op jit(solution)/shard_map/layer_forward/pallas_call | solution.py:763
  235.0 52.2 %layer_forward.3 = (bf16[128,768]{1,0:T(8,128)(2,1)}, bf16[4,128,192]{2,1,0:T(8,128)(2,1)}, bf16[8,128,384]{2,1,0:T(8,128)(2,1)}, f32[4,128,128]{2,1,0:T(8,128)}...) custom-call(bf16[128,768]{1,0:T(8,128)(2,1)} %get-tuple-element.74.s, ...), custom_call_target="tpu_custom_call" | custom-call | tf_op jit(solution)/shard_map/layer_forward/pallas_call | solution.py:763
  287.2 52.8 %layer_backward.2 = (f32[128,768]{1,0:T(8,128)}, f32[768,128]{1,0:T(8,128)}, bf16[768,128]{1,0:T(8,128)(2,1)}, bf16[768,128]{1,0:T(8,128)(2,1)}, bf16[768,128]{1...) custom-call(bf16[128,768]{1,0:T(8,128)(2,1)} %select_bitcast_fusion., ...), custom_call_target="tpu_custom_call" | custom-call | tf_op jit(solution)/shard_map/layer_backward/pallas_call | solution.py:990
  340.0 1.7 convert_element_type.67.grad
  341.7 54.2 %layer_backward.3 = (f32[128,768]{1,0:T(8,128)}, f32[768,128]{1,0:T(8,128)}, bf16[768,128]{1,0:T(8,128)(2,1)}, bf16[768,128]{1,0:T(8,128)(2,1)}, bf16[768,128]{1...) custom-call(bf16[128,768]{1,0:T(8,128)(2,1)} %convert_element_type.6, ...), custom_call_target="tpu_custom_call" | custom-call | tf_op jit(solution)/shard_map/layer_backward/pallas_call | solution.py:990
  396.2 0.6 collective-permute-start.1
  396.7 0.8 broadcast_select_fusion.1
  397.5 1.0 collective-permute-start.2
  398.6 0.8 maximum_bitcast_fusion.1
  399.4 0.8 select_add_fusion.refs_24_
  400.2 219.8 %weight_grads.1 = (f32[16,7296]{1,0:T(8,128)}, f32[32,768]{1,0:T(8,128)}, f32[96,4096]{1,0:T(8,128)}, f32[256,768]{1,0:T(8,128)}) custom-call(bf16[768,128]{1,0:T(8,128)(2,1)} %get-tuple-element.96.refs_0_, bf16[768,128]{1,0:T(8,128)(2,1)} %get-tuple-element.97.refs_1_, bf16[768,128]{1,0:T(8,128)(2,1)} %get-tuple-element.98.refs_2_, ...), custom_call_target="tpu_custom_call" | custom-call | tf_op jit(solution)/shard_map/weight_grads/pallas_call | solution.py:489
  620.0 1.2 slice_bitcast_fusion
  621.4 0.9 copy.110
  622.2 0.8 copy.107
  623.0 0.7 copy.108
  623.7 0.7 copy.109
  624.3 0.6 copy.106
  625.0 1.3 select_bitcast_fusion.1
  626.2 0.9 maximum_bitcast_fusion
  627.2 0.6 copy.116
  627.8 1.1 copy.117
  629.0 0.9 copy.118
  (56 shorter events, 0.8 us)
Async XLA Ops:
  0.6 167.8 %copy-start.11 = (bf16[2,1,128,768]{3,2,1,0:T(8,128)(2,1)S(1)}, bf16[2,1,128,768]{3,2,1,0:T(8,128)(2,1)}, u32[]{:S(2)}) copy-start(bf16[2,1,128,768]{3,2,1,0:T(8,128)(2,1)} %param.13) | copy-start | bytes 1179652
  0.7 168.5 %copy-start.12 = (bf16[2,1,128,768]{3,2,1,0:T(8,128)(2,1)S(1)}, bf16[2,1,128,768]{3,2,1,0:T(8,128)(2,1)}, u32[]{:S(2)}) copy-start(bf16[2,1,128,768]{3,2,1,0:T(8,128)(2,1)} %param.14) | copy-start | bytes 1179652
  1.8 171.2 %collective-permute-start = (s32[2,128,2]{2,1,0:T(8,128)S(1)}, s32[2,128,2]{2,1,0:T(8,128)S(1)}, u32[]{:S(2)}, u32[]{:S(2)}) collective-permute-start(s32[2,128,2]{2,1,0:T(8,128)S(1)} %select_bitcast_fusion.6), channel_id=1, source_target_pairs={{0,64},{64,0},{1,65},{65,1},{2,66},{66,2},{3,67},{67,3},{4,68},{68... | collective-permute-start | bytes 6152 | tf_op jit(solution)/shard_map/ppermute | solution.py:1049
  8.5 1.1 copy-start.1
  9.6 1.0 copy-start.2
  10.6 0.8 copy-start.3
  167.7 7.3 %copy-start = (bf16[2,768,128]{2,1,0:T(8,128)(2,1)}, bf16[2,768,128]{2,1,0:T(8,128)(2,1)S(1)}, u32[]{:S(2)}) copy-start(bf16[2,768,128]{2,1,0:T(8,128)(2,1)S(1)} %get-tuple-element.68.g_small) | copy-start | bytes 1179652
  341.7 54.3 %copy-start.7 = (f32[768,128]{1,0:T(8,128)S(1)}, f32[768,128]{1,0:T(8,128)}, u32[]{:S(2)}) copy-start(f32[768,128]{1,0:T(8,128)} %get-tuple-element.121) | copy-start | bytes 1179652
  341.7 54.4 %copy-start.5 = (bf16[128,768]{1,0:T(8,128)(2,1)S(1)}, bf16[128,768]{1,0:T(8,128)(2,1)}, u32[]{:S(2)}) copy-start(bf16[128,768]{1,0:T(8,128)(2,1)} %get-tuple-element.74.state) | copy-start | bytes 589828
  341.7 54.4 %copy-start.10 = (bf16[128,768]{1,0:T(8,128)(2,1)S(1)}, bf16[128,768]{1,0:T(8,128)(2,1)}, u32[]{:S(2)}) copy-start(bf16[128,768]{1,0:T(8,128)(2,1)} %get-tuple-element.75) | copy-start | bytes 589828
  341.7 55.0 %copy-start.4 = (f32[128,768]{1,0:T(8,128)S(1)}, f32[128,768]{1,0:T(8,128)}, u32[]{:S(2)}) copy-start(f32[128,768]{1,0:T(8,128)} %get-tuple-element.85) | copy-start | bytes 1179652
  396.0 3.4 copy-start.8
  396.0 3.4 collective-permute-start.3
  396.2 2.4 collective-permute-start.1
  397.5 227.4 %collective-permute-start.2 = (f32[128,768]{1,0:T(8,128)}, f32[128,768]{1,0:T(8,128)}, u32[]{:S(2)}, u32[]{:S(2)}) collective-permute-start(f32[128,768]{1,0:T(8,128)} %broadcast_select_fusion.1), channel_id=1, source_target_pairs={{0,64},{64,0},{1,65},{65,1},{2,66},{66,2},{3,67},{67,3},{4,68},{68... | collective-permute-start | bytes 1179656 | tf_op jit(solution)/shard_map/ppermute | solution.py:1049
  620.0 7.1 %copy-start.13 = (f32[32,768]{1,0:T(8,128)S(1)}, f32[32,768]{1,0:T(8,128)}, u32[]{:S(2)}) copy-start(f32[32,768]{1,0:T(8,128)} %get-tuple-element.123) | copy-start | bytes 294916
  620.0 7.8 %copy-start.6 = (f32[96,4096]{1,0:T(8,128)S(1)}, f32[96,4096]{1,0:T(8,128)}, u32[]{:S(2)}) copy-start(f32[96,4096]{1,0:T(8,128)} %get-tuple-element.124) | copy-start | bytes 4718596
  625.0 4.0 copy-start.9

commit v3 on v2

v3 whole, which is shorter than its diff:
```python
import functools
import math

import jax
import jax.numpy as jnp
from jax import lax
from jax.experimental import pallas as pl
from jax.experimental.pallas import tpu as pltpu
from jax.sharding import PartitionSpec as P

MESH = pl.DeviceIdType.MESH
ANY = pl.BlockSpec(memory_space=pl.ANY)
VMEM = pl.BlockSpec(memory_space=pltpu.VMEM)
DMA = pltpu.SemaphoreType.DMA

D = 768
FF = 2048
WIDE = 3072
SMALL = 128
PACK = WIDE + 2 * FF + SMALL
OWN = 12
HEADS = 12
HEAD_DIM = 64
TOP = 2
CONT = 8
EXPERTS = 8
SEQ = 1024
ROWS = 128
CAP = 40
PAD_CAP = 48
SLOTS = EXPERTS * PAD_CAP
SCALE = 1.0 / math.sqrt(HEAD_DIM)
EPS = 1e-06
NEG = -1e30


def place_ids():
    section = lax.axis_index("section")
    ctx = lax.axis_index("ctx")
    fsdp = lax.axis_index("fsdp")
    return section, ctx // 4, lax.rem(ctx, 4), fsdp // 2, lax.rem(fsdp, 2)


def ctx_of(half, ring):
    return lax.rem(half + 2, 2) * 4 + lax.rem(ring + 4, 4)


def fsdp_of(ring, half):
    return lax.rem(ring + 4, 4) * 2 + lax.rem(half + 2, 2)


def neighbours():
    section, a, z, y, h = place_ids()
    ctx, fsdp = ctx_of(a, z), fsdp_of(y, h)
    return dict(
        core=(1 - section, ctx, fsdp),
        zp=(section, ctx_of(a, z + 1), fsdp),
        zm=(section, ctx_of(a, z - 1), fsdp),
        zx=(section, ctx_of(a + 1, z), fsdp),
        yp=(section, ctx, fsdp_of(y + 1, h)),
        ym=(section, ctx, fsdp_of(y - 1, h)),
        yx=(section, ctx, fsdp_of(y, h + 1)),
    )


def greet(devices):
    barrier = pltpu.get_barrier_semaphore()
    for device in devices:
        pl.semaphore_signal(barrier, inc=1, device_id=device, device_id_type=MESH)
    pl.semaphore_wait(barrier, len(devices))


def rows_at(ref, block, rows, part=None):
    if part is None:
        return ref.at[pl.ds(pl.multiple_of(block * rows, 16), rows)]
    half = rows // 2
    return ref.at[pl.ds(pl.multiple_of(block * rows + part * half, 16), half)]


class Hop:
    def __init__(self, sources, targets, device, send, recv):
        self.copies = [
            pltpu.make_async_remote_copy(s, t, send.at[i], recv.at[i], device_id=device, device_id_type=MESH)
            for i, (s, t) in enumerate(zip(sources, targets))
        ]

    def start(self):
        for copy in self.copies:
            copy.start()
        return self

    def wait_recv(self):
        for copy in self.copies:
            copy.wait_recv()

    def wait_send(self):
        for copy in self.copies:
            copy.wait_send()


class Tree:
    def __init__(self, over_ctx, layer, own, whole, rows, send, recv, c_send, c_recv, l_sem):
        section, a, z, y, h = place_ids()
        near = neighbours()
        self.over_ctx = over_ctx
        ring, pair = ("z", "zx") if over_ctx else ("y", "yx")
        plus, minus, across = near[ring + "p"], near[ring + "m"], near[pair]

        def block(step, side):
            return ctx_of(a + side, z + step) if over_ctx else fsdp_of(y + step, h + side)

        def views(step, side, part=None):
            return [rows_at(w, block(step, side), r, part) for w, r in zip(whole, rows)]

        def hop(index, sources, targets, device):
            return Hop(sources, targets, device, send.at[index], recv.at[index])

        mine = views(0, 0)
        self.hops = [
            hop(0, own, mine, plus),
            hop(1, own, mine, minus),
            hop(2, own, mine, across),
            hop(3, views(-1, 0, 0), views(-1, 0, 0), plus),
            hop(4, views(1, 0, 1), views(1, 0, 1), minus),
            hop(5, views(0, 1), views(0, 1), plus),
            hop(6, views(0, 1), views(0, 1), minus),
        ]
        if over_ctx:
            self.hops.append(hop(7, views(2, 0), views(2, 0), across))
        else:
            self.hops.append(hop(7, views(-1, 1, 0), views(-1, 1, 0), plus))
            self.hops.append(hop(8, views(1, 1, 1), views(1, 1, 1), minus))
        places = [(0, 0), (-1, 0), (1, 0), (0, 1), (2, 0), (-1, 1), (1, 1), (2, 1)]
        self.cores = [
            Hop(own if k == 0 else views(*p), views(*p), near["core"], c_send.at[k], c_recv.at[k]) for k, p in enumerate(places)
        ]
        self.stays = [pltpu.make_async_copy(o, m, l_sem.at[i]) for i, (o, m) in enumerate(zip(own, mine))]

    def start_own(self):
        for index in (0, 1, 2):
            self.hops[index].start()
        self.cores[0].start()
        for copy in self.stays:
            copy.start()

    def forward1(self):
        for index, starts, core in ((0, (3,), 1), (1, (4,), 2), (2, (5, 6), 3)):
            self.hops[index].wait_recv()
            for later in starts:
                self.hops[later].start()
            self.cores[core].start()

    def forward2(self):
        self.hops[3].wait_recv()
        self.hops[4].wait_recv()
        if self.over_ctx:
            self.hops[7].start()
        self.cores[4].start()
        if not self.over_ctx:
            for index, later, core in ((5, 7, 5), (6, 8, 6)):
                self.hops[index].wait_recv()
                self.hops[later].start()
                self.cores[core].start()

    def finish(self):
        if self.over_ctx:
            for index, core in ((5, 5), (6, 6), (7, 7)):
                self.hops[index].wait_recv()
                self.cores[core].start()
        else:
            self.hops[7].wait_recv()
            self.hops[8].wait_recv()
            self.cores[7].start()
        for copy in self.stays:
            copy.wait()

    def receive(self):
        for hop in self.cores:
            hop.wait_recv()

    def drain(self):
        for hop in self.hops + self.cores:
            hop.wait_send()


class Shards:
    def __init__(self, pack, sd, packs, own_sd, send, recv, l_sem):
        section, a, z, y, h = place_ids()
        ctx, fsdp = ctx_of(a, z), fsdp_of(y, h)
        wide = slice(0, WIDE + SMALL)
        rest = slice(WIDE + SMALL, PACK)
        mine = packs.at[pl.ds(pl.multiple_of(fsdp * 16, 16), 16)]
        pieces = [(pack.at[:, wide], mine.at[:, wide]), (pack.at[:, rest], mine.at[:, rest]), (sd, rows_at(own_sd, fsdp, 32))]
        self.hops = [
            [
                Hop([s], [t], device, send.at[k, pl.ds(i, 1)], recv.at[k, pl.ds(i, 1)])
                for k, device in enumerate(fsdp_peers())
            ]
            for i, (s, t) in enumerate(pieces)
        ]
        self.stays = [pltpu.make_async_copy(s, t, l_sem.at[i]) for i, (s, t) in enumerate(pieces)]

    def start(self, pieces):
        for i in pieces:
            for hop in self.hops[i]:
                hop.start()
            self.stays[i].start()

    def wait(self, pieces):
        for i in pieces:
            for hop in self.hops[i]:
                hop.wait_recv()
            self.stays[i].wait()

    def drain(self):
        for hops in self.hops:
            for hop in hops:
                hop.wait_send()


FSDP_STEPS = [(dy, dh) for dy in (1, 3, 2, 0) for dh in (0, 1) if (dy, dh) != (0, 0)]


def fsdp_peers():
    section, a, z, y, h = place_ids()
    ctx = ctx_of(a, z)
    return [(section, ctx, fsdp_of(y + dy, h + dh)) for dy, dh in FSDP_STEPS]


def close_rows(sel, packs, target, start):
    width = target.shape[1]
    step = min(width, 512)

    @pl.loop(0, width // step)
    def _(j):
        off = pl.multiple_of(j * step, 128)
        block = packs[:, pl.ds(pl.multiple_of(start + off, 128), step)]
        target[:, pl.ds(off, step)] = low(dot(sel[...], block))


def close_table(rows_from, rows_to):
    cols, rows = jnp.arange(rows_from), jnp.arange(rows_to)
    return low((rows[:, None] // OWN == cols[None, :] // 16) & (rows[:, None] % OWN == cols[None, :] % 16))


LEFT = (("na", (D, 128)), ("at", (D, 128)), ("nf", (D, 128)), ("sh", (FF, 128)), ("rc", (D, SLOTS)), ("hd", (FF, SLOTS)))
RIGHT = (
    ("qkv", (128, 3 * D)), ("pr", (128, D)), ("gu", (128, 2 * FF)), ("sd", (128, D)), ("j", (SLOTS, 2 * FF)),
    ("er", (EXPERTS, PAD_CAP, D)), ("small", (D, SMALL)),
)
OPERANDS = LEFT + RIGHT
N_OPS = len(OPERANDS)


def operand_type(name):
    return jnp.float32 if name == "small" else jnp.bfloat16


ATTENTION = (("wide", "na", "qkv", 96, 0, 3 * D, D), ("wide", "at", "pr", 96, 3 * D, D, D))
SHARED = (("gu", "nf", "gu", 96, 0, 2 * FF, 1024), ("sd", "sh", "sd", 256, 0, D, D))
EXPERT = (("egu", "rc", "j", 96, 0, 2 * FF, 1024), ("ed", "hd", "er", 256, 0, D, D))


def grads_kernel(*refs):
    lower, upper = refs[:N_OPS], refs[N_OPS : 2 * N_OPS]
    sel_t = refs[2 * N_OPS]
    out_qkv, out_out, out_small, out_gu, out_sd, out_egu, out_ed = refs[2 * N_OPS + 1 : 2 * N_OPS + 8]
    rest = refs[2 * N_OPS + 8 :]
    held = rest[:N_OPS]
    (b_wide, b_gu, b_small, b_sd, c_gu, c_sd, packs, in_pack, in_sd,
     o_local, w_send, w_recv, r_send, r_recv, e_send, e_recv, s_send, s_recv) = rest[N_OPS:]
    names = [n for n, _ in OPERANDS]
    ops = dict(zip(names, held))
    section, a, z, y, h = place_ids()
    ctx, fsdp = ctx_of(a, z), fsdp_of(y, h)
    near = neighbours()

    def bring(source, i, which):
        n, shape = OPERANDS[i]
        if i < len(LEFT):
            target = held[i].at[:, pl.ds(which * shape[1], shape[1])]
        elif n in ("er", "small"):
            target = held[i].at[which]
        else:
            target = held[i].at[pl.ds(which * shape[0], shape[0])]
        return pltpu.make_async_copy(source[i].at[which], target, o_local.at[i, which])

    order = [names.index(n) for n in ("na", "qkv", "at", "pr", "small", "nf", "gu", "sh", "sd", "rc", "j", "hd", "er")]
    for layer, source in enumerate((lower, upper)):

        @pl.when(section == layer)
        def _(source=source):
            for i in order:
                for which in range(2):
                    bring(source, i, which).start()

    greet([near["zp"], near["zm"], near["zx"]] + fsdp_peers())

    def ready(*wanted):
        for n in wanted:
            for which in range(2):
                bring(lower, names.index(n), which).wait()

    kinds = dict(wide=b_wide, gu=b_gu, small=b_small, sd=b_sd, egu=c_gu, ed=c_sd)
    buffers = {
        ATTENTION: ((b_wide, 96), (b_small, 96)),
        SHARED: ((b_gu, 96), (b_sd, 256)),
        EXPERT: ((c_gu, 96), (c_sd, 256)),
    }
    semaphores = {ATTENTION: (w_send, w_recv), SHARED: (r_send, r_recv), EXPERT: (e_send, e_recv)}

    def combine(pieces, block, slot, adds=(), part=None, target=None):
        for kind, left, right, rows, first, width, step in pieces:
            n = rows if part is None else rows // 2
            off = 0 if part is None else part * n
            lhs_rows = pl.ds(pl.multiple_of(block * rows + off, 16), n)

            @pl.loop(0, width // step)
            def _(j, kind=kind, left=left, right=right, first=first, n=n, off=off, lhs_rows=lhs_rows, step=step):
                at = pl.ds(pl.multiple_of(j * step, 256), step)
                to = pl.ds(pl.multiple_of(first + j * step, 256), step)
                if right == "er":
                    right_part = ops[right][:, :, :, at].reshape(2 * SLOTS, step)
                else:
                    right_part = ops[right][:, at]
                total = dot(ops[left][lhs_rows, :], right_part)
                for other in adds:
                    total += kinds[kind][other, off : off + n, to].astype(jnp.float32)
                if target is None:
                    kinds[kind][slot, off : off + n, to] = low(total)
                else:
                    target[kind][off : off + n, to] = total

        if pieces is ATTENTION:
            n = 96 if part is None else 48
            off = 0 if part is None else part * n
            at = pl.ds(pl.multiple_of(block * 96 + off, 16), n)
            total = ops["small"][0, at, :] + ops["small"][1, at, :]
            for other in adds:
                total += b_small[other, off : off + n, :].astype(jnp.float32)
            b_small[slot, off : off + n, :] = low(total)

    hops = {}

    def send(pieces, index, slot, to_slot, device, part=None):
        def views(which):
            return [rows_at(b.at[which], 0, r, part) for b, r in buffers[pieces]]

        sems = semaphores[pieces]
        hops[pieces, index] = Hop(views(slot), views(to_slot), near[device], sems[0].at[index], sems[1].at[index]).start()

    def arrived(pieces, *indices):
        for index in indices:
            hops[pieces, index].wait_recv()

    def sent(pieces, *indices):
        for index in indices:
            hops[pieces, index].wait_send()

    def d_block(dz, da):
        return ctx_of(a + da, z + dz)

    def e_block(dy, dh):
        return fsdp_of(y + dy, h + dh)

    def spread(pieces):
        combine(pieces, d_block(2, 1), 0)
        send(pieces, 0, 0, 1, "zx")
        combine(pieces, d_block(-1, 1), 2)
        send(pieces, 1, 2, 5, "zm")
        combine(pieces, d_block(1, 1), 3)
        send(pieces, 2, 3, 6, "zp")

    def halves(pieces):
        arrived(pieces, 0)
        combine(pieces, d_block(2, 0), 1, (1,))
        send(pieces, 3, 1, 4, "zm", 0)
        send(pieces, 4, 1, 4, "zp", 1)

    def next_ones(pieces):
        sent(pieces, 0)
        combine(pieces, d_block(-1, 0), 0, (), 1)
        arrived(pieces, 3)
        combine(pieces, d_block(-1, 0), 0, (4,), 0)
        send(pieces, 5, 0, 7, "zm")
        sent(pieces, 3, 4)
        combine(pieces, d_block(1, 0), 1, (), 0)
        arrived(pieces, 4)
        combine(pieces, d_block(1, 0), 1, (4,), 1)
        send(pieces, 6, 1, 8, "zp")

    def pair(pieces):
        arrived(pieces, 1, 2)
        combine(pieces, d_block(0, 1), 5, (5, 6))
        send(pieces, 7, 5, 9, "zx")

    def own(pieces):
        arrived(pieces, 5, 6, 7)
        combine(pieces, ctx, 7, (7, 8, 9))

    def open_rows(kind, start, width):
        step = min(width, 1024)

        @pl.loop(0, width // step)
        def _(j):
            off = pl.multiple_of(j * step, 128)
            block = kinds[kind][7, :, pl.ds(off, step)]
            packs[:, pl.ds(pl.multiple_of(start + off, 128), step)] = low(dot(sel_t[...], block))

    last = [[], [], []]
    split_at = WIDE + SMALL

    def to_owners(which):
        for k, device in enumerate(fsdp_peers()):
            dy, dh = FSDP_STEPS[k]
            block = e_block(dy, dh)
            rows = packs.at[pl.ds(pl.multiple_of(block * 16, 16), 16)]
            source, target = (
                (rows.at[:, :split_at], in_pack.at[k, :, :split_at]),
                (rows.at[:, split_at:], in_pack.at[k, :, split_at:]),
                (rows_at(b_sd.at[7], block, 32), in_sd.at[k]),
            )[which]
            last[which].append(
                Hop([source], [target], device, s_send.at[k, pl.ds(which, 1)], s_recv.at[k, pl.ds(which, 1)]).start()
            )

    def total_of(which, start, width, out):
        step = min(width, 256)

        @pl.loop(0, width // step)
        def _(j):
            at = pl.ds(pl.multiple_of(start + j * step, 128), step)
            total = packs[pl.ds(pl.multiple_of(fsdp * 16, 16), 16), at].astype(jnp.float32)
            for k in range(7):
                total += in_pack[k, :, at].astype(jnp.float32)
            out[:, pl.ds(pl.multiple_of(j * step, 128), step)] = total[:OWN]

    ready("na", "qkv", "at", "pr", "small")
    spread(ATTENTION)
    ready("nf", "gu", "sh", "sd")
    spread(SHARED)
    ready("rc", "j", "hd", "er")
    combine(EXPERT, e_block(2, 1), 0)
    send(EXPERT, 0, 0, 4, "ym", 0)
    send(EXPERT, 1, 0, 4, "yp", 1)
    halves(ATTENTION)
    combine(EXPERT, e_block(2, 0), 1)
    send(EXPERT, 2, 1, 5, "ym", 0)
    send(EXPERT, 3, 1, 5, "yp", 1)
    combine(EXPERT, e_block(-1, 1), 2, (), 1)
    combine(EXPERT, e_block(1, 1), 3, (), 0)
    arrived(EXPERT, 0)
    combine(EXPERT, e_block(-1, 1), 2, (4,), 0)
    send(EXPERT, 4, 2, 6, "ym")
    arrived(EXPERT, 1)
    combine(EXPERT, e_block(1, 1), 3, (4,), 1)
    send(EXPERT, 5, 3, 7, "yp")
    pair(ATTENTION)
    halves(SHARED)
    next_ones(ATTENTION)
    pair(SHARED)
    sent(EXPERT, 0, 1)
    combine(EXPERT, e_block(-1, 0), 0, (), 1)
    arrived(EXPERT, 2)
    combine(EXPERT, e_block(-1, 0), 0, (5,), 0)
    send(EXPERT, 6, 0, 8, "ym")
    sent(EXPERT, 2, 3)
    combine(EXPERT, e_block(1, 0), 1, (), 0)
    arrived(EXPERT, 3)
    combine(EXPERT, e_block(1, 0), 1, (5,), 1)
    send(EXPERT, 7, 1, 9, "yp")
    next_ones(SHARED)
    arrived(EXPERT, 4, 5)
    combine(EXPERT, e_block(0, 1), 6, (6, 7))
    send(EXPERT, 8, 6, 10, "yx")
    own(ATTENTION)
    open_rows("wide", 0, WIDE)
    open_rows("small", WIDE, SMALL)
    to_owners(0)
    own(SHARED)
    open_rows("gu", split_at, 2 * FF)
    to_owners(1)
    to_owners(2)
    for hop in last[0]:
        hop.wait_recv()
    total_of(0, 0, 3 * D, out_qkv)
    total_of(0, 3 * D, D, out_out)
    total_of(0, WIDE, SMALL, out_small)
    arrived(EXPERT, 6, 7, 8)
    combine(EXPERT, fsdp, 0, (8, 9, 10), None, dict(egu=out_egu, ed=out_ed))
    for hop in last[1] + last[2]:
        hop.wait_recv()
    total_of(1, split_at, 2 * FF, out_gu)
    total = b_sd[7, pl.ds(pl.multiple_of(fsdp * 32, 16), 32), :].astype(jnp.float32)
    for k in range(7):
        total += in_sd[k].astype(jnp.float32)
    out_sd[...] = total
    for pieces in (ATTENTION, SHARED):
        sent(pieces, 1, 2, 5, 6, 7)
    sent(EXPERT, 4, 5, 6, 7, 8)
    for hop in last[0] + last[1] + last[2]:
        hop.wait_send()


def weight_grads(lower, upper):
    bf, f32 = jnp.bfloat16, jnp.float32
    held = [pltpu.VMEM((shape[0], 2 * shape[1]), bf) for _, shape in LEFT]
    for name, shape in RIGHT:
        whole = (2,) + shape if name in ("er", "small") else (2 * shape[0], shape[1])
        held.append(pltpu.VMEM(whole, operand_type(name)))
    shapes = [(OWN, 3 * D), (OWN, D), (OWN, SMALL), (OWN, 2 * FF), (32, D), (96, 2 * FF), (256, D)]
    return pl.pallas_call(
        grads_kernel,
        out_shape=[jax.ShapeDtypeStruct(shape, f32) for shape in shapes],
        in_specs=[ANY] * (2 * N_OPS) + [VMEM],
        out_specs=[VMEM] * len(shapes),
        scratch_shapes=held + [
            pltpu.VMEM((10, 96, WIDE), bf),
            pltpu.VMEM((10, 96, 2 * FF), bf),
            pltpu.VMEM((10, 96, SMALL), bf),
            pltpu.VMEM((10, 256, D), bf),
            pltpu.VMEM((11, 96, 2 * FF), bf),
            pltpu.VMEM((11, 256, D), bf),
            pltpu.VMEM((128, PACK), bf),
            pltpu.VMEM((7, 16, PACK), bf),
            pltpu.VMEM((7, 32, D), bf),
            DMA((N_OPS, 2)),
            DMA((8, 2)), DMA((8, 2)), DMA((8, 2)), DMA((8, 2)),
            DMA((9, 2)), DMA((9, 2)),
            DMA((7, 3)), DMA((7, 3)),
        ],
        compiler_params=pltpu.CompilerParams(collective_id=5, has_side_effects=True, vmem_limit_bytes=62 << 20),
        name="weight_grads",
    )(*lower, *upper, close_table(128, 96).T)


def split(values):
    high = low(values)
    return high, low(values - high.astype(jnp.float32))


def rms_parts(values):
    scale = lax.rsqrt(jnp.mean(values * values, axis=-1, keepdims=True) + EPS)
    return scale, values * scale


def rms_back(grad, gain, scale, unit):
    inner = grad * gain
    grad_values = scale * (inner - unit * jnp.mean(inner * unit, axis=-1, keepdims=True))
    return grad_values, jnp.sum(grad * unit, axis=0, keepdims=True)


def dot(left, right):
    return jnp.dot(left, right, preferred_element_type=jnp.float32)


def dot_t(left, right):
    return lax.dot_general(left, right, (((1,), (1,)), ((), ())), preferred_element_type=jnp.float32)


def t_dot(left, right):
    return lax.dot_general(left, right, (((0,), (0,)), ((), ())), preferred_element_type=jnp.float32)


def low(values):
    return values.astype(jnp.bfloat16)


def rotate(values, cosine, sine):
    half = HEAD_DIM // 2
    lower = lax.broadcasted_iota(jnp.int32, (values.shape[0], 128), 1) % HEAD_DIM < half
    parts = []
    for start in range(0, values.shape[1], 128):
        span = slice(start, start + 128)
        part = values[:, span]
        other = jnp.where(lower, pltpu.roll(part, 128 - half, 1), pltpu.roll(part, half, 1))
        parts.append(part * cosine[:, span] + other * sine[:, span])
    return jnp.concatenate(parts, axis=1)


def visible_keys(qidx, qlab, klab):
    kidx = lax.broadcasted_iota(jnp.int32, (qidx.shape[0], klab.shape[1]), 1)
    return (kidx <= qidx) & ((klab == 0) | (klab == qlab))


def pair_gates(logits, route):
    lane = lax.broadcasted_iota(jnp.int32, logits.shape, 1)
    picks = [lane == route[:, c : c + 1] + 2 for c in range(TOP)]
    first, second = [jnp.sum(jnp.where(p, logits, 0.0), axis=1, keepdims=True) for p in picks]
    top = jnp.maximum(first, second)
    first, second = jnp.exp(first - top), jnp.exp(second - top)
    total = first + second
    return picks, [first / total, second / total]


class Exchange:
    def __init__(self, source, target, send, recv, everyone, block_of=None):
        section, a, z, y, h = place_ids()
        fsdp = fsdp_of(y, h)
        offsets = [(1, 0), (1, 1), (1, 3), (1, 2)] if everyone else []
        self.copies = []
        for k, (da, dz) in enumerate(offsets + [(0, 1), (0, 3), (0, 2)]):
            c, zz = ctx_of(a + da, z + dz), lax.rem(z + dz, 4)
            block = zz if block_of == "ring" or not everyone else c
            to = ctx_of(a, z) if everyone else z
            self.copies.append(
                pltpu.make_async_remote_copy(
                    source.at[block], target.at[to], send.at[k], recv.at[k], device_id=(section, c, fsdp), device_id_type=MESH
                )
            )

    def start(self):
        for copy in self.copies:
            copy.start()

    def wait_recv(self):
        for copy in self.copies:
            copy.wait_recv()

    def wait_send(self):
        for copy in self.copies:
            copy.wait_send()


def ctx_peers():
    section, a, z, y, h = place_ids()
    fsdp = fsdp_of(y, h)
    return [(section, ctx_of(a + da, z + dz), fsdp) for da in range(2) for dz in range(4) if (da, dz) != (0, 0)]


def forward_kernel(
    pack, g_sd, g_egu, g_ed, sel,
    state, cosine, sine, qidx, qlab, klab, route, first_table, second_table, taken_t,
    out_lower, out_upper,
    l_wide, l_gu, l_small, l_sd, l_egu, l_ed, u_wide, u_gu, u_small, u_sd, u_egu, u_ed,
    *rest,
):
    kept = (rest[:9], rest[9:18])
    (wide, gu, small, sd, egu, ed, w_sem,
     packs, own_wide, own_small, own_gu, own_sd, g_stay, sh_send, sh_recv,
     w_send, w_recv, r_send, r_recv, e_send, e_recv, wc_send, wc_recv, rc_send, rc_recv, ec_send, ec_recv,
     kv_pack, q_pack, kv_all, q_all, o_pack, o_in, lse, att, res, sj, sh, sent, rc, ej, eh, result, ret, k_sem,
     x_send, x_recv) = rest[18:]
    section, a, z, y, h = place_ids()
    ctx = ctx_of(a, z)
    wholes = ((l_wide, l_gu, l_small, l_sd, l_egu, l_ed), (u_wide, u_gu, u_small, u_sd, u_egu, u_ed))
    greet([neighbours()["core"]] + ctx_peers() + fsdp_peers())

    shards = Shards(pack, g_sd, packs, own_sd, sh_send, sh_recv, g_stay.at[0])
    trees = []
    for layer in range(2):
        t_wide, t_gu, t_small, t_sd, t_egu, t_ed = wholes[layer]
        trees.append(
            dict(
                w=Tree(True, layer, [own_wide, own_small], [t_wide, t_small], (96, 96),
                       w_send, w_recv, wc_send.at[layer], wc_recv.at[layer], g_stay.at[1]),
                r=Tree(True, layer, [own_gu, own_sd], [t_gu, t_sd], (96, 256),
                       r_send, r_recv, rc_send.at[layer], rc_recv.at[layer], g_stay.at[2]),
                e=Tree(False, layer, [g_egu, g_ed], [t_egu, t_ed], (96, 256),
                       e_send, e_recv, ec_send.at[layer], ec_recv.at[layer], g_stay.at[3]),
            )
        )

    def drive(layer, *steps):
        @pl.when(section == layer)
        def _():
            for step in steps:
                step()

    def close_wide():
        shards.wait((0,))
        close_rows(sel, packs, own_wide, 0)
        close_rows(sel, packs, own_small, WIDE)

    def close_rest():
        shards.wait((1, 2))
        close_rows(sel, packs, own_gu, WIDE + SMALL)

    def arrived(layer, group):
        drive(layer, trees[layer][group].finish)

        @pl.when(section != layer)
        def _():
            trees[layer][group].receive()

    def load(layer, *which):
        for i in which:
            target = (wide.at[layer], gu, small.at[layer], sd, egu, ed)[i]
            pltpu.make_async_copy(wholes[layer][i], target, w_sem.at[layer, i]).start()

    def loaded(layer, *which):
        for i in which:
            target = (wide.at[layer], gu, small.at[layer], sd, egu, ed)[i]
            pltpu.make_async_copy(wholes[layer][i], target, w_sem.at[layer, i]).wait()

    lower, upper = trees
    hooks = {
        (0, "start"): lambda: (
            drive(0, lambda: shards.start((0,)), close_wide, lambda: shards.start((1, 2)), lower["w"].start_own, close_rest,
                  lower["w"].forward1, lower["e"].start_own, lower["w"].forward2, lower["r"].start_own),
            arrived(0, "w"), load(0, 0, 2),
        ),
        (0, "keys"): lambda: (drive(0, lower["e"].forward1), drive(1, lambda: shards.start((0, 1, 2)))),
        (0, "queries"): lambda: drive(0, lower["r"].forward1),
        (0, "block1"): lambda: drive(0, lower["e"].forward2),
        (0, "block2"): lambda: drive(1, close_wide, upper["w"].start_own),
        (0, "attended"): lambda: (drive(0, lower["r"].forward2), drive(1, close_rest)),
        (0, "sent"): lambda: (arrived(0, "r"), load(0, 1, 3)),
        (0, "shared0"): lambda: (drive(1, upper["w"].forward1, upper["e"].start_own),),
        (0, "shared"): lambda: (arrived(0, "e"), load(0, 4, 5)),
        (0, "expert1"): lambda: drive(1, upper["r"].start_own),
        (0, "expert2"): lambda: drive(1, upper["w"].forward2),
        (0, "expert3"): lambda: drive(1, upper["e"].forward1),
        (0, "returned"): lambda: drive(1, upper["r"].forward1),
        (1, "start"): lambda: (arrived(1, "w"), load(1, 0, 2)),
        (1, "keys"): lambda: drive(1, upper["e"].forward2),
        (1, "block0"): lambda: drive(1, upper["r"].forward2),
        (1, "sent"): lambda: (arrived(1, "r"), load(1, 1, 3)),
        (1, "shared"): lambda: (arrived(1, "e"), load(1, 4, 5)),
    }

    def one_layer(layer, x, out):
        def hook(name):
            if (layer, name) in hooks:
                hooks[layer, name]()

        k_q, k_kv, k_lse, k_att, k_res, k_sj, k_rc, k_ej, k_ret = kept[layer]
        saves = []

        def save(source, target):
            copy = pltpu.make_async_copy(source, target, k_sem.at[len(saves)])
            copy.start()
            saves.append(copy)

        def exchange(index, source, target, everyone, block_of=None):
            sems = x_send.at[layer, index], x_recv.at[layer, index]
            return Exchange(source, target, *sems, everyone, block_of)

        scale, unit = rms_parts(x)
        hook("start")
        loaded(layer, 0, 2)
        wide_l, small_l = wide.at[layer], small.at[layer]
        gains = jnp.transpose(small_l[...].astype(jnp.float32))
        normed = low(unit * gains[0:1, :])
        keys = low(rotate(dot(normed, wide_l[:, D : 2 * D]), cosine[...], sine[...]))
        values = low(dot(normed, wide_l[:, 2 * D : 3 * D]))
        for g in range(4):
            kv_pack[g, :, 0:192] = keys[:, 192 * g : 192 * g + 192]
            kv_pack[g, :, 192:384] = values[:, 192 * g : 192 * g + 192]
        ex_kv = exchange(0, kv_pack, kv_all, True, "ring")
        ex_kv.start()
        hook("keys")
        queries = low(rotate(dot(normed, wide_l[:, 0:D]), cosine[...], sine[...]))
        for g in range(4):
            q_pack[g] = queries[:, 192 * g : 192 * g + 192]
        ex_q = exchange(1, q_pack, q_all, False)
        ex_q.start()
        kv_all[ctx] = kv_pack[z]
        q_all[z] = q_pack[z]
        hook("queries")
        ex_q.wait_recv()
        ex_kv.wait_recv()
        save(kv_all, k_kv)
        save(q_all, k_q)

        def attend(d):
            block = lax.rem(z + d + 1, 4)
            seen = visible_keys(qidx[block], qlab[block], klab[...])
            for head in range(3):
                span = slice(64 * head, 64 * head + 64)
                vspan = slice(192 + 64 * head, 256 + 64 * head)
                k = kv_all[:, :, span].reshape(SEQ, HEAD_DIM)
                v = kv_all[:, :, vspan].reshape(SEQ, HEAD_DIM)
                scores = jnp.where(seen, dot_t(q_all[block, :, span], k) * SCALE, NEG)
                top = jnp.max(scores, axis=-1, keepdims=True)
                weights = jnp.exp(scores - top)
                total = jnp.sum(weights, axis=-1, keepdims=True)
                o_pack[block, :, span] = low(dot(low(weights / total), v))
                lse[block, :, head : head + 1] = top + jnp.log(total)

        for d in range(4):
            pl.loop(d, d + 1)(attend)
            hook(f"block{d}")

        ex_o = exchange(2, o_pack, o_in, False)
        ex_o.start()
        save(lse, k_lse)
        o_in[z] = o_pack[z]
        hook("attended")
        ex_o.wait_recv()
        for g in range(4):
            att[:, 192 * g : 192 * g + 192] = o_in[g]
        save(att, k_att)
        res[...] = x + dot(att[...], wide_l[:, 3 * D :])
        save(res, k_res)
        scale, unit = rms_parts(res[...])
        normed = low(unit * gains[1:2, :])
        sent[...] = low(dot(taken_t[layer], normed)).reshape(EXPERTS, PAD_CAP, D)
        ex_s = exchange(3, sent, rc, True)
        ex_s.start()
        rc[ctx] = sent[ctx]
        _, gates = pair_gates(dot(normed, small_l[...]), route[layer])
        mix = first_table[layer].astype(jnp.float32) * gates[0] + second_table[layer].astype(jnp.float32) * gates[1]
        hook("sent")
        loaded(layer, 1)

        def shared_part(j):
            at = pl.ds(pl.multiple_of(j * 256, 256), 256)
            up_at = pl.ds(pl.multiple_of(FF + j * 256, 256), 256)
            gate, up = dot(normed, gu[:, at]), dot(normed, gu[:, up_at])
            sj[:, at] = gate
            sj[:, up_at] = up
            sh[:, at] = low(gate * jax.nn.sigmoid(gate) * up)

        for d in range(2):
            pl.loop(4 * d, 4 * d + 4)(shared_part)
            hook(f"shared{d}")

        save(sj, k_sj)
        hook("shared")
        loaded(layer, 3)
        shared_out = dot(sh[...], sd[...])
        ex_s.wait_recv()
        save(rc, k_rc)
        loaded(layer, 4)

        def expert_part(j):
            at = pl.ds(pl.multiple_of(j * 256, 256), 256)
            up_at = pl.ds(pl.multiple_of(FF + j * 256, 256), 256)
            gate, up = dot(rc[...].reshape(SLOTS, D), egu[:, at]), dot(rc[...].reshape(SLOTS, D), egu[:, up_at])
            ej[:, at] = gate
            ej[:, up_at] = up
            eh[:, at] = low(gate * jax.nn.sigmoid(gate) * up)

        for d in range(4):
            pl.loop(2 * d, 2 * d + 2)(expert_part)
            hook(f"expert{d}")

        save(ej, k_ej)
        loaded(layer, 5)
        for j in range(D // 256):
            span = slice(256 * j, 256 * j + 256)
            result[:, :, span] = low(dot(eh[...], ed[:, span])).reshape(EXPERTS, PAD_CAP, 256)
        ex_r = exchange(4, result, ret, True)
        for copy in saves[:2]:
            copy.wait()
        ex_r.start()
        ret[ctx] = result[ctx]
        hook("returned")
        ex_r.wait_recv()
        save(ret, k_ret)
        high, rest_of = split(mix)
        returned = ret[...].reshape(SLOTS, D)
        mixed = dot(high, returned) + dot(rest_of, returned)
        out[...] = low(res[...] + shared_out + mixed)
        for ex in (ex_kv, ex_q, ex_o, ex_s, ex_r):
            ex.wait_send()
        for copy in saves[2:]:
            copy.wait()

    one_layer(0, state[...].astype(jnp.float32), out_lower)
    one_layer(1, out_lower[...].astype(jnp.float32), out_upper)
    for layer in range(2):
        drive(layer, shards.drain, *[tree.drain for tree in trees[layer].values()])


def weight_scratch():
    bf = jnp.bfloat16
    return [
        pltpu.VMEM((D, WIDE), bf), pltpu.VMEM((D, 2 * FF), bf), pltpu.VMEM((D, SMALL), bf),
        pltpu.VMEM((FF, D), bf), pltpu.VMEM((D, 2 * FF), bf), pltpu.VMEM((FF, D), bf), DMA((6,)),
    ]


KEPT = (
    ((4, ROWS, 192), jnp.bfloat16), ((8, ROWS, 384), jnp.bfloat16), ((4, ROWS, 128), jnp.float32), ((ROWS, D), jnp.bfloat16),
    ((ROWS, D), jnp.float32), ((ROWS, 2 * FF), jnp.float32), ((EXPERTS, PAD_CAP, D), jnp.bfloat16),
    ((SLOTS, 2 * FF), jnp.float32), ((EXPERTS, PAD_CAP, D), jnp.bfloat16),
)


WEIGHTS = ((D, WIDE), (D, 2 * FF), (D, SMALL), (FF, D), (D, 2 * FF), (FF, D))


def forward(pack, sd, egu, ed, state, geometry, plans):
    bf, f32 = jnp.bfloat16, jnp.float32
    slots = pltpu.VMEM((EXPERTS, PAD_CAP, D), bf)
    tables = [jnp.stack(pair) for pair in zip(*plans)]
    outs = pl.pallas_call(
        forward_kernel,
        out_shape=[jax.ShapeDtypeStruct((ROWS, D), bf)] * 2
        + [jax.ShapeDtypeStruct(s, bf) for s in WEIGHTS] * 2
        + [jax.ShapeDtypeStruct(s, t) for s, t in KEPT] * 2,
        in_specs=[ANY] * 4 + [VMEM] * 11,
        out_specs=[VMEM] * 2 + [ANY] * (2 * len(WEIGHTS) + 2 * len(KEPT)),
        scratch_shapes=[
            pltpu.VMEM((2, D, WIDE), bf), pltpu.VMEM((D, 2 * FF), bf), pltpu.VMEM((2, D, SMALL), bf),
            pltpu.VMEM((FF, D), bf), pltpu.VMEM((D, 2 * FF), bf), pltpu.VMEM((FF, D), bf), DMA((2, 6)),
            pltpu.VMEM((128, PACK), bf), pltpu.VMEM((96, WIDE), bf), pltpu.VMEM((96, SMALL), bf),
            pltpu.VMEM((96, 2 * FF), bf), pltpu.VMEM((256, D), bf), DMA((4, 3)), DMA((7, 3)), DMA((7, 3)),
            DMA((8, 2)), DMA((8, 2)), DMA((8, 2)), DMA((8, 2)), DMA((9, 2)), DMA((9, 2)),
        ]
        + [DMA((2, 8, 2))] * 6
        + [
            pltpu.VMEM((4, ROWS, 384), bf), pltpu.VMEM((4, ROWS, 192), bf),
            pltpu.VMEM((8, ROWS, 384), bf), pltpu.VMEM((4, ROWS, 192), bf),
            pltpu.VMEM((4, ROWS, 192), bf), pltpu.VMEM((4, ROWS, 192), bf),
            pltpu.VMEM((4, ROWS, 128), f32), pltpu.VMEM((ROWS, D), bf), pltpu.VMEM((ROWS, D), f32),
            pltpu.VMEM((ROWS, 2 * FF), f32), pltpu.VMEM((ROWS, FF), bf),
            slots, slots, pltpu.VMEM((SLOTS, 2 * FF), f32), pltpu.VMEM((SLOTS, FF), bf), slots, slots, DMA((len(KEPT),)),
            DMA((2, 5, 7)), DMA((2, 5, 7)),
        ],
        compiler_params=pltpu.CompilerParams(collective_id=1, has_side_effects=True, vmem_limit_bytes=60 << 20),
        name="forward",
    )(pack, sd, egu, ed, close_table(128, 96), state, *geometry, *tables)
    weights, kept = outs[2 : 2 + 2 * len(WEIGHTS)], outs[2 + 2 * len(WEIGHTS) :]
    return outs[:2], (weights[: len(WEIGHTS)], weights[len(WEIGHTS) :]), (kept[: len(KEPT)], kept[len(KEPT) :])


def backward_kernel(
    layer,
    grad, state, cosine, sine, qidx, qlab, klab, route, first_table, second_table, taken, small_t,
    g_wide, g_gu, g_small, g_sd, g_egu, g_ed,
    k_q, k_kv, k_lse, k_att, k_res, k_sj, k_rc, k_ej, k_ret,
    out, out_both,
    p_na, p_at, p_nf, p_sh, p_rc, p_hd, p_qkv, p_pr, p_gu, p_sd, p_j, p_er, p_small,
    wide, gu, small, sd, egu, ed, w_sem,
    q_all, kv_all, lse, att, res, sj, rc, ej, ret, i_sem,
    t_na, t_at, t_nf, t_sh, t_rc, t_hd, m_qkv, m_pr, m_gu, m_sd, m_j, grad_small, p_sem, p_send, p_recv,
    sent, er, back, slots, o_pack, o_in, dq_pack, dq_in, dkv_pack, dkv_in, dkv_sum, normed_grad, sh, eh,
    s_send, s_recv, r_send, r_recv, o_send, o_recv, q_send, q_recv, kv_send, kv_recv,
):
    section, a, z, y, h = place_ids()
    ctx = ctx_of(a, z)
    loads = [
        pltpu.make_async_copy(s, t, w_sem.at[i])
        for i, (s, t) in enumerate(((g_wide, wide), (g_gu, gu), (g_small, small), (g_sd, sd), (g_egu, egu), (g_ed, ed)))
    ]
    reads = [
        pltpu.make_async_copy(s, t, i_sem.at[i])
        for i, (s, t) in enumerate(zip((k_q, k_kv, k_lse, k_att, k_res, k_sj, k_rc, k_ej, k_ret), (q_all, kv_all, lse, att, res, sj, rc, ej, ret)))
    ]
    loads[2].start()
    reads[4].start()
    loads[3].start()
    reads[5].start()
    loads[1].start()
    reads[8].start()
    loads[5].start()
    reads[7].start()
    loads[4].start()
    for i in (6, 3, 0, 1, 2):
        reads[i].start()
    loads[0].start()
    near = neighbours()
    greet([near["core"]] + ctx_peers())
    saves = []

    def save(source, target):
        i = len(saves)
        here = pltpu.make_async_copy(source, target.at[0], p_sem.at[i])
        away = pltpu.make_async_remote_copy(
            source, target.at[1], p_send.at[i], p_recv.at[i], device_id=near["core"], device_id_type=MESH
        )
        saves.append((here, away))

        @pl.when(section == layer)
        def _():
            here.start()

        @pl.when(section != layer)
        def _():
            away.start()

    grad_out = grad[...].astype(jnp.float32)
    m_sd[...] = low(grad_out)
    save(m_sd, p_sd)
    loads[2].wait()
    reads[4].wait()
    scale_ffn, unit_ffn = rms_parts(res[...])
    normed = low(unit_ffn * small_t[1:2, :])
    picks, gates = pair_gates(dot(normed, small[...]), route[...])
    first, second = first_table[...].astype(jnp.float32), second_table[...].astype(jnp.float32)
    mix_high, mix_rest = split(first * gates[0] + second * gates[1])
    out_high, out_rest = split(grad_out)
    slot_grads = t_dot(mix_high, out_high) + t_dot(mix_rest, out_high) + t_dot(mix_high, out_rest)
    sent[...] = low(slot_grads).reshape(EXPERTS, PAD_CAP, D)
    ex_s = Exchange(sent, er, s_send, s_recv, True)
    ex_s.start()
    er[ctx] = sent[ctx]

    loads[3].wait()
    reads[5].wait()

    @pl.loop(0, FF // 256)
    def _(j):
        at = pl.ds(pl.multiple_of(j * 256, 256), 256)
        up_at = pl.ds(pl.multiple_of(FF + j * 256, 256), 256)
        hidden_grad = dot_t(m_sd[...], sd[at, :])
        gate, up = sj[:, at], sj[:, up_at]
        sig = jax.nn.sigmoid(gate)
        m_gu[:, at] = low(hidden_grad * up * sig * (1.0 + gate * (1.0 - sig)))
        m_gu[:, up_at] = low(hidden_grad * gate * sig)
        sh[:, at] = low(gate * sig * up)
        t_sh[at, :] = low(jnp.transpose(gate * sig * up))

    save(m_gu, p_gu)
    save(t_sh, p_sh)
    t_nf[...] = low(jnp.transpose(unit_ffn * small_t[1:2, :]))
    save(t_nf, p_nf)
    loads[1].wait()

    @pl.loop(0, D // 256)
    def _(j):
        at = pl.ds(pl.multiple_of(j * 256, 256), 256)
        normed_grad[:, at] = dot_t(m_gu[...], gu[at, :])

    reads[8].wait()
    products = dot_t(m_sd[...], ret[...].reshape(SLOTS, D))
    gate_grads = [jnp.sum(products * first, axis=1, keepdims=True), jnp.sum(products * second, axis=1, keepdims=True)]
    inner = gates[0] * gate_grads[0] + gates[1] * gate_grads[1]
    chosen = [g * (d - inner) for g, d in zip(gates, gate_grads)]
    logit_grads = jnp.where(picks[0], chosen[0], 0.0) + jnp.where(picks[1], chosen[1], 0.0)
    logit_high, logit_rest = split(logit_grads)
    grad_small[...] = t_dot(normed, logit_high) + t_dot(normed, logit_rest)
    normed_grad[...] += dot_t(logit_high, small[...]) + dot_t(logit_rest, small[...])

    loads[5].wait()
    reads[7].wait()
    ex_s.wait_recv()
    save(er, p_er)

    @pl.loop(0, FF // 256)
    def _(j):
        at = pl.ds(pl.multiple_of(j * 256, 256), 256)
        up_at = pl.ds(pl.multiple_of(FF + j * 256, 256), 256)
        hidden_grad = dot_t(er[...].reshape(SLOTS, D), ed[at, :])
        gate, up = ej[:, at], ej[:, up_at]
        sig = jax.nn.sigmoid(gate)
        m_j[:, at] = low(hidden_grad * up * sig * (1.0 + gate * (1.0 - sig)))
        m_j[:, up_at] = low(hidden_grad * gate * sig)
        eh[:, at] = low(gate * sig * up)

    save(m_j, p_j)
    loads[4].wait()

    @pl.loop(0, D // 256)
    def _(j):
        at = pl.ds(pl.multiple_of(j * 256, 256), 256)
        back[:, :, at] = low(dot_t(m_j[...], egu[at, :])).reshape(EXPERTS, PAD_CAP, 256)

    ex_r = Exchange(back, slots, r_send, r_recv, True)
    ex_r.start()
    slots[ctx] = back[ctx]
    reads[6].wait()
    t_hd[...] = jnp.transpose(eh[...])
    save(t_hd, p_hd)
    t_rc[...] = jnp.transpose(rc[...].reshape(SLOTS, D))
    save(t_rc, p_rc)
    reads[3].wait()
    t_at[...] = jnp.transpose(att[...])
    save(t_at, p_at)
    loads[0].wait()
    ex_r.wait_recv()
    grad_normed = normed_grad[...] + dot(taken[...], slots[...].reshape(SLOTS, D))
    grad_values, gain_ffn = rms_back(grad_normed, small_t[1:2, :], scale_ffn, unit_ffn)
    grad_res = grad_out + grad_values
    m_pr[...] = low(grad_res)
    save(m_pr, p_pr)
    grad_att = low(dot_t(m_pr[...], wide[:, 3 * D :]))
    for g in range(4):
        o_pack[g] = grad_att[:, 192 * g : 192 * g + 192]
    ex_o = Exchange(o_pack, o_in, o_send, o_recv, False)
    ex_o.start()
    o_in[z] = o_pack[z]
    scale_attn, unit_attn = rms_parts(state[...].astype(jnp.float32))
    t_na[...] = low(jnp.transpose(unit_attn * small_t[0:1, :]))
    save(t_na, p_na)
    dkv_sum[...] = jnp.zeros_like(dkv_sum)
    for i in (0, 1, 2):
        reads[i].wait()
    ex_o.wait_recv()

    @pl.loop(0, 4)
    def _(d):
        block = lax.rem(z + d + 1, 4)
        seen = visible_keys(qidx[block], qlab[block], klab[...])
        for head in range(3):
            span = slice(64 * head, 64 * head + 64)
            vspan = slice(192 + 64 * head, 256 + 64 * head)
            q, do = q_all[block, :, span], o_in[block, :, span]
            k = kv_all[:, :, span].reshape(SEQ, HEAD_DIM)
            v = kv_all[:, :, vspan].reshape(SEQ, HEAD_DIM)
            scores = dot_t(q, k) * SCALE
            probs = jnp.where(seen, jnp.exp(scores - lse[block, :, head : head + 1]), 0.0)
            dprobs = dot_t(do, v)
            delta = jnp.sum(probs * dprobs, axis=-1, keepdims=True)
            dscores = low(probs * (dprobs - delta))
            dq_pack[block, :, span] = low(dot(dscores, k) * SCALE)
            dkv_sum[:, span] += t_dot(dscores, q) * SCALE
            dkv_sum[:, vspan] += t_dot(low(probs), do)

    ex_q = Exchange(dq_pack, dq_in, q_send, q_recv, False)
    ex_q.start()
    dkv_pack[...] = low(dkv_sum[...]).reshape(8, ROWS, 384)
    ex_kv = Exchange(dkv_pack, dkv_in, kv_send, kv_recv, True)
    ex_kv.start()
    dq_in[z] = dq_pack[z]
    dkv_in[ctx] = dkv_pack[ctx]
    ex_q.wait_recv()
    ex_kv.wait_recv()
    dq = jnp.concatenate([dq_in[g].astype(jnp.float32) for g in range(4)], axis=1)
    both = [dkv_in[g].astype(jnp.float32) + dkv_in[4 + g].astype(jnp.float32) for g in range(4)]
    dk = jnp.concatenate([v[:, :192] for v in both], axis=1)
    dv = jnp.concatenate([v[:, 192:] for v in both], axis=1)
    m_qkv[:, 0:D] = low(rotate(dq, cosine[...], -sine[...]))
    m_qkv[:, D : 2 * D] = low(rotate(dk, cosine[...], -sine[...]))
    m_qkv[:, 2 * D :] = low(dv)
    save(m_qkv, p_qkv)
    grad_normed = dot_t(m_qkv[...], wide[:, 0 : 3 * D])
    grad_values, gain_attn = rms_back(grad_normed, small_t[0:1, :], scale_attn, unit_attn)
    out[...] = grad_res + grad_values
    lane = lax.broadcasted_iota(jnp.int32, (D, SMALL), 1)
    gains_t = jnp.transpose(jnp.concatenate([gain_attn, gain_ffn, jnp.zeros((SMALL - 2, D), jnp.float32)], axis=0))
    grad_small[...] = jnp.where(lane < 2, gains_t, grad_small[...])
    save(grad_small, p_small)
    save(out, out_both)
    for ex in (ex_s, ex_r, ex_o, ex_q, ex_kv):
        ex.wait_send()

    @pl.when(section == layer)
    def _():
        for here, away in saves:
            here.wait()
            away.wait_recv()

    @pl.when(section != layer)
    def _():
        for here, away in saves:
            away.wait_send()


def layer_backward(layer, grad, state, geometry, plan, taken, small_t, weights, kept):
    bf, f32 = jnp.bfloat16, jnp.float32
    cosine, sine, qidx, qlab, klab = geometry
    route, first_table, second_table, _ = plan
    slots = pltpu.VMEM((EXPERTS, PAD_CAP, D), bf)
    shapes = dict(OPERANDS)
    order = ("na", "at", "nf", "sh", "rc", "hd", "qkv", "pr", "gu", "sd", "j", "er", "small")
    outs = pl.pallas_call(
        functools.partial(backward_kernel, layer),
        out_shape=[jax.ShapeDtypeStruct((ROWS, D), f32), jax.ShapeDtypeStruct((2, ROWS, D), f32)]
        + [jax.ShapeDtypeStruct((2,) + shapes[n], operand_type(n)) for n in order],
        in_specs=[VMEM] * 12 + [ANY] * (6 + len(KEPT)),
        out_specs=[VMEM, ANY] + [ANY] * N_OPS,
        scratch_shapes=weight_scratch()
        + [pltpu.VMEM(s, t) for s, t in KEPT] + [DMA((len(KEPT),))]
        + [pltpu.VMEM(shapes[n], operand_type(n)) for n in order if n != "er"] + [DMA((N_OPS + 1,))] * 3
        + [
            slots, slots, slots, slots,
            pltpu.VMEM((4, ROWS, 192), bf), pltpu.VMEM((4, ROWS, 192), bf),
            pltpu.VMEM((4, ROWS, 192), bf), pltpu.VMEM((4, ROWS, 192), bf),
            pltpu.VMEM((8, ROWS, 384), bf), pltpu.VMEM((8, ROWS, 384), bf), pltpu.VMEM((SEQ, 384), f32),
            pltpu.VMEM((ROWS, D), f32), pltpu.VMEM((ROWS, FF), bf), pltpu.VMEM((SLOTS, FF), bf),
            DMA((7,)), DMA((7,)), DMA((7,)), DMA((7,)), DMA((3,)), DMA((3,)), DMA((3,)), DMA((3,)), DMA((7,)), DMA((7,)),
        ],
        compiler_params=pltpu.CompilerParams(collective_id=3 + layer, has_side_effects=True, vmem_limit_bytes=62 << 20),
        name="layer_backward",
    )(grad, state, cosine, sine, qidx, qlab, klab, route, first_table, second_table, taken, small_t, *weights, *kept)
    return outs[0], outs[1], outs[2:]


def token_positions(group_row):
    labels = jnp.arange(CONT + 1, dtype=jnp.int32)
    member = (group_row[:, None] == labels[None, :]).astype(jnp.int32)
    run_sizes = jnp.sum(member, axis=0)
    run_starts = jnp.cumsum(run_sizes) - run_sizes
    first_index = jnp.sum(member * run_starts[None, :], axis=1)
    token_index = jnp.arange(group_row.shape[0], dtype=jnp.int32)
    return jnp.where(group_row == 0, token_index, run_sizes[0] + token_index - first_index)


def rotation_tables(positions):
    half = HEAD_DIM // 2
    frequency = jnp.exp(-math.log(10000.0) * jnp.arange(half, dtype=jnp.float32) / half)
    angles = positions.astype(jnp.float32)[:, None] * frequency[None, :]
    cosine, sine = jnp.cos(angles), jnp.sin(angles)
    cosine = jnp.tile(jnp.concatenate([cosine, cosine], axis=1), (1, HEADS))
    sine = jnp.tile(jnp.concatenate([-sine, sine], axis=1), (1, HEADS))
    return cosine, sine


def slot_tables(route, rank):
    pairs = ROWS * TOP
    expert = route.reshape(-1)
    key = rank.reshape(-1) * pairs + jnp.arange(pairs, dtype=jnp.int32)
    earlier = (expert[None, :] == expert[:, None]) & (key[None, :] < key[:, None])
    slot = jnp.sum(earlier.astype(jnp.int32), axis=1)
    place = jnp.where(slot < CAP, expert * PAD_CAP + slot, -1).reshape(ROWS, TOP)
    every = jnp.arange(SLOTS, dtype=jnp.int32)
    first, second = [place[:, c : c + 1] == every[None, :] for c in range(TOP)]
    both = low(first | second)
    return (route, low(first), low(second), both.T), both


def swap_cores(value):
    return lax.ppermute(value, "section", [(0, 1), (1, 0)])


def on_device(
    x_in, cotangent, group_ids, routes, priority,
    gains, w_qkv, w_out, router, shared_gate_up, shared_down, expert_gate_up, expert_down,
):
    section = lax.axis_index("section")
    ctx = lax.axis_index("ctx")
    first = section == 0

    pack = jnp.concatenate(
        [w_qkv[0], w_out[0], gains[0], router[0], jnp.zeros((OWN, SMALL - 2 - EXPERTS), jnp.bfloat16), shared_gate_up[0]],
        axis=1,
    )
    pack = jnp.pad(pack, ((0, 16 - OWN), (0, 0)))

    def mine(value):
        return jnp.where(first, value[0], value[1])

    def other(value):
        return jnp.where(first, value[1], value[0])

    picked = jnp.stack([routes[0, :, 0], priority[0, :, 0]], axis=1)
    passed = swap_cores(other(picked))
    own = mine(picked)
    plans = [jnp.where(first, own, passed), jnp.where(first, passed, own)]
    plans, taken = zip(*[slot_tables(plan[0], plan[1]) for plan in plans])

    group_row = mine(group_ids[:, 0])
    positions = token_positions(group_row)
    cosine, sine = rotation_tables(lax.dynamic_slice_in_dim(positions, ctx * ROWS, ROWS))
    half_start = ctx // 4 * 512
    qlab = lax.dynamic_slice_in_dim(group_row, half_start, 512).reshape(4, ROWS, 1)
    qidx = (half_start + jnp.arange(512, dtype=jnp.int32)).reshape(4, ROWS, 1)
    geometry = (cosine, sine, qidx, qlab, group_row[None, :])

    state = mine(x_in[:, 0])
    (hidden, final), weights, kept = forward(
        pack, shared_down[0], expert_gate_up[0, 0], expert_down[0, 0], state, geometry, plans
    )
    small_t = [weights[layer][2][:, :8].astype(jnp.float32).T for layer in range(2)]
    hidden_grad, hidden_grads, operands_upper = layer_backward(
        1, mine(cotangent[:, 0]), hidden, geometry, plans[1], taken[1], small_t[1], weights[1], kept[1]
    )
    _, input_grads, operands_lower = layer_backward(
        0, low(hidden_grad), state, geometry, plans[0], taken[0], small_t[0], weights[0], kept[0]
    )
    qkv_grad, out_grad, small_grad, gu_grad, sd_grad, egu_grad, ed_grad = weight_grads(operands_lower, operands_upper)

    outputs = jnp.where(first, hidden, final)
    arrived = swap_cores(jnp.where(first, final, hidden))
    outputs = jnp.stack([jnp.where(first, outputs, arrived), jnp.where(first, arrived, outputs)])
    grads = jnp.where(first, input_grads, hidden_grads[::-1])
    return (
        outputs.reshape(1, 2, 1, ROWS, D),
        grads.reshape(1, 2, 1, ROWS, D),
        small_grad[None, :, :2],
        qkv_grad[None],
        out_grad[None],
        small_grad[None, :, 2 : 2 + EXPERTS],
        gu_grad[None],
        sd_grad[None],
        egu_grad[None, None],
        ed_grad[None, None],
    )


def solution(mesh):
    dense = P("section", ("ctx", "fsdp"), None)
    expert = P("section", "ctx", "fsdp", None)
    tokens = P("section", None, "fsdp", "ctx", None)
    rows = P(None, "fsdp", "ctx", None)
    return jax.shard_map(
        on_device,
        mesh=mesh,
        in_specs=(rows, rows, P(None, "fsdp", None), tokens, tokens) + (dense,) * 6 + (expert,) * 2,
        out_specs=(tokens, tokens) + (dense,) * 6 + (expert,) * 2,
        check_vma=False,
    )
```

time: 640 us -> 544 us (0.85)
  Pallas kernels: 591 us -> 495 us
    pallas_call x4 -> x2, Pallas kernels: 484 us -> 375 us  [the longest x1 237 us: forward(): pl.pallas_call(forward_kernel, out_shape=[jax.ShapeDtypeStruct((ROWS, D),...]
    pallas_call x2, Pallas kernels: 107 us -> 120 us  [layer_backward(): pl.pallas_call(functools.partial(backward_kernel, layer), out_shape=[jax....]
  transfers between devices with their start and end apart: 4 -> 2, of which waited for: 0 -> 1; matrix products, arithmetic and copies ran while one was open for 3% -> 2% of each run, Pallas kernels for 60% -> 0%
where the time goes in v3:
time: 544 us; the launch traced here: 535 us
  Pallas kernels  495 us (91%)
  other arithmetic  20.5 us (4%)
  local copies, waits for them, and re-layouts  17 us (3%)
    pallas_call x1, Pallas kernels, forward(): pl.pallas_call(forward_kernel, out_shape=[jax.ShapeDtypeStruct((ROWS, D),...  237 us
    pallas_call x1, Pallas kernels, weight_grads(): pl.pallas_call(grads_kernel, out_shape=[jax.ShapeDtypeStruct(shape, f32)...  138 us
    pallas_call x2, Pallas kernels, layer_backward(): pl.pallas_call(functools.partial(backward_kernel, layer), out_shape=[jax....  120 us
  transfers between devices with their start and end apart: 2, of which 1 were waited for; matrix products, arithmetic and copies ran while one was open for 2% of the time, Pallas kernels for 0%

profile of v3, /device:TPU:0, one launch (start us, length us, event | category | flops | bytes accessed | tf_op | source)
XLA Modules:
  0.0 534.7 jit_solution(12334394118930182939)
XLA Ops:
  0.7 0.8 fusion.11
  1.5 0.1 copy.105
  1.6 0.1 copy.106
  1.8 0.1 collective-permute-start
  1.9 0.7 add_add_fusion.qidx
  2.7 0.7 broadcast_select_fusion.3
  3.4 1.3 fusion.12.klab
  4.7 0.7 and_convert_fusion.1.sel
  5.4 0.7 and_convert_fusion.refs_26_
  6.1 0.1 convert_reduce_fusion.2
  6.2 0.2 reduce-window.8
  6.4 0.1 select_reduce_fusion
  6.5 1.7 select_bitcast_fusion.4.state
  8.3 1.7 select_bitcast_fusion.1.grad
  10.1 0.1 fusion.10
  10.3 0.9 copy.89.qlab
  11.2 0.9 copy.87.cosine
  12.1 0.9 copy.88.sine
  13.0 0.1 copy.83
  13.3 0.1 concatenate.9
  13.4 0.7 pad.4.pack
  14.1 0.6 slice_bitcast_fusion.1
  14.7 0.1 eq.292
  14.9 0.1 mul.74
  15.0 0.2 convert_reduce_fusion.1
  15.2 0.1 reduce_sum.43
  15.4 0.7 slice_bitcast_fusion
  16.0 0.1 eq.300
  16.2 0.1 mul.77
  16.3 0.2 convert_reduce_fusion
  16.6 0.1 reduce_sum.45
  16.7 0.2 slice_reduce_fusion
  16.9 0.1 iota_compare_fusion.8
  17.1 0.1 iota_compare_fusion.10
  17.2 0.2 slice_reduce_fusion.1
  17.4 0.1 iota_compare_fusion.9
  17.5 0.1 iota_compare_fusion.11
  17.6 0.7 pad_add_fusion.route
  18.3 0.8 fusion.6
  19.1 0.8 fusion.7
  19.9 0.7 add_convert_fusion.2.taken_t
  20.6 0.7 add_convert_fusion.1.second_table
  21.3 0.7 add_convert_fusion.first_table
  22.1 237.2 %forward.1 = (bf16[128,768]{1,0:T(8,128)(2,1)}, bf16[128,768]{1,0:T(8,128)(2,1)}, bf16[768,3072]{1,0:T(8,128)(2,1)}, bf16[768,4096]{1,0:T(8,128)(2,1)}, bf16[768...) custom-call(bf16[16,7296]{1,0:T(8,128)(2,1)} %pad.4.pack, ...), custom_call_target="tpu_custom_call" | custom-call | tf_op jit(solution)/shard_map/forward/pallas_call | solution.py:889
  259.3 1.1 copy.90
  260.3 0.6 convert_bitcast_fusion.1.small_t
  260.9 58.2 %layer_backward.2 = (f32[128,768]{1,0:T(8,128)}, f32[2,128,768]{2,1,0:T(8,128)}, bf16[2,768,128]{2,1,0:T(8,128)(2,1)}, bf16[2,768,128]{2,1,0:T(8,128)(2,1)}, bf1...) custom-call(bf16[128,768]{1,0:T(8,128)(2,1)} %select_bitcast_fusion., ...), custom_call_target="tpu_custom_call" | custom-call | tf_op jit(solution)/shard_map/layer_backward/pallas_call | solution.py:1150
  319.1 1.7 convert_element_type.51.grad
  320.8 0.1 copy.94
  321.0 0.6 convert_bitcast_fusion.small_t
  321.6 62.1 %layer_backward.3 = (f32[128,768]{1,0:T(8,128)}, f32[2,128,768]{2,1,0:T(8,128)}, bf16[2,768,128]{2,1,0:T(8,128)(2,1)}, bf16[2,768,128]{2,1,0:T(8,128)(2,1)}, bf1...) custom-call(bf16[128,768]{1,0:T(8,128)(2,1)} %convert_element_type.5, ...), custom_call_target="tpu_custom_call" | custom-call | tf_op jit(solution)/shard_map/layer_backward/pallas_call | solution.py:1150
  383.7 137.6 %weight_grads.1 = (f32[12,2304]{1,0:T(8,128)}, f32[12,768]{1,0:T(8,128)}, f32[12,128]{1,0:T(8,128)}, f32[12,4096]{1,0:T(8,128)}, f32[32,768]{1,0:T(8,128)}, /*index=5*/f32[96,4096]{1,0:T(8,128)}, f32[256,768]{1,0:T(8,128)}) custom-call(bf16[2,768,128]{2,1,0:T(8,128)(2,1)} %get-tuple-element.113.refs_0_, bf16[2,768,128]{2,1,0:T(8,128)(2,1)} %get-tuple-element.114.refs_1_, ...), custom_call_target="tpu_custom_call" | custom-call | tf_op jit(solution)/shard_map/weight_grads/pallas_call | solution.py:512
  521.3 1.9 copy.104
  523.3 1.7 copy.102
  525.0 1.5 copy.103
  526.4 0.8 slice.91
  527.2 0.7 copy.99
  527.9 1.3 copy.98
  529.3 1.0 select_bitcast_fusion
  530.3 0.4 collective-permute-done.1
  530.8 0.8 maximum_bitcast_fusion
  531.6 0.6 copy.110
  532.2 1.1 copy.111
  533.4 0.9 copy.112
  (49 shorter events, 0.7 us)
Async XLA Ops:
  0.6 12.4 %copy-start.12 = (bf16[1,12,2]{1,2,0:T(2,128)(2,1)S(1)}, bf16[1,12,2]{1,2,0:T(2,128)(2,1)}, u32[]{:S(2)}) copy-start(bf16[1,12,2]{1,2,0:T(2,128)(2,1)} %param.18) | copy-start | bytes 148
  0.7 12.5 %copy-start.11 = (bf16[1,12,8]{1,2,0:T(8,128)(2,1)S(1)}, bf16[1,12,8]{1,2,0:T(8,128)(2,1)}, u32[]{:S(2)}) copy-start(bf16[1,12,8]{1,2,0:T(8,128)(2,1)} %param.21) | copy-start | bytes 580
  0.7 12.6 %copy-start.9 = (bf16[1,12,2304]{2,1,0:T(8,128)(2,1)S(1)}, bf16[1,12,2304]{2,1,0:T(8,128)(2,1)}, u32[]{:S(2)}) copy-start(bf16[1,12,2304]{2,1,0:T(8,128)(2,1)} %param.19) | copy-start | bytes 165892
  0.7 12.6 %copy-start.10 = (bf16[1,12,768]{2,1,0:T(8,128)(2,1)S(1)}, bf16[1,12,768]{2,1,0:T(8,128)(2,1)}, u32[]{:S(2)}) copy-start(bf16[1,12,768]{2,1,0:T(8,128)(2,1)} %param.20) | copy-start | bytes 55300
  0.7 12.6 %copy-start.7 = (bf16[1,12,4096]{2,1,0:T(8,128)(2,1)S(1)}, bf16[1,12,4096]{2,1,0:T(8,128)(2,1)}, u32[]{:S(2)}) copy-start(bf16[1,12,4096]{2,1,0:T(8,128)(2,1)} %param.22) | copy-start | bytes 294916
  1.8 12.3 %collective-permute-start = (s32[2,128,2]{2,1,0:T(8,128)S(1)}, s32[2,128,2]{2,1,0:T(8,128)S(1)}, u32[]{:S(2)}, u32[]{:S(2)}) collective-permute-start(s32[2,128,2]{2,1,0:T(8,128)S(1)} %select_bitcast_fusion.5), channel_id=1, source_target_pairs={{0,64},{64,0},{1,65},{65,1},{2,66},{66,2},{3,67},{67,3},{4,68},{68... | collective-permute-start | bytes 6152 | tf_op jit(solution)/shard_map/ppermute | solution.py:1207
  260.9 59.9 %copy-start.2 = (bf16[768,128]{1,0:T(8,128)(2,1)S(1)}, bf16[768,128]{1,0:T(8,128)(2,1)}, u32[]{:S(2)}) copy-start(bf16[768,128]{1,0:T(8,128)(2,1)} %get-tuple-element.96.g_small) | copy-start | bytes 589828
  383.7 145.5 %copy-start = (bf16[128,768]{1,0:T(8,128)(2,1)S(1)}, bf16[128,768]{1,0:T(8,128)(2,1)}, u32[]{:S(2)}) copy-start(bf16[128,768]{1,0:T(8,128)(2,1)} %get-tuple-element.78.state) | copy-start | bytes 589828
  383.7 145.5 %copy-start.6 = (bf16[128,768]{1,0:T(8,128)(2,1)S(1)}, bf16[128,768]{1,0:T(8,128)(2,1)}, u32[]{:S(2)}) copy-start(bf16[128,768]{1,0:T(8,128)(2,1)} %get-tuple-element.79) | copy-start | bytes 589828
  383.7 145.6 %copy-start.3 = (f32[2,128,768]{2,1,0:T(8,128)S(1)}, f32[2,128,768]{2,1,0:T(8,128)}, u32[]{:S(2)}) copy-start(f32[2,128,768]{2,1,0:T(8,128)} %get-tuple-element.112) | copy-start | bytes 2359300
  383.7 145.6 %copy-start.4 = (f32[2,128,768]{2,1,0:T(8,128)S(1)}, f32[2,128,768]{2,1,0:T(8,128)}, u32[]{:S(2)}) copy-start(f32[2,128,768]{2,1,0:T(8,128)} %get-tuple-element.111) | copy-start | bytes 2359300
  521.3 10.9 %copy-start.1 = (f32[96,4096]{1,0:T(8,128)S(1)}, f32[96,4096]{1,0:T(8,128)}, u32[]{:S(2)}) copy-start(f32[96,4096]{1,0:T(8,128)} %get-tuple-element.144) | copy-start | bytes 4718596
  529.2 2.4 copy-start.8
  529.2 1.5 collective-permute-start.1
  530.3 3.1 copy-start.5

commit v4 on v3

--- a/solution.py
+++ b/solution.py
@@ -98,24 +98,34 @@
             copy.wait_send()
 
 
+def row_view(rows):
+    return lambda whole, block, part: rows_at(whole, block, rows, part)
+
+
+def shard_view(whole, block, part):
+    if part is None:
+        return whole.at[:, block]
+    return whole.at[4 * part : 4 * part + 4, block]
+
+
 class Tree:
-    def __init__(self, over_ctx, layer, own, whole, rows, send, recv, c_send, c_recv, l_sem):
+    def __init__(self, over_ctx, halves, own, whole, view, send, recv, c_send, c_recv, l_sem):
         section, a, z, y, h = place_ids()
         near = neighbours()
-        self.over_ctx = over_ctx
+        self.halves = halves
         ring, pair = ("z", "zx") if over_ctx else ("y", "yx")
         plus, minus, across = near[ring + "p"], near[ring + "m"], near[pair]
 
-        def block(step, side):
-            return ctx_of(a + side, z + step) if over_ctx else fsdp_of(y + step, h + side)
-
         def views(step, side, part=None):
-            return [rows_at(w, block(step, side), r, part) for w, r in zip(whole, rows)]
+            block = ctx_of(a + side, z + step) if over_ctx else fsdp_of(y + step, h + side)
+            return [v(w, block, part) for w, v in zip(whole, view)]
 
         def hop(index, sources, targets, device):
             return Hop(sources, targets, device, send.at[index], recv.at[index])
 
         mine = views(0, 0)
+        self.stays = [] if own is None else [pltpu.make_async_copy(o, m, l_sem.at[i]) for i, (o, m) in enumerate(zip(own, mine))]
+        own = mine if own is None else own
         self.hops = [
             hop(0, own, mine, plus),
             hop(1, own, mine, minus),
@@ -125,16 +135,15 @@
             hop(5, views(0, 1), views(0, 1), plus),
             hop(6, views(0, 1), views(0, 1), minus),
         ]
-        if over_ctx:
-            self.hops.append(hop(7, views(2, 0), views(2, 0), across))
-        else:
+        if halves:
             self.hops.append(hop(7, views(-1, 1, 0), views(-1, 1, 0), plus))
             self.hops.append(hop(8, views(1, 1, 1), views(1, 1, 1), minus))
+        else:
+            self.hops.append(hop(7, views(2, 0), views(2, 0), across))
         places = [(0, 0), (-1, 0), (1, 0), (0, 1), (2, 0), (-1, 1), (1, 1), (2, 1)]
         self.cores = [
             Hop(own if k == 0 else views(*p), views(*p), near["core"], c_send.at[k], c_recv.at[k]) for k, p in enumerate(places)
         ]
-        self.stays = [pltpu.make_async_copy(o, m, l_sem.at[i]) for i, (o, m) in enumerate(zip(own, mine))]
 
     def start_own(self):
         for index in (0, 1, 2):
@@ -143,34 +152,39 @@
         for copy in self.stays:
             copy.start()
 
-    def forward1(self):
-        for index, starts, core in ((0, (3,), 1), (1, (4,), 2), (2, (5, 6), 3)):
+    def pass_ring(self):
+        for index, later, core in ((0, 3, 1), (1, 4, 2)):
             self.hops[index].wait_recv()
-            for later in starts:
-                self.hops[later].start()
+            self.hops[later].start()
             self.cores[core].start()
 
-    def forward2(self):
-        self.hops[3].wait_recv()
-        self.hops[4].wait_recv()
-        if self.over_ctx:
-            self.hops[7].start()
-        self.cores[4].start()
-        if not self.over_ctx:
+    def pass_pair(self):
+        self.hops[2].wait_recv()
+        self.hops[5].start()
+        self.hops[6].start()
+        self.cores[3].start()
+
+    def pass_far(self):
+        if self.halves:
             for index, later, core in ((5, 7, 5), (6, 8, 6)):
                 self.hops[index].wait_recv()
                 self.hops[later].start()
                 self.cores[core].start()
+        self.hops[3].wait_recv()
+        self.hops[4].wait_recv()
+        if not self.halves:
+            self.hops[7].start()
+        self.cores[4].start()
 
     def finish(self):
-        if self.over_ctx:
+        if self.halves:
+            self.hops[7].wait_recv()
+            self.hops[8].wait_recv()
+            self.cores[7].start()
+        else:
             for index, core in ((5, 5), (6, 6), (7, 7)):
                 self.hops[index].wait_recv()
                 self.cores[core].start()
-        else:
-            self.hops[7].wait_recv()
-            self.hops[8].wait_recv()
-            self.cores[7].start()
         for copy in self.stays:
             copy.wait()
 
@@ -184,29 +198,30 @@
 
 
 class Shards:
-    def __init__(self, pack, sd, packs, own_sd, send, recv, l_sem):
+    def __init__(self, pack, packs, sd, whole_sd, send, recv, l_sem):
         section, a, z, y, h = place_ids()
         ctx, fsdp = ctx_of(a, z), fsdp_of(y, h)
         wide = slice(0, WIDE + SMALL)
         rest = slice(WIDE + SMALL, PACK)
         mine = packs.at[pl.ds(pl.multiple_of(fsdp * 16, 16), 16)]
-        pieces = [(pack.at[:, wide], mine.at[:, wide]), (pack.at[:, rest], mine.at[:, rest]), (sd, rows_at(own_sd, fsdp, 32))]
+        pieces = [
+            (pack.at[:, wide], mine.at[:, wide], fsdp_peers()),
+            (pack.at[:, rest], mine.at[:, rest], fsdp_peers()),
+            (sd, whole_sd.at[ctx, fsdp], ctx_peers()),
+        ]
         self.hops = [
-            [
-                Hop([s], [t], device, send.at[k, pl.ds(i, 1)], recv.at[k, pl.ds(i, 1)])
-                for k, device in enumerate(fsdp_peers())
-            ]
-            for i, (s, t) in enumerate(pieces)
+            [Hop([s], [t], device, send.at[k, pl.ds(i, 1)], recv.at[k, pl.ds(i, 1)]) for k, device in enumerate(peers)]
+            for i, (s, t, peers) in enumerate(pieces)
         ]
-        self.stays = [pltpu.make_async_copy(s, t, l_sem.at[i]) for i, (s, t) in enumerate(pieces)]
-
-    def start(self, pieces):
+        self.stays = [pltpu.make_async_copy(s, t, l_sem.at[i]) for i, (s, t, _) in enumerate(pieces)]
+
+    def start(self, *pieces):
         for i in pieces:
             for hop in self.hops[i]:
                 hop.start()
             self.stays[i].start()
 
-    def wait(self, pieces):
+    def wait(self, *pieces):
         for i in pieces:
             for hop in self.hops[i]:
                 hop.wait_recv()
@@ -622,14 +637,17 @@
             copy.wait_send()
 
 
+CTX_STEPS = [(1, 0), (0, 1), (0, 3), (0, 2), (1, 1), (1, 3), (1, 2)]
+
+
 def ctx_peers():
     section, a, z, y, h = place_ids()
     fsdp = fsdp_of(y, h)
-    return [(section, ctx_of(a + da, z + dz), fsdp) for da in range(2) for dz in range(4) if (da, dz) != (0, 0)]
+    return [(section, ctx_of(a + da, z + dz), fsdp) for da, dz in CTX_STEPS]
 
 
 def forward_kernel(
-    pack, g_sd, g_egu, g_ed, sel,
+    pack, i_sd, i_egu, i_ed, sel,
     state, cosine, sine, qidx, qlab, klab, route, first_table, second_table, taken_t,
     out_lower, out_upper,
     l_wide, l_gu, l_small, l_sd, l_egu, l_ed, u_wide, u_gu, u_small, u_sd, u_egu, u_ed,
@@ -637,26 +655,36 @@
 ):
     kept = (rest[:9], rest[9:18])
     (wide, gu, small, sd, egu, ed, w_sem,
-     packs, own_wide, own_small, own_gu, own_sd, g_stay, sh_send, sh_recv,
-     w_send, w_recv, r_send, r_recv, e_send, e_recv, wc_send, wc_recv, rc_send, rc_recv, ec_send, ec_recv,
+     packs, own_wide, own_small, own_gu, g_sd, g_egu, g_ed, g_stay, sh_send, sh_recv,
+     w_send, w_recv, g_send, g_recv, d_send, d_recv, e_send, e_recv,
+     wc_send, wc_recv, gc_send, gc_recv, dc_send, dc_recv, ec_send, ec_recv,
      kv_pack, q_pack, kv_all, q_all, o_pack, o_in, lse, att, res, sj, sh, sent, rc, ej, eh, result, ret, k_sem,
      x_send, x_recv) = rest[18:]
     section, a, z, y, h = place_ids()
     ctx = ctx_of(a, z)
     wholes = ((l_wide, l_gu, l_small, l_sd, l_egu, l_ed), (u_wide, u_gu, u_small, u_sd, u_egu, u_ed))
+    shards_in = [
+        pltpu.make_async_copy(s, t, g_stay.at[4, i]) for i, (s, t) in enumerate(((i_sd, g_sd), (i_egu, g_egu), (i_ed, g_ed)))
+    ]
+    for copy in shards_in:
+        copy.start()
     greet([neighbours()["core"]] + ctx_peers() + fsdp_peers())
-
-    shards = Shards(pack, g_sd, packs, own_sd, sh_send, sh_recv, g_stay.at[0])
-    trees = []
+    for copy in shards_in:
+        copy.wait()
+
+    trees, firsts = [], []
     for layer in range(2):
         t_wide, t_gu, t_small, t_sd, t_egu, t_ed = wholes[layer]
+        firsts.append(Shards(pack, packs, g_sd, t_sd, sh_send, sh_recv, g_stay.at[0]))
         trees.append(
             dict(
-                w=Tree(True, layer, [own_wide, own_small], [t_wide, t_small], (96, 96),
+                w=Tree(True, False, [own_wide, own_small], [t_wide, t_small], [row_view(96)] * 2,
                        w_send, w_recv, wc_send.at[layer], wc_recv.at[layer], g_stay.at[1]),
-                r=Tree(True, layer, [own_gu, own_sd], [t_gu, t_sd], (96, 256),
-                       r_send, r_recv, rc_send.at[layer], rc_recv.at[layer], g_stay.at[2]),
-                e=Tree(False, layer, [g_egu, g_ed], [t_egu, t_ed], (96, 256),
+                g=Tree(True, True, [own_gu], [t_gu], [row_view(96)],
+                       g_send, g_recv, gc_send.at[layer], gc_recv.at[layer], g_stay.at[2]),
+                d=Tree(False, True, None, [t_sd], [shard_view],
+                       d_send, d_recv, dc_send.at[layer], dc_recv.at[layer], None),
+                e=Tree(False, True, [g_egu, g_ed], [t_egu, t_ed], [row_view(96), row_view(256)],
                        e_send, e_recv, ec_send.at[layer], ec_recv.at[layer], g_stay.at[3]),
             )
         )
@@ -668,12 +696,12 @@
                 step()
 
     def close_wide():
-        shards.wait((0,))
+        firsts[0].wait(0)
         close_rows(sel, packs, own_wide, 0)
         close_rows(sel, packs, own_small, WIDE)
 
-    def close_rest():
-        shards.wait((1, 2))
+    def close_gu():
+        firsts[0].wait(1)
         close_rows(sel, packs, own_gu, WIDE + SMALL)
 
     def arrived(layer, group):
@@ -693,30 +721,50 @@
             target = (wide.at[layer], gu, small.at[layer], sd, egu, ed)[i]
             pltpu.make_async_copy(wholes[layer][i], target, w_sem.at[layer, i]).wait()
 
+    def first(layer, *pieces):
+        return lambda: firsts[layer].start(*pieces)
+
+    def down(layer):
+        def step():
+            firsts[layer].wait(2)
+            trees[layer]["d"].start_own()
+
+        return step
+
     lower, upper = trees
     hooks = {
         (0, "start"): lambda: (
-            drive(0, lambda: shards.start((0,)), close_wide, lambda: shards.start((1, 2)), lower["w"].start_own, close_rest,
-                  lower["w"].forward1, lower["e"].start_own, lower["w"].forward2, lower["r"].start_own),
+            drive(0, first(0, 0, 2), close_wide, lower["w"].start_own, first(0, 1), lower["e"].start_own,
+                  lower["w"].pass_ring, lower["w"].pass_pair, close_gu, lower["g"].start_own, lower["w"].pass_far),
             arrived(0, "w"), load(0, 0, 2),
         ),
-        (0, "keys"): lambda: (drive(0, lower["e"].forward1), drive(1, lambda: shards.start((0, 1, 2)))),
-        (0, "queries"): lambda: drive(0, lower["r"].forward1),
-        (0, "block1"): lambda: drive(0, lower["e"].forward2),
-        (0, "block2"): lambda: drive(1, close_wide, upper["w"].start_own),
-        (0, "attended"): lambda: (drive(0, lower["r"].forward2), drive(1, close_rest)),
-        (0, "sent"): lambda: (arrived(0, "r"), load(0, 1, 3)),
-        (0, "shared0"): lambda: (drive(1, upper["w"].forward1, upper["e"].start_own),),
-        (0, "shared"): lambda: (arrived(0, "e"), load(0, 4, 5)),
-        (0, "expert1"): lambda: drive(1, upper["r"].start_own),
-        (0, "expert2"): lambda: drive(1, upper["w"].forward2),
-        (0, "expert3"): lambda: drive(1, upper["e"].forward1),
-        (0, "returned"): lambda: drive(1, upper["r"].forward1),
+        (0, "keys"): lambda: (drive(0, lower["e"].pass_ring, lower["e"].pass_pair), drive(1, first(1, 0, 1, 2))),
+        (0, "queries"): lambda: drive(0, lower["g"].pass_pair),
+        (0, "block1"): lambda: drive(0, down(0)),
+        (0, "attended"): lambda: (
+            drive(0, lower["g"].pass_ring, lower["e"].pass_far), drive(1, close_wide, upper["w"].start_own),
+        ),
+        (0, "sent"): lambda: (
+            drive(0, lower["g"].pass_far, lower["d"].pass_ring, lower["d"].pass_pair),
+            drive(1, upper["w"].pass_ring, upper["w"].pass_pair, close_gu),
+            arrived(0, "e"), load(0, 4, 5),
+        ),
+        (0, "expert0"): lambda: drive(1, upper["e"].start_own),
+        (0, "expert1"): lambda: drive(0, lower["d"].pass_far),
+        (0, "expert2"): lambda: drive(1, upper["w"].pass_far),
+        (0, "returned"): lambda: (
+            arrived(0, "g"), load(0, 1), drive(1, upper["g"].start_own, upper["e"].pass_ring, upper["e"].pass_pair),
+            arrived(0, "d"), load(0, 3),
+        ),
         (1, "start"): lambda: (arrived(1, "w"), load(1, 0, 2)),
-        (1, "keys"): lambda: drive(1, upper["e"].forward2),
-        (1, "block0"): lambda: drive(1, upper["r"].forward2),
-        (1, "sent"): lambda: (arrived(1, "r"), load(1, 1, 3)),
-        (1, "shared"): lambda: (arrived(1, "e"), load(1, 4, 5)),
+        (1, "queries"): lambda: drive(1, upper["g"].pass_pair),
+        (1, "block1"): lambda: drive(1, down(1), upper["e"].pass_far),
+        (1, "attended"): lambda: drive(1, upper["g"].pass_ring),
+        (1, "sent"): lambda: (
+            drive(1, upper["g"].pass_far, upper["d"].pass_ring, upper["d"].pass_pair), arrived(1, "e"), load(1, 4, 5),
+        ),
+        (1, "expert1"): lambda: drive(1, upper["d"].pass_far),
+        (1, "returned"): lambda: (arrived(1, "g"), load(1, 1), arrived(1, "d"), load(1, 3)),
     }
 
     def one_layer(layer, x, out):
@@ -802,24 +850,6 @@
         _, gates = pair_gates(dot(normed, small_l[...]), route[layer])
         mix = first_table[layer].astype(jnp.float32) * gates[0] + second_table[layer].astype(jnp.float32) * gates[1]
         hook("sent")
-        loaded(layer, 1)
-
-        def shared_part(j):
-            at = pl.ds(pl.multiple_of(j * 256, 256), 256)
-            up_at = pl.ds(pl.multiple_of(FF + j * 256, 256), 256)
-            gate, up = dot(normed, gu[:, at]), dot(normed, gu[:, up_at])
-            sj[:, at] = gate
-            sj[:, up_at] = up
-            sh[:, at] = low(gate * jax.nn.sigmoid(gate) * up)
-
-        for d in range(2):
-            pl.loop(4 * d, 4 * d + 4)(shared_part)
-            hook(f"shared{d}")
-
-        save(sj, k_sj)
-        hook("shared")
-        loaded(layer, 3)
-        shared_out = dot(sh[...], sd[...])
         ex_s.wait_recv()
         save(rc, k_rc)
         loaded(layer, 4)
@@ -847,6 +877,21 @@
         ex_r.start()
         ret[ctx] = result[ctx]
         hook("returned")
+        loaded(layer, 1)
+
+        def shared_part(j):
+            at = pl.ds(pl.multiple_of(j * 256, 256), 256)
+            up_at = pl.ds(pl.multiple_of(FF + j * 256, 256), 256)
+            gate, up = dot(normed, gu[:, at]), dot(normed, gu[:, up_at])
+            sj[:, at] = gate
+            sj[:, up_at] = up
+            sh[:, at] = low(gate * jax.nn.sigmoid(gate) * up)
+
+        pl.loop(0, FF // 256)(shared_part)
+
+        save(sj, k_sj)
+        loaded(layer, 3)
+        shared_out = dot(sh[...], sd[...].reshape(FF, D))
         ex_r.wait_recv()
         save(ret, k_ret)
         high, rest_of = split(mix)
@@ -861,14 +906,14 @@
     one_layer(0, state[...].astype(jnp.float32), out_lower)
     one_layer(1, out_lower[...].astype(jnp.float32), out_upper)
     for layer in range(2):
-        drive(layer, shards.drain, *[tree.drain for tree in trees[layer].values()])
+        drive(layer, firsts[layer].drain, *[tree.drain for tree in trees[layer].values()])
 
 
 def weight_scratch():
     bf = jnp.bfloat16
     return [
         pltpu.VMEM((D, WIDE), bf), pltpu.VMEM((D, 2 * FF), bf), pltpu.VMEM((D, SMALL), bf),
-        pltpu.VMEM((FF, D), bf), pltpu.VMEM((D, 2 * FF), bf), pltpu.VMEM((FF, D), bf), DMA((6,)),
+        pltpu.VMEM((8, 8, 32, D), bf), pltpu.VMEM((D, 2 * FF), bf), pltpu.VMEM((FF, D), bf), DMA((6,)),
     ]
 
 
@@ -879,7 +924,7 @@
 )
 
 
-WEIGHTS = ((D, WIDE), (D, 2 * FF), (D, SMALL), (FF, D), (D, 2 * FF), (FF, D))
+WEIGHTS = ((D, WIDE), (D, 2 * FF), (D, SMALL), (8, 8, 32, D), (D, 2 * FF), (FF, D))
 
 
 def forward(pack, sd, egu, ed, state, geometry, plans):
@@ -895,12 +940,13 @@
         out_specs=[VMEM] * 2 + [ANY] * (2 * len(WEIGHTS) + 2 * len(KEPT)),
         scratch_shapes=[
             pltpu.VMEM((2, D, WIDE), bf), pltpu.VMEM((D, 2 * FF), bf), pltpu.VMEM((2, D, SMALL), bf),
-            pltpu.VMEM((FF, D), bf), pltpu.VMEM((D, 2 * FF), bf), pltpu.VMEM((FF, D), bf), DMA((2, 6)),
+            pltpu.VMEM((8, 8, 32, D), bf), pltpu.VMEM((D, 2 * FF), bf), pltpu.VMEM((FF, D), bf), DMA((2, 6)),
             pltpu.VMEM((128, PACK), bf), pltpu.VMEM((96, WIDE), bf), pltpu.VMEM((96, SMALL), bf),
-            pltpu.VMEM((96, 2 * FF), bf), pltpu.VMEM((256, D), bf), DMA((4, 3)), DMA((7, 3)), DMA((7, 3)),
-            DMA((8, 2)), DMA((8, 2)), DMA((8, 2)), DMA((8, 2)), DMA((9, 2)), DMA((9, 2)),
+            pltpu.VMEM((96, 2 * FF), bf), pltpu.VMEM((32, D), bf), pltpu.VMEM((96, 2 * FF), bf), pltpu.VMEM((256, D), bf),
+            DMA((5, 3)), DMA((7, 3)), DMA((7, 3)),
         ]
-        + [DMA((2, 8, 2))] * 6
+        + [DMA((9, 2))] * 8
+        + [DMA((2, 8, 2))] * 8
         + [
             pltpu.VMEM((4, ROWS, 384), bf), pltpu.VMEM((4, ROWS, 192), bf),
             pltpu.VMEM((8, ROWS, 384), bf), pltpu.VMEM((4, ROWS, 192), bf),
@@ -992,11 +1038,11 @@
     loads[3].wait()
     reads[5].wait()
 
-    @pl.loop(0, FF // 256)
+    @pl.loop(0, FF // 1024)
     def _(j):
-        at = pl.ds(pl.multiple_of(j * 256, 256), 256)
-        up_at = pl.ds(pl.multiple_of(FF + j * 256, 256), 256)
-        hidden_grad = dot_t(m_sd[...], sd[at, :])
+        at = pl.ds(pl.multiple_of(j * 1024, 256), 1024)
+        up_at = pl.ds(pl.multiple_of(FF + j * 1024, 256), 1024)
+        hidden_grad = dot_t(m_sd[...], sd[pl.ds(j * 4, 4)].reshape(1024, D))
         gate, up = sj[:, at], sj[:, up_at]
         sig = jax.nn.sigmoid(gate)
         m_gu[:, at] = low(hidden_grad * up * sig * (1.0 + gate * (1.0 - sig)))
@@ -1010,9 +1056,9 @@
     save(t_nf, p_nf)
     loads[1].wait()
 
-    @pl.loop(0, D // 256)
+    @pl.loop(0, D // 768)
     def _(j):
-        at = pl.ds(pl.multiple_of(j * 256, 256), 256)
+        at = pl.ds(pl.multiple_of(j * 768, 256), 768)
         normed_grad[:, at] = dot_t(m_gu[...], gu[at, :])
 
     reads[8].wait()
@@ -1030,10 +1076,10 @@
     ex_s.wait_recv()
     save(er, p_er)
 
-    @pl.loop(0, FF // 256)
+    @pl.loop(0, FF // 1024)
     def _(j):
-        at = pl.ds(pl.multiple_of(j * 256, 256), 256)
-        up_at = pl.ds(pl.multiple_of(FF + j * 256, 256), 256)
+        at = pl.ds(pl.multiple_of(j * 1024, 256), 1024)
+        up_at = pl.ds(pl.multiple_of(FF + j * 1024, 256), 1024)
         hidden_grad = dot_t(er[...].reshape(SLOTS, D), ed[at, :])
         gate, up = ej[:, at], ej[:, up_at]
         sig = jax.nn.sigmoid(gate)
@@ -1044,10 +1090,10 @@
     save(m_j, p_j)
     loads[4].wait()
 
-    @pl.loop(0, D // 256)
+    @pl.loop(0, D // 768)
     def _(j):
-        at = pl.ds(pl.multiple_of(j * 256, 256), 256)
-        back[:, :, at] = low(dot_t(m_j[...], egu[at, :])).reshape(EXPERTS, PAD_CAP, 256)
+        at = pl.ds(pl.multiple_of(j * 768, 256), 768)
+        back[:, :, at] = low(dot_t(m_j[...], egu[at, :])).reshape(EXPERTS, PAD_CAP, 768)
 
     ex_r = Exchange(back, slots, r_send, r_recv, True)
     ex_r.start()

time: 544 us -> 514 us (0.945)
  Pallas kernels: 495 us -> 465 us
    pallas_call x1, Pallas kernels: 237 us -> 207 us  [forward(): pl.pallas_call(forward_kernel, out_shape=[jax.ShapeDtypeStruct((ROWS, D),...]
  transfers between devices with their start and end apart: 2 -> 2, of which waited for: 1 -> 1; matrix products, arithmetic and copies ran while one was open for 2% -> 3% of each run, Pallas kernels for 0% -> 0%
where the time goes in v4:
time: 514 us; the launch traced here: 505 us
  Pallas kernels  465 us (90%)
  other arithmetic  20.5 us (4%)
  local copies, waits for them, and re-layouts  17 us (3%)
    pallas_call x1, Pallas kernels, forward(): pl.pallas_call(forward_kernel, out_shape=[jax.ShapeDtypeStruct((ROWS, D),...  207 us
    pallas_call x1, Pallas kernels, weight_grads(): pl.pallas_call(grads_kernel, out_shape=[jax.ShapeDtypeStruct(shape, f32)...  139 us
    pallas_call x2, Pallas kernels, layer_backward(): pl.pallas_call(functools.partial(backward_kernel, layer), out_shape=[jax....  119 us
  transfers between devices with their start and end apart: 2, of which 1 were waited for; matrix products, arithmetic and copies ran while one was open for 3% of the time, Pallas kernels for 0%

profile of v4, /device:TPU:0, one launch (start us, length us, event | category | flops | bytes accessed | tf_op | source)
XLA Modules:
  0.0 504.7 jit_solution(9064110776729174732)
XLA Ops:
  0.7 0.8 fusion.11
  1.5 0.1 copy.105
  1.6 0.1 copy.106
  1.8 0.1 collective-permute-start
  1.9 0.7 add_add_fusion.qidx
  2.7 0.7 broadcast_select_fusion.3
  3.4 1.3 fusion.12.klab
  4.7 0.7 and_convert_fusion.1.sel
  5.4 0.7 and_convert_fusion.refs_26_
  6.1 0.1 convert_reduce_fusion.2
  6.2 0.2 reduce-window.8
  6.4 0.1 select_reduce_fusion
  6.5 1.7 select_bitcast_fusion.4.state
  8.3 1.7 select_bitcast_fusion.1.grad
  10.1 0.1 fusion.10
  10.3 0.9 copy.89.qlab
  11.2 0.9 copy.87.cosine
  12.1 0.9 copy.88.sine
  13.0 0.1 copy.83
  13.3 0.1 concatenate.9
  13.4 0.7 pad.4.pack
  14.1 0.6 slice_bitcast_fusion.1
  14.7 0.1 eq.292
  14.9 0.1 mul.74
  15.0 0.2 convert_reduce_fusion.1
  15.2 0.1 reduce_sum.43
  15.4 0.7 slice_bitcast_fusion
  16.0 0.1 eq.300
  16.2 0.1 mul.77
  16.3 0.2 convert_reduce_fusion
  16.6 0.1 reduce_sum.45
  16.7 0.2 slice_reduce_fusion
  16.9 0.1 iota_compare_fusion.8
  17.1 0.1 iota_compare_fusion.10
  17.2 0.2 slice_reduce_fusion.1
  17.4 0.1 iota_compare_fusion.9
  17.5 0.1 iota_compare_fusion.11
  17.6 0.7 pad_add_fusion.route
  18.3 0.8 fusion.6
  19.1 0.8 fusion.7
  19.9 0.7 add_convert_fusion.2.taken_t
  20.6 0.7 add_convert_fusion.1.second_table
  21.3 0.7 add_convert_fusion.first_table
  22.1 206.8 %forward.1 = (bf16[128,768]{1,0:T(8,128)(2,1)}, bf16[128,768]{1,0:T(8,128)(2,1)}, bf16[768,3072]{1,0:T(8,128)(2,1)}, bf16[768,4096]{1,0:T(8,128)(2,1)}, bf16[768...) custom-call(bf16[16,7296]{1,0:T(8,128)(2,1)} %pad.4.pack, ...), custom_call_target="tpu_custom_call" | custom-call | tf_op jit(solution)/shard_map/forward/pallas_call | solution.py:934
  228.9 1.1 copy.90
  229.9 0.6 convert_bitcast_fusion.1.small_t
  230.5 56.6 %layer_backward.2 = (f32[128,768]{1,0:T(8,128)}, f32[2,128,768]{2,1,0:T(8,128)}, bf16[2,768,128]{2,1,0:T(8,128)(2,1)}, bf16[2,768,128]{2,1,0:T(8,128)(2,1)}, bf1...) custom-call(bf16[128,768]{1,0:T(8,128)(2,1)} %select_bitcast_fusion., ...), custom_call_target="tpu_custom_call" | custom-call | tf_op jit(solution)/shard_map/layer_backward/pallas_call | solution.py:1196
  287.1 1.7 convert_element_type.51.grad
  288.8 0.1 copy.94
  289.0 0.6 convert_bitcast_fusion.small_t
  289.6 62.2 %layer_backward.3 = (f32[128,768]{1,0:T(8,128)}, f32[2,128,768]{2,1,0:T(8,128)}, bf16[2,768,128]{2,1,0:T(8,128)(2,1)}, bf16[2,768,128]{2,1,0:T(8,128)(2,1)}, bf1...) custom-call(bf16[128,768]{1,0:T(8,128)(2,1)} %convert_element_type.5, ...), custom_call_target="tpu_custom_call" | custom-call | tf_op jit(solution)/shard_map/layer_backward/pallas_call | solution.py:1196
  351.9 139.5 %weight_grads.1 = (f32[12,2304]{1,0:T(8,128)}, f32[12,768]{1,0:T(8,128)}, f32[12,128]{1,0:T(8,128)}, f32[12,4096]{1,0:T(8,128)}, f32[32,768]{1,0:T(8,128)}, /*index=5*/f32[96,4096]{1,0:T(8,128)}, f32[256,768]{1,0:T(8,128)}) custom-call(bf16[2,768,128]{2,1,0:T(8,128)(2,1)} %get-tuple-element.113.refs_0_, bf16[2,768,128]{2,1,0:T(8,128)(2,1)} %get-tuple-element.114.refs_1_, ...), custom_call_target="tpu_custom_call" | custom-call | tf_op jit(solution)/shard_map/weight_grads/pallas_call | solution.py:527
  491.4 1.9 copy.104
  493.3 1.7 copy.102
  495.0 1.5 copy.103
  496.5 0.8 slice.91
  497.2 0.7 copy.99
  497.9 1.3 copy.98
  499.4 1.0 select_bitcast_fusion
  500.4 0.4 collective-permute-done.1
  500.8 0.8 maximum_bitcast_fusion
  501.6 0.6 copy.110
  502.3 1.1 copy.111
  503.4 0.9 copy.112
  (49 shorter events, 0.7 us)
Async XLA Ops:
  0.6 12.4 %copy-start.12 = (bf16[1,12,2]{1,2,0:T(2,128)(2,1)S(1)}, bf16[1,12,2]{1,2,0:T(2,128)(2,1)}, u32[]{:S(2)}) copy-start(bf16[1,12,2]{1,2,0:T(2,128)(2,1)} %param.18) | copy-start | bytes 148
  0.7 12.5 %copy-start.11 = (bf16[1,12,8]{1,2,0:T(8,128)(2,1)S(1)}, bf16[1,12,8]{1,2,0:T(8,128)(2,1)}, u32[]{:S(2)}) copy-start(bf16[1,12,8]{1,2,0:T(8,128)(2,1)} %param.21) | copy-start | bytes 580
  0.7 12.6 %copy-start.9 = (bf16[1,12,2304]{2,1,0:T(8,128)(2,1)S(1)}, bf16[1,12,2304]{2,1,0:T(8,128)(2,1)}, u32[]{:S(2)}) copy-start(bf16[1,12,2304]{2,1,0:T(8,128)(2,1)} %param.19) | copy-start | bytes 165892
  0.7 12.6 %copy-start.10 = (bf16[1,12,768]{2,1,0:T(8,128)(2,1)S(1)}, bf16[1,12,768]{2,1,0:T(8,128)(2,1)}, u32[]{:S(2)}) copy-start(bf16[1,12,768]{2,1,0:T(8,128)(2,1)} %param.20) | copy-start | bytes 55300
  0.7 12.6 %copy-start.7 = (bf16[1,12,4096]{2,1,0:T(8,128)(2,1)S(1)}, bf16[1,12,4096]{2,1,0:T(8,128)(2,1)}, u32[]{:S(2)}) copy-start(bf16[1,12,4096]{2,1,0:T(8,128)(2,1)} %param.22) | copy-start | bytes 294916
  1.8 12.3 %collective-permute-start = (s32[2,128,2]{2,1,0:T(8,128)S(1)}, s32[2,128,2]{2,1,0:T(8,128)S(1)}, u32[]{:S(2)}, u32[]{:S(2)}) collective-permute-start(s32[2,128,2]{2,1,0:T(8,128)S(1)} %select_bitcast_fusion.5), channel_id=1, source_target_pairs={{0,64},{64,0},{1,65},{65,1},{2,66},{66,2},{3,67},{67,3},{4,68},{68... | collective-permute-start | bytes 6152 | tf_op jit(solution)/shard_map/ppermute | solution.py:1253
  230.5 58.3 %copy-start.2 = (bf16[768,128]{1,0:T(8,128)(2,1)S(1)}, bf16[768,128]{1,0:T(8,128)(2,1)}, u32[]{:S(2)}) copy-start(bf16[768,128]{1,0:T(8,128)(2,1)} %get-tuple-element.96.g_small) | copy-start | bytes 589828
  351.8 147.4 %copy-start = (bf16[128,768]{1,0:T(8,128)(2,1)S(1)}, bf16[128,768]{1,0:T(8,128)(2,1)}, u32[]{:S(2)}) copy-start(bf16[128,768]{1,0:T(8,128)(2,1)} %get-tuple-element.78.state) | copy-start | bytes 589828
  351.8 147.4 %copy-start.6 = (bf16[128,768]{1,0:T(8,128)(2,1)S(1)}, bf16[128,768]{1,0:T(8,128)(2,1)}, u32[]{:S(2)}) copy-start(bf16[128,768]{1,0:T(8,128)(2,1)} %get-tuple-element.79) | copy-start | bytes 589828
  351.9 147.5 %copy-start.3 = (f32[2,128,768]{2,1,0:T(8,128)S(1)}, f32[2,128,768]{2,1,0:T(8,128)}, u32[]{:S(2)}) copy-start(f32[2,128,768]{2,1,0:T(8,128)} %get-tuple-element.112) | copy-start | bytes 2359300
  351.9 147.5 %copy-start.4 = (f32[2,128,768]{2,1,0:T(8,128)S(1)}, f32[2,128,768]{2,1,0:T(8,128)}, u32[]{:S(2)}) copy-start(f32[2,128,768]{2,1,0:T(8,128)} %get-tuple-element.111) | copy-start | bytes 2359300
  491.4 10.9 %copy-start.1 = (f32[96,4096]{1,0:T(8,128)S(1)}, f32[96,4096]{1,0:T(8,128)}, u32[]{:S(2)}) copy-start(f32[96,4096]{1,0:T(8,128)} %get-tuple-element.144) | copy-start | bytes 4718596
  499.2 2.4 copy-start.8
  499.3 1.5 collective-permute-start.1
  500.4 3.1 copy-start.5

commit v5 on v4

--- a/solution.py
+++ b/solution.py
@@ -242,7 +242,14 @@
     return [(section, ctx, fsdp_of(y + dy, h + dh)) for dy, dh in FSDP_STEPS]
 
 
-def close_rows(sel, packs, target, start):
+def close_table(transposed=False):
+    shape, dims = ((128, 96), (1, 0)) if transposed else ((96, 128), (0, 1))
+    closed, padded = [lax.broadcasted_iota(jnp.int32, shape, d) for d in dims]
+    within = padded % 16
+    return low(jnp.where((within < OWN) & (closed == OWN * (padded // 16) + within), 1.0, 0.0))
+
+
+def close_rows(packs, target, start):
     width = target.shape[1]
     step = min(width, 512)
 
@@ -250,12 +257,7 @@
     def _(j):
         off = pl.multiple_of(j * step, 128)
         block = packs[:, pl.ds(pl.multiple_of(start + off, 128), step)]
-        target[:, pl.ds(off, step)] = low(dot(sel[...], block))
-
-
-def close_table(rows_from, rows_to):
-    cols, rows = jnp.arange(rows_from), jnp.arange(rows_to)
-    return low((rows[:, None] // OWN == cols[None, :] // 16) & (rows[:, None] % OWN == cols[None, :] % 16))
+        target[:, pl.ds(off, step)] = low(dot(close_table(), block))
 
 
 LEFT = (("na", (D, 128)), ("at", (D, 128)), ("nf", (D, 128)), ("sh", (FF, 128)), ("rc", (D, SLOTS)), ("hd", (FF, SLOTS)))
@@ -278,9 +280,8 @@
 
 def grads_kernel(*refs):
     lower, upper = refs[:N_OPS], refs[N_OPS : 2 * N_OPS]
-    sel_t = refs[2 * N_OPS]
-    out_qkv, out_out, out_small, out_gu, out_sd, out_egu, out_ed = refs[2 * N_OPS + 1 : 2 * N_OPS + 8]
-    rest = refs[2 * N_OPS + 8 :]
+    out_qkv, out_out, out_small, out_gu, out_sd, out_egu, out_ed = refs[2 * N_OPS : 2 * N_OPS + 7]
+    rest = refs[2 * N_OPS + 7 :]
     held = rest[:N_OPS]
     (b_wide, b_gu, b_small, b_sd, c_gu, c_sd, packs, in_pack, in_sd,
      o_local, w_send, w_recv, r_send, r_recv, e_send, e_recv, s_send, s_recv) = rest[N_OPS:]
@@ -420,7 +421,7 @@
         def _(j):
             off = pl.multiple_of(j * step, 128)
             block = kinds[kind][7, :, pl.ds(off, step)]
-            packs[:, pl.ds(pl.multiple_of(start + off, 128), step)] = low(dot(sel_t[...], block))
+            packs[:, pl.ds(pl.multiple_of(start + off, 128), step)] = low(dot(close_table(True), block))
 
     last = [[], [], []]
     split_at = WIDE + SMALL
@@ -527,7 +528,7 @@
     return pl.pallas_call(
         grads_kernel,
         out_shape=[jax.ShapeDtypeStruct(shape, f32) for shape in shapes],
-        in_specs=[ANY] * (2 * N_OPS) + [VMEM],
+        in_specs=[ANY] * (2 * N_OPS),
         out_specs=[VMEM] * len(shapes),
         scratch_shapes=held + [
             pltpu.VMEM((10, 96, WIDE), bf),
@@ -546,7 +547,7 @@
         ],
         compiler_params=pltpu.CompilerParams(collective_id=5, has_side_effects=True, vmem_limit_bytes=62 << 20),
         name="weight_grads",
-    )(*lower, *upper, close_table(128, 96).T)
+    )(*lower, *upper)
 
 
 def split(values):
@@ -647,7 +648,7 @@
 
 
 def forward_kernel(
-    pack, i_sd, i_egu, i_ed, sel,
+    pack, i_sd, i_egu, i_ed,
     state, cosine, sine, qidx, qlab, klab, route, first_table, second_table, taken_t,
     out_lower, out_upper,
     l_wide, l_gu, l_small, l_sd, l_egu, l_ed, u_wide, u_gu, u_small, u_sd, u_egu, u_ed,
@@ -697,12 +698,12 @@
 
     def close_wide():
         firsts[0].wait(0)
-        close_rows(sel, packs, own_wide, 0)
-        close_rows(sel, packs, own_small, WIDE)
+        close_rows(packs, own_wide, 0)
+        close_rows(packs, own_small, WIDE)
 
     def close_gu():
         firsts[0].wait(1)
-        close_rows(sel, packs, own_gu, WIDE + SMALL)
+        close_rows(packs, own_gu, WIDE + SMALL)
 
     def arrived(layer, group):
         drive(layer, trees[layer][group].finish)
@@ -734,8 +735,8 @@
     lower, upper = trees
     hooks = {
         (0, "start"): lambda: (
-            drive(0, first(0, 0, 2), close_wide, lower["w"].start_own, first(0, 1), lower["e"].start_own,
-                  lower["w"].pass_ring, lower["w"].pass_pair, close_gu, lower["g"].start_own, lower["w"].pass_far),
+            drive(0, first(0, 0), close_wide, lower["w"].start_own, first(0, 1, 2), lower["w"].pass_ring, lower["w"].pass_pair,
+                  lower["w"].pass_far, lower["e"].start_own, close_gu, lower["g"].start_own),
             arrived(0, "w"), load(0, 0, 2),
         ),
         (0, "keys"): lambda: (drive(0, lower["e"].pass_ring, lower["e"].pass_pair), drive(1, first(1, 0, 1, 2))),
@@ -936,7 +937,7 @@
         out_shape=[jax.ShapeDtypeStruct((ROWS, D), bf)] * 2
         + [jax.ShapeDtypeStruct(s, bf) for s in WEIGHTS] * 2
         + [jax.ShapeDtypeStruct(s, t) for s, t in KEPT] * 2,
-        in_specs=[ANY] * 4 + [VMEM] * 11,
+        in_specs=[ANY] * 4 + [VMEM] * 10,
         out_specs=[VMEM] * 2 + [ANY] * (2 * len(WEIGHTS) + 2 * len(KEPT)),
         scratch_shapes=[
             pltpu.VMEM((2, D, WIDE), bf), pltpu.VMEM((D, 2 * FF), bf), pltpu.VMEM((2, D, SMALL), bf),
@@ -958,7 +959,7 @@
         ],
         compiler_params=pltpu.CompilerParams(collective_id=1, has_side_effects=True, vmem_limit_bytes=60 << 20),
         name="forward",
-    )(pack, sd, egu, ed, close_table(128, 96), state, *geometry, *tables)
+    )(pack, sd, egu, ed, state, *geometry, *tables)
     weights, kept = outs[2 : 2 + 2 * len(WEIGHTS)], outs[2 + 2 * len(WEIGHTS) :]
     return outs[:2], (weights[: len(WEIGHTS)], weights[len(WEIGHTS) :]), (kept[: len(KEPT)], kept[len(KEPT) :])
 

time: 514 us -> 521 us (1.014)
  Pallas kernels: 465 us -> 472 us
    pallas_call x1, Pallas kernels: 207 us -> 216 us  [forward(): pl.pallas_call(forward_kernel, out_shape=[jax.ShapeDtypeStruct((ROWS, D),...]
  transfers between devices with their start and end apart: 2 -> 2, of which waited for: 1 -> 1; matrix products, arithmetic and copies ran while one was open for 3% -> 2% of each run, Pallas kernels for 0% -> 0%
where the time goes in v5:
time: 521 us; the launch traced here: 511 us
  Pallas kernels  472 us (91%)
  other arithmetic  19.1 us (4%)
  local copies, waits for them, and re-layouts  17 us (3%)
    pallas_call x1, Pallas kernels, forward(): pl.pallas_call(forward_kernel, out_shape=[jax.ShapeDtypeStruct((ROWS, D),...  216 us
    pallas_call x1, Pallas kernels, weight_grads(): pl.pallas_call(grads_kernel, out_shape=[jax.ShapeDtypeStruct(shape, f32)...  138 us
    pallas_call x2, Pallas kernels, layer_backward(): pl.pallas_call(functools.partial(backward_kernel, layer), out_shape=[jax....  118 us
  transfers between devices with their start and end apart: 2, of which 1 were waited for; matrix products, arithmetic and copies ran while one was open for 2% of the time, Pallas kernels for 0%

profile of v5, /device:TPU:0, one launch (start us, length us, event | category | flops | bytes accessed | tf_op | source)
XLA Modules:
  0.0 510.6 jit_solution(3630674735890116829)
XLA Ops:
  0.7 0.8 fusion.11
  1.5 0.1 copy.105
  1.6 0.1 copy.106
  1.8 0.1 collective-permute-start
  1.9 0.7 add_add_fusion.qidx
  2.7 0.7 broadcast_select_fusion.3
  3.4 1.3 fusion.12.klab
  4.7 0.1 convert_reduce_fusion.2
  4.8 0.2 reduce-window.8
  5.0 0.1 select_reduce_fusion
  5.1 1.7 select_bitcast_fusion.4.state
  6.8 1.7 select_bitcast_fusion.1.grad
  8.7 0.1 fusion.10
  8.9 0.9 copy.87.cosine
  9.8 0.9 copy.88.sine
  10.7 0.9 copy.89.qlab
  11.6 0.1 copy.83
  11.7 0.1 copy.84
  11.8 0.1 concatenate.9
  11.9 0.7 pad.4.pack
  12.7 0.6 slice_bitcast_fusion.1
  13.3 0.1 eq.226
  13.4 0.1 mul.74
  13.6 0.2 convert_reduce_fusion.1
  13.8 0.1 reduce_sum.43
  14.0 0.6 slice_bitcast_fusion
  14.6 0.1 eq.234
  14.7 0.1 mul.77
  14.9 0.2 convert_reduce_fusion
  15.1 0.1 reduce_sum.45
  15.3 0.2 slice_reduce_fusion
  15.5 0.1 iota_compare_fusion.8
  15.6 0.1 iota_compare_fusion.10
  15.7 0.2 slice_reduce_fusion.1
  15.9 0.1 iota_compare_fusion.9
  16.1 0.1 iota_compare_fusion.11
  16.2 0.7 pad_add_fusion.route
  16.8 0.8 fusion.6
  17.7 0.8 fusion.7
  18.5 0.7 add_convert_fusion.2.taken_t
  19.2 0.7 add_convert_fusion.1.second_table
  19.9 0.7 add_convert_fusion.first_table
  20.6 216.5 %forward.1 = (bf16[128,768]{1,0:T(8,128)(2,1)}, bf16[128,768]{1,0:T(8,128)(2,1)}, bf16[768,3072]{1,0:T(8,128)(2,1)}, bf16[768,4096]{1,0:T(8,128)(2,1)}, bf16[768...) custom-call(bf16[16,7296]{1,0:T(8,128)(2,1)} %pad.4.pack, ...), custom_call_target="tpu_custom_call" | custom-call | tf_op jit(solution)/shard_map/forward/pallas_call | solution.py:935
  237.1 1.1 copy.90
  238.1 0.6 convert_bitcast_fusion.1.small_t
  238.7 57.4 %layer_backward.2 = (f32[128,768]{1,0:T(8,128)}, f32[2,128,768]{2,1,0:T(8,128)}, bf16[2,768,128]{2,1,0:T(8,128)(2,1)}, bf16[2,768,128]{2,1,0:T(8,128)(2,1)}, bf1...) custom-call(bf16[128,768]{1,0:T(8,128)(2,1)} %select_bitcast_fusion., ...), custom_call_target="tpu_custom_call" | custom-call | tf_op jit(solution)/shard_map/layer_backward/pallas_call | solution.py:1197
  296.1 1.7 convert_element_type.44.grad
  297.8 0.1 copy.94
  297.9 0.6 convert_bitcast_fusion.small_t
  298.6 60.6 %layer_backward.3 = (f32[128,768]{1,0:T(8,128)}, f32[2,128,768]{2,1,0:T(8,128)}, bf16[2,768,128]{2,1,0:T(8,128)(2,1)}, bf16[2,768,128]{2,1,0:T(8,128)(2,1)}, bf1...) custom-call(bf16[128,768]{1,0:T(8,128)(2,1)} %convert_element_type.4, ...), custom_call_target="tpu_custom_call" | custom-call | tf_op jit(solution)/shard_map/layer_backward/pallas_call | solution.py:1197
  359.2 138.0 %weight_grads.1 = (f32[12,2304]{1,0:T(8,128)}, f32[12,768]{1,0:T(8,128)}, f32[12,128]{1,0:T(8,128)}, f32[12,4096]{1,0:T(8,128)}, f32[32,768]{1,0:T(8,128)}, /*index=5*/f32[96,4096]{1,0:T(8,128)}, f32[256,768]{1,0:T(8,128)}) custom-call(bf16[2,768,128]{2,1,0:T(8,128)(2,1)} %get-tuple-element.113.refs_0_, bf16[2,768,128]{2,1,0:T(8,128)(2,1)} %get-tuple-element.114.refs_1_, ...), custom_call_target="tpu_custom_call" | custom-call | tf_op jit(solution)/shard_map/weight_grads/pallas_call | solution.py:528
  497.3 1.9 copy.104
  499.2 1.7 copy.102
  500.9 1.5 copy.103
  502.3 0.8 slice.91
  503.1 0.7 copy.99
  503.8 1.3 copy.98
  505.1 0.1 collective-permute-start.1
  505.3 1.0 select_bitcast_fusion
  506.2 0.4 collective-permute-done.1
  506.7 0.8 maximum_bitcast_fusion
  507.5 0.6 copy.110
  508.1 1.1 copy.111
  509.3 0.9 copy.112
  (45 shorter events, 0.5 us)
Async XLA Ops:
  0.6 11.0 %copy-start.12 = (bf16[1,12,2]{1,2,0:T(2,128)(2,1)S(1)}, bf16[1,12,2]{1,2,0:T(2,128)(2,1)}, u32[]{:S(2)}) copy-start(bf16[1,12,2]{1,2,0:T(2,128)(2,1)} %param.18) | copy-start | bytes 148
  0.7 11.0 %copy-start.11 = (bf16[1,12,8]{1,2,0:T(8,128)(2,1)S(1)}, bf16[1,12,8]{1,2,0:T(8,128)(2,1)}, u32[]{:S(2)}) copy-start(bf16[1,12,8]{1,2,0:T(8,128)(2,1)} %param.21) | copy-start | bytes 580
  0.7 11.1 %copy-start.9 = (bf16[1,12,2304]{2,1,0:T(8,128)(2,1)S(1)}, bf16[1,12,2304]{2,1,0:T(8,128)(2,1)}, u32[]{:S(2)}) copy-start(bf16[1,12,2304]{2,1,0:T(8,128)(2,1)} %param.19) | copy-start | bytes 165892
  0.7 11.1 %copy-start.10 = (bf16[1,12,768]{2,1,0:T(8,128)(2,1)S(1)}, bf16[1,12,768]{2,1,0:T(8,128)(2,1)}, u32[]{:S(2)}) copy-start(bf16[1,12,768]{2,1,0:T(8,128)(2,1)} %param.20) | copy-start | bytes 55300
  0.7 11.1 %copy-start.7 = (bf16[1,12,4096]{2,1,0:T(8,128)(2,1)S(1)}, bf16[1,12,4096]{2,1,0:T(8,128)(2,1)}, u32[]{:S(2)}) copy-start(bf16[1,12,4096]{2,1,0:T(8,128)(2,1)} %param.22) | copy-start | bytes 294916
  1.8 10.8 %collective-permute-start = (s32[2,128,2]{2,1,0:T(8,128)S(1)}, s32[2,128,2]{2,1,0:T(8,128)S(1)}, u32[]{:S(2)}, u32[]{:S(2)}) collective-permute-start(s32[2,128,2]{2,1,0:T(8,128)S(1)} %select_bitcast_fusion.5), channel_id=1, source_target_pairs={{0,64},{64,0},{1,65},{65,1},{2,66},{66,2},{3,67},{67,3},{4,68},{68... | collective-permute-start | bytes 6152 | tf_op jit(solution)/shard_map/ppermute | solution.py:1254
  238.7 59.1 %copy-start.2 = (bf16[768,128]{1,0:T(8,128)(2,1)S(1)}, bf16[768,128]{1,0:T(8,128)(2,1)}, u32[]{:S(2)}) copy-start(bf16[768,128]{1,0:T(8,128)(2,1)} %get-tuple-element.96.g_small) | copy-start | bytes 589828
  359.2 145.9 %copy-start = (bf16[128,768]{1,0:T(8,128)(2,1)S(1)}, bf16[128,768]{1,0:T(8,128)(2,1)}, u32[]{:S(2)}) copy-start(bf16[128,768]{1,0:T(8,128)(2,1)} %get-tuple-element.78.state) | copy-start | bytes 589828
  359.2 145.9 %copy-start.6 = (bf16[128,768]{1,0:T(8,128)(2,1)S(1)}, bf16[128,768]{1,0:T(8,128)(2,1)}, u32[]{:S(2)}) copy-start(bf16[128,768]{1,0:T(8,128)(2,1)} %get-tuple-element.79) | copy-start | bytes 589828
  359.2 146.0 %copy-start.3 = (f32[2,128,768]{2,1,0:T(8,128)S(1)}, f32[2,128,768]{2,1,0:T(8,128)}, u32[]{:S(2)}) copy-start(f32[2,128,768]{2,1,0:T(8,128)} %get-tuple-element.112) | copy-start | bytes 2359300
  359.2 146.0 %copy-start.4 = (f32[2,128,768]{2,1,0:T(8,128)S(1)}, f32[2,128,768]{2,1,0:T(8,128)}, u32[]{:S(2)}) copy-start(f32[2,128,768]{2,1,0:T(8,128)} %get-tuple-element.111) | copy-start | bytes 2359300
  497.3 10.9 %copy-start.1 = (f32[96,4096]{1,0:T(8,128)S(1)}, f32[96,4096]{1,0:T(8,128)}, u32[]{:S(2)}) copy-start(f32[96,4096]{1,0:T(8,128)} %get-tuple-element.144) | copy-start | bytes 4718596
  505.1 2.4 copy-start.8
  505.1 1.5 collective-permute-start.1
  506.2 3.1 copy-start.5
